TPU v7x, 256 devices: a whole 4x4x8 slice. The times are simulated.
256 devices in a mesh: space: 64 (over x, z, core), chan: 4 (over y).
Axes of the slice: x: 4, y: 4, z: 8, core: 2. Of those that a mesh axis runs over, the one named last changes fastest.
Arguments:
- features: bfloat16 [128, 256, 512], P('chan', 'space'), may hold values from -6 to 6
- weight: bfloat16 [27, 128, 128], P(None, 'chan'), may hold values from -0.21875 to 0.21875
- cotangent: bfloat16 [128, 256, 512], P('chan', 'space'), may hold values from -6 to 6
- neighbours: int32 [256, 27], P('space'), may hold values from 0 to 68, as said below
- send_slots: int32 [512, 8], P('space'), may hold values from 0 to 4, as said below
Outputs:
- output: bfloat16 [128, 256, 512], P('chan', 'space')
- grad_input: bfloat16 [128, 256, 512], P('chan', 'space')
- grad_weight: float32 [27, 128, 128], P(None, 'chan')
Inputs may be any that keep to these rules, and one draw needn't show every extreme that they name: `neighbours`: each owner has a tile of 4 x 4 x 2 brick places; its occupied places fill its first brick slots, and in some owner all 4 slots are occupied. Row b, column 9 (ox + 1) + 3 (oy + 1) + oz + 1 names the pool entry of the brick at brick offset (ox, oy, oz) from brick b, 0 where that place is empty or outside the grid; rows of unoccupied slots are all 0. Between occupied bricks the relation is symmetric: if b2 is at offset (ox, oy, oz) from b, b is at (-ox, -oy, -oz) from b2. Entries 1 + d * 8 + j occur only where the owner in direction d exists and lists an occupied brick in slot j of its side facing back. `send_slots`: row 8 s + e lists, one slot per brick place in a fixed order, the bricks of owner s on its tile's side facing direction e: a face of 4 x 2 or 4 x 2 places, or a corner column of 2 places; 4 marks an empty place, an unused slot, or a side whose neighbouring owner does not exist.
All inputs are finite; a program needn't handle non-finite values.
Results may differ from a plain program's by a relative error of at most 0.0042.
Values may be sent and summed in bfloat16 or wider, within the bound.
No kernel may reach another device: no remote copies, remote signals or barrier semaphores. Data moves between devices by JAX's collectives and lax.ppermute only.
A program may use at most 192 MiB of HBM per device.

v0:
```python
import jax
import jax.numpy as jnp
from jax import lax
from jax.sharding import PartitionSpec as P

OWNER_ROWS = 4


compass = ((-1, -1), (-1, 0), (-1, 1), (0, -1), (0, 1), (1, -1), (1, 0), (1, 1))


def shifted(value, axis, steps):
    count = lax.axis_size(axis)
    first, last = (max(0, -steps), min(count, count - steps))
    return lax.ppermute(value, axis, [(source, source + steps) for source in range(first, last)])


def face_pick(bricks):
    channels, slot_count = (bricks.shape[0], bricks.shape[1])
    return bricks.reshape(channels, slot_count * 512)


def face_place(flattened, slot_count):
    channels = flattened.shape[0]
    return flattened.reshape(channels, slot_count, 512)


def pack_face(extended, send_slots, facing):
    chosen = jnp.take(extended, send_slots[compass.index(facing)], axis=1)
    return face_pick(chosen)


def gather_pool(field, send_slots):
    channels = field.shape[0]
    slot_count = send_slots.shape[1]
    blank = jnp.zeros((channels, 1, field.shape[2]), field.dtype)
    extended = jnp.concatenate([field, blank], axis=1)
    received = {}
    for i in range(8):
        shift_x, shift_y = compass[i]
        outgoing = pack_face(extended, send_slots, compass[7 - i])
        incoming = shifted(outgoing, "space", -(shift_x * OWNER_ROWS + shift_y))
        received[compass[i]] = incoming
    arrived = [face_place(received[compass[i]], slot_count) for i in range(8)]
    return [blank] + arrived + [field]


def brick_margin(pool_parts, lookup):
    channels = pool_parts[0].shape[0]
    cubes = [member.reshape(channels, member.shape[1], 8, 8, 8) for member in pool_parts]
    own_cube = cubes[-1]
    centre_keep = (lookup[:, 13] > 0)[None, :, None, None, None]
    layer_cuts = ((7, 8), (0, 8), (0, 1))
    planes = []
    for i in range(3):
        row_parts = []
        for j in range(3):
            column_parts = []
            for k in range(3):
                if i == 1 and j == 1 and (k == 1):
                    column_parts.append(
                        jnp.where(centre_keep, own_cube, jnp.zeros((), own_cube.dtype))
                    )
                else:
                    slabs = [
                        cube[
                            :,
                            :,
                            layer_cuts[i][0] : layer_cuts[i][1],
                            layer_cuts[j][0] : layer_cuts[j][1],
                            layer_cuts[k][0] : layer_cuts[k][1],
                        ]
                        for cube in cubes
                    ]
                    slab_pool = jnp.concatenate(slabs, axis=1)
                    column_parts.append(jnp.take(slab_pool, lookup[:, 9 * i + 3 * j + k], axis=1))
            row_parts.append(jnp.concatenate(column_parts, axis=4))
        planes.append(jnp.concatenate(row_parts, axis=3))
    return jnp.concatenate(planes, axis=2)


def stack_group(padded, offset_x):
    channels, bricks = (padded.shape[0], padded.shape[1])
    slices = []
    for j in range(3):
        for k in range(3):
            slices.append(
                padded[:, :, offset_x : offset_x + 8, j : j + 8, k : k + 8].reshape(
                    channels, bricks * 512
                )
            )
    return jnp.concatenate(slices, axis=0)


def tap_terms(stacks, groups):
    running = None
    for i in range(3):
        sliced = groups[i]
        term = lax.dot_general(
            sliced, stacks[i], (((0,), (0,)), ((), ())), preferred_element_type=jnp.float32
        )
        running = term if i == 0 else running + term
    return running


def per_device(features, weight, cotangent, neighbours, send_slots):
    channels, bricks = (features.shape[0], features.shape[1])
    all_chan = weight.shape[2]
    feat_flat = features.reshape(channels, bricks * 512).astype(jnp.float32)
    cot_flat = cotangent.reshape(channels, bricks * 512).astype(jnp.float32)
    columns = lax.all_to_all(weight, "chan", split_axis=2, concat_axis=1, tiled=True)
    feat_pool = gather_pool(features, send_slots)
    feat_stacks = [stack_group(brick_margin(feat_pool, neighbours), i) for i in range(3)]
    weight_groups = [weight[9 * i : 9 * i + 9].reshape(9 * channels, all_chan) for i in range(3)]
    hidden = lax.psum_scatter(
        tap_terms(feat_stacks, weight_groups), "chan", scatter_dimension=0, tiled=True
    )
    gate_sig = jax.nn.sigmoid(hidden)
    output = (feat_flat + hidden * gate_sig).astype(jnp.bfloat16).reshape(channels, bricks, 512)
    grad_h = (
        (cot_flat * gate_sig * (1.0 + hidden * (1.0 - gate_sig)))
        .astype(jnp.bfloat16)
        .reshape(channels, bricks, 512)
    )
    segment = lax.all_gather(grad_h, "chan", axis=0, tiled=True)
    flattened = segment.reshape(segment.shape[0], bricks * 512)
    blocks = [
        lax.dot_general(
            tap_stack, flattened, (((1,), (1,)), ((), ())), preferred_element_type=jnp.float32
        ).reshape(9, channels, segment.shape[0])
        for tap_stack in feat_stacks
    ]
    partial_grad = jnp.concatenate(blocks, axis=0)
    flipped = jnp.flip(columns, 0).transpose(0, 2, 1)
    flipped_groups = [flipped[9 * i : 9 * i + 9].reshape(9 * channels, all_chan) for i in range(3)]
    grad_pool = gather_pool(grad_h, send_slots)
    grad_stacks = [stack_group(brick_margin(grad_pool, neighbours), i) for i in range(3)]
    transposed = lax.psum_scatter(
        tap_terms(grad_stacks, flipped_groups), "chan", scatter_dimension=0, tiled=True
    )
    grad_weight = lax.psum(partial_grad, "space")
    grad_input = (cot_flat + transposed).astype(jnp.bfloat16).reshape(channels, bricks, 512)
    return (output, grad_input, grad_weight)


def solution(mesh):
    return jax.shard_map(
        per_device,
        mesh=mesh,
        in_specs=(
            P("chan", "space", None),
            P(None, "chan", None),
            P("chan", "space", None),
            P("space", None),
            P("space", None),
        ),
        out_specs=(P("chan", "space", None), P("chan", "space", None), P(None, "chan", None)),
        check_vma=False,
    )
```

profile of v0, /device:TPU:1, one launch (start us, length us, event | category | flops | bytes accessed | tf_op | source)
XLA Modules:
  0.0 1121.7 jit_solution(8831643793292784361)
XLA Ops:
  10.7 8.3 collective-permute-start
  20.4 4.5 collective-permute-start.1
  219.1 6.0 concatenate.504
  227.4 6.8 concatenate.514
  295.9 6.5 maximum_maximum_fusion.1
  359.1 6.2 concatenate.498
  366.5 6.1 concatenate.503
  374.1 6.1 concatenate.518
  409.1 8.7 reduce-scatter.7.cloned.1.call-done
  446.2 7.3 collective-permute-start.8
  460.7 11.9 %collective-permute-start.9 = (bf16[32,4096]{1,0:T(8,128)(2,1)}, bf16[32,4096]{1,0:T(8,128)(2,1)S(1)}, u32[]{:S(2)}, u32[]{:S(2)}) collective-permute-start(bf16[32,4096]{1,0:T(8,128)(2,1)} %bitcast.478), channel_id=1, source_target_pairs={{0,16},{4,20},{8,24},{12,28},{16,32},{20,36},{24,40},{28,44},{32,4... | collective-permute-start | bytes 786440 | tf_op jit(solution)/shard_map/ppermute | solution.py:15
  480.8 5.4 collective-permute-start.10
  490.9 5.4 collective-permute-done.10
  558.1 6.3 concatenate.552
  575.7 6.0 concatenate.554
  743.9 6.5 maximum_maximum_fusion.3
  773.9 6.2 concatenate.520
  789.5 5.6 concatenate.522
  865.1 6.5 concatenate.546
  874.6 6.5 concatenate.551
  883.4 6.5 concatenate.566
  901.4 10.8 all_gather.3
  919.8 9.4 reduce-scatter.9.cloned.1.call-done
  931.4 181.7 %all-reduce.4.cloned.1.call-done = f32[27,32,128]{2,1,0:T(8,128)} async-done(((f32[27,32,128]{2,1,0:T(8,128)}), f32[27,32,128]{2,1,0:T(8,128)}) %all-reduce.4.cloned.1.call-update) | async-done | bytes 442384 | tf_op jit(solution)/shard_map/psum | solution.py:141
  (1532 shorter events, 762.1 us)
Async XLA Ops:
  7.2 410.6 %reduce-scatter.7.cloned.1.call-start = ((), (), s32[]{:S(2)}) async-start(), calls=%async_computation.4 | async-start | bytes 1310720
  8.3 78.1 %copy-start.279 = (pred[8]{0:T(512)(128)(4,1)}, pred[8]{0:T(512)(128)(4,1)S(1)}, u32[]{:S(2)}) copy-start(pred[8]{0:T(512)(128)(4,1)S(1)} %get-tuple-element.603) | copy-start | bytes 28
  8.3 78.2 %copy-start.285 = (pred[8]{0:T(512)(128)(4,1)}, pred[8]{0:T(512)(128)(4,1)S(1)}, u32[]{:S(2)}) copy-start(pred[8]{0:T(512)(128)(4,1)S(1)} %get-tuple-element.615) | copy-start | bytes 28
  8.3 78.3 %copy-start.283 = (pred[8]{0:T(512)(128)(4,1)}, pred[8]{0:T(512)(128)(4,1)S(1)}, u32[]{:S(2)}) copy-start(pred[8]{0:T(512)(128)(4,1)S(1)} %get-tuple-element.57) | copy-start | bytes 28
  10.7 79.4 %collective-permute-start = (bf16[32,4096]{1,0:T(8,128)(2,1)}, bf16[32,4096]{1,0:T(8,128)(2,1)}, u32[]{:S(2)}, u32[]{:S(2)}) collective-permute-start(bf16[32,4096]{1,0:T(8,128)(2,1)} %bitcast.460), channel_id=1, source_target_pairs={{0,20},{4,24},{8,28},{12,32},{16,36},{20,40},{24,44},{28,48},{32,5... | collective-permute-start | bytes 786440 | tf_op jit(solution)/shard_map/ppermute | solution.py:15
  20.4 73.7 %collective-permute-start.1 = (bf16[32,4096]{1,0:T(8,128)(2,1)}, bf16[32,4096]{1,0:T(8,128)(2,1)S(1)}, u32[]{:S(2)}, u32[]{:S(2)}) collective-permute-start(bf16[32,4096]{1,0:T(8,128)(2,1)} %bitcast.462), channel_id=1, source_target_pairs={{0,16},{4,20},{8,24},{12,28},{16,32},{20,36},{24,40},{28,44},{32,4... | collective-permute-start | bytes 786440 | tf_op jit(solution)/shard_map/ppermute | solution.py:15
  26.4 72.6 %collective-permute-start.2 = (bf16[32,4096]{1,0:T(8,128)(2,1)}, bf16[32,4096]{1,0:T(8,128)(2,1)}, u32[]{:S(2)}, u32[]{:S(2)}) collective-permute-start(bf16[32,4096]{1,0:T(8,128)(2,1)} %bitcast.464), channel_id=1, source_target_pairs={{0,12},{4,16},{8,20},{12,24},{16,28},{20,32},{24,36},{28,40},{32,4... | collective-permute-start | bytes 786440 | tf_op jit(solution)/shard_map/ppermute | solution.py:15
  31.2 75.2 %collective-permute-start.3 = (bf16[32,4096]{1,0:T(8,128)(2,1)}, bf16[32,4096]{1,0:T(8,128)(2,1)}, u32[]{:S(2)}, u32[]{:S(2)}) collective-permute-start(bf16[32,4096]{1,0:T(8,128)(2,1)} %bitcast.466), channel_id=1, source_target_pairs={{0,4},{4,8},{8,12},{12,16},{16,20},{20,24},{24,28},{28,32},{32,36}... | collective-permute-start | bytes 786440 | tf_op jit(solution)/shard_map/ppermute | solution.py:15
  35.5 76.5 %collective-permute-start.4 = (bf16[32,4096]{1,0:T(8,128)(2,1)}, bf16[32,4096]{1,0:T(8,128)(2,1)S(1)}, u32[]{:S(2)}, u32[]{:S(2)}) collective-permute-start(bf16[32,4096]{1,0:T(8,128)(2,1)} %bitcast.468), channel_id=1, source_target_pairs={{4,0},{8,4},{12,8},{16,12},{20,16},{24,20},{28,24},{32,28},{36,32}... | collective-permute-start | bytes 786440 | tf_op jit(solution)/shard_map/ppermute | solution.py:15
  90.1 26.6 %collective-permute-start.5 = (bf16[32,4096]{1,0:T(8,128)(2,1)}, bf16[32,4096]{1,0:T(8,128)(2,1)}, u32[]{:S(2)}, u32[]{:S(2)}) collective-permute-start(bf16[32,4096]{1,0:T(8,128)(2,1)} %bitcast.470), channel_id=1, source_target_pairs={{12,0},{16,4},{20,8},{24,12},{28,16},{32,20},{36,24},{40,28},{44,3... | collective-permute-start | bytes 786440 | tf_op jit(solution)/shard_map/ppermute | solution.py:15
  94.9 27.4 %collective-permute-start.6 = (bf16[32,4096]{1,0:T(8,128)(2,1)}, bf16[32,4096]{1,0:T(8,128)(2,1)}, u32[]{:S(2)}, u32[]{:S(2)}) collective-permute-start(bf16[32,4096]{1,0:T(8,128)(2,1)} %bitcast.472), channel_id=1, source_target_pairs={{16,0},{20,4},{24,8},{28,12},{32,16},{36,20},{40,24},{44,28},{48,3... | collective-permute-start | bytes 786440 | tf_op jit(solution)/shard_map/ppermute | solution.py:15
  99.0 29.0 %collective-permute-start.7 = (bf16[32,4096]{1,0:T(8,128)(2,1)}, bf16[32,4096]{1,0:T(8,128)(2,1)}, u32[]{:S(2)}, u32[]{:S(2)}) collective-permute-start(bf16[32,4096]{1,0:T(8,128)(2,1)} %bitcast.1227), channel_id=1, source_target_pairs={{20,0},{24,4},{28,8},{32,12},{36,16},{40,20},{44,24},{48,28},{52,3... | collective-permute-start | bytes 786440 | tf_op jit(solution)/shard_map/ppermute | solution.py:15
  389.0 12.8 %all-to-all-start = ((bf16[4,2,13824]{2,1,0:T(2,128)(2,1)}), bf16[4,2,13824]{2,1,0:T(2,128)(2,1)S(1)}, u32[]{:S(2)}, u32[]{:S(2)}) async-start(bf16[4,2,13824]{2,1,0:T(2,128)(2,1)} %reshape.1676), calls=%async_computation | async-start | bytes 442368 | tf_op jit(solution)/shard_map/all_to_all | solution.py:111
  393.2 535.9 %reduce-scatter.9.cloned.1.call-start = ((), (), s32[]{:S(2)}) async-start(), calls=%async_computation.5 | async-start | bytes 1310720
  435.1 83.7 %collective-permute-start.14 = (bf16[32,4096]{1,0:T(8,128)(2,1)}, bf16[32,4096]{1,0:T(8,128)(2,1)}, u32[]{:S(2)}, u32[]{:S(2)}) collective-permute-start(bf16[32,4096]{1,0:T(8,128)(2,1)} %bitcast.488), channel_id=1, source_target_pairs={{16,0},{20,4},{24,8},{28,12},{32,16},{36,20},{40,24},{44,28},{48,3... | collective-permute-start | bytes 786440 | tf_op jit(solution)/shard_map/ppermute | solution.py:15
  437.1 87.4 %collective-permute-start.15 = (bf16[32,4096]{1,0:T(8,128)(2,1)}, bf16[32,4096]{1,0:T(8,128)(2,1)}, u32[]{:S(2)}, u32[]{:S(2)}) collective-permute-start(bf16[32,4096]{1,0:T(8,128)(2,1)} %bitcast.490), channel_id=1, source_target_pairs={{20,0},{24,4},{28,8},{32,12},{36,16},{40,20},{44,24},{48,28},{52,3... | collective-permute-start | bytes 786440 | tf_op jit(solution)/shard_map/ppermute | solution.py:15
  439.4 68.1 %collective-permute-start.12 = (bf16[32,4096]{1,0:T(8,128)(2,1)}, bf16[32,4096]{1,0:T(8,128)(2,1)}, u32[]{:S(2)}, u32[]{:S(2)}) collective-permute-start(bf16[32,4096]{1,0:T(8,128)(2,1)} %bitcast.484), channel_id=1, source_target_pairs={{4,0},{8,4},{12,8},{16,12},{20,16},{24,20},{28,24},{32,28},{36,32}... | collective-permute-start | bytes 786440 | tf_op jit(solution)/shard_map/ppermute | solution.py:15
  444.7 68.5 %collective-permute-start.13 = (bf16[32,4096]{1,0:T(8,128)(2,1)}, bf16[32,4096]{1,0:T(8,128)(2,1)}, u32[]{:S(2)}, u32[]{:S(2)}) collective-permute-start(bf16[32,4096]{1,0:T(8,128)(2,1)} %bitcast.486), channel_id=1, source_target_pairs={{12,0},{16,4},{20,8},{24,12},{28,16},{32,20},{36,24},{40,28},{44,3... | collective-permute-start | bytes 786440 | tf_op jit(solution)/shard_map/ppermute | solution.py:15
  446.2 14.5 %collective-permute-start.8 = (bf16[32,4096]{1,0:T(8,128)(2,1)S(1)}, bf16[32,4096]{1,0:T(8,128)(2,1)S(1)}, u32[]{:S(2)}, u32[]{:S(2)}) collective-permute-start(bf16[32,4096]{1,0:T(8,128)(2,1)S(1)} %bitcast.1230), channel_id=1, source_target_pairs={{0,20},{4,24},{8,28},{12,32},{16,36},{20,40},{24,44},{28,48},{32,5... | collective-permute-start | bytes 786440 | tf_op jit(solution)/shard_map/ppermute | solution.py:15
  460.7 20.1 %collective-permute-start.9 = (bf16[32,4096]{1,0:T(8,128)(2,1)}, bf16[32,4096]{1,0:T(8,128)(2,1)S(1)}, u32[]{:S(2)}, u32[]{:S(2)}) collective-permute-start(bf16[32,4096]{1,0:T(8,128)(2,1)} %bitcast.478), channel_id=1, source_target_pairs={{0,16},{4,20},{8,24},{12,28},{16,32},{20,36},{24,40},{28,44},{32,4... | collective-permute-start | bytes 786440 | tf_op jit(solution)/shard_map/ppermute | solution.py:15
  480.8 15.5 %collective-permute-start.10 = (bf16[32,4096]{1,0:T(8,128)(2,1)}, bf16[32,4096]{1,0:T(8,128)(2,1)S(1)}, u32[]{:S(2)}, u32[]{:S(2)}) collective-permute-start(bf16[32,4096]{1,0:T(8,128)(2,1)} %bitcast.1229), channel_id=1, source_target_pairs={{0,12},{4,16},{8,20},{12,24},{16,28},{20,32},{24,36},{28,40},{32,4... | collective-permute-start | bytes 786440 | tf_op jit(solution)/shard_map/ppermute | solution.py:15
  496.3 6.6 collective-permute-start.11
  552.9 64.1 %copy-start.222 = (bf16[32,8,1,1,1]{0,4,3,2,1:T(2,128)(2,1)S(1)}, bf16[32,8,1,1,1]{0,4,3,2,1:T(2,128)(2,1)}, u32[]{:S(2)}) copy-start(bf16[32,8,1,1,1]{0,4,3,2,1:T(2,128)(2,1)} %get-tuple-element.134) | copy-start | bytes 1540
  895.4 217.7 %all-reduce.4.cloned.1.call-start = ((), (), s32[]{:S(2)}) async-start(), calls=%async_computation.3 | async-start | bytes 884736 | tf_op jit(solution)/shard_map/psum | solution.py:141
  (316 other events, 4584.1 us)
Sparse Core Ops, SparseCore 0:
  386.3 31.4 reduce-scatter.6
  895.5 33.5 reduce-scatter.8
  933.2 179.9 all-reduce.3
where the time goes:
time: 1140 us; the launch traced here: 1120 us
  local copies, waits for them, and re-layouts  703 us (62%)
  waiting for transfers between devices  209 us (18%)
  other arithmetic  101 us (9%)
  starting transfers between devices  64.8 us (6%)
  between operations  18.4 us (2%)
  matrix products  15.1 us (1%)
    unnamed x1029, local copies, waits for them, and re-layouts  294 us
    psum x1, waiting for transfers between devices, per_device(): grad_weight = lax.psum(partial_grad, 'space')  182 us
    slice x75, local copies, waits for them, and re-layouts, brick_margin(): cube[:, :, layer_cuts[i][0]:layer_cuts[i][1], layer_cuts[j][0]:layer_cuts...  101 us
    concatenate x47, local copies, waits for them, and re-layouts, brick_margin(): slab_pool = jnp.concatenate(slabs, axis=1)  74.2 us
    gather x52, local copies, waits for them, and re-layouts, brick_margin(): jnp.take(slab_pool, lookup[:, 9 * i + 3 * j + k], axis=1)  67.6 us
    ppermute x16, starting transfers between devices, shifted(): lax.ppermute(value, axis, [(source, source + steps) for source in range(f...  60.5 us
    slice x60, local copies, waits for them, and re-layouts, stack_group(): padded[:, :, offset_x:offset_x + 8, j:j + 8, k:k + 8]  59.3 us
    concatenate x9, local copies, waits for them, and re-layouts, stack_group(): return jnp.concatenate(slices, axis=0)  43.5 us
  transfers between devices with their start and end apart: 20, of which 5 were waited for; matrix products, arithmetic and copies ran while one was open for 15% of the time, Pallas kernels for 0%

commit v1 on v0

v1 whole, which is shorter than its diff:
```python
import jax
import jax.numpy as jnp
from jax import lax
from jax.experimental import pallas as pl
from jax.experimental.pallas import tpu as pltpu
from jax.sharding import Mesh, PartitionSpec as P

ROWS = 4
CH = 128
BR = 4
VOX = 512
TAPS = 27
SLOTS = 8
ZERO = 36
F32 = jnp.float32
BF16 = jnp.bfloat16
SPACE = ("x", "z", "core")
XC = ("x", "core")
VMEM = pl.BlockSpec(memory_space=pltpu.VMEM)
SMEM = pl.BlockSpec(memory_space=pltpu.SMEM)

compass = ((-1, -1), (-1, 0), (-1, 1), (0, -1), (0, 1), (1, -1), (1, 0), (1, 1))
BASE = {facing: 4 + 4 * i for i, facing in enumerate(compass)}
PARAMS = pltpu.CompilerParams(vmem_limit_bytes=56 * 2**20)


def shifted(value, steps):
    count = lax.axis_size(SPACE)
    first, last = max(0, -steps), min(count, count - steps)
    return lax.ppermute(value, SPACE, [(i, i + steps) for i in range(first, last)])


def emit_faces(tiles, table_ref, face_refs):
    for index, ref in enumerate(face_refs):
        for b in range(BR):
            if index < 2:
                block = tiles[b, :, :, :].reshape(8, 8, 8, CH)[:, 7 * index]
            else:
                block = tiles[b, 56 * (index - 2) : 56 * (index - 2) + 8]
            ref[64 * b : 64 * b + 64] = block.reshape(64, CH).astype(BF16)
        ref[256:272] = table_ref[...]


def prep_kernel(field_ref, table_ref, tiles_ref, ym_ref, yp_ref, xm_ref, xp_ref):
    for b in range(BR):
        for k in range(4):
            start = VOX * b + 128 * k
            turned = field_ref[:, start : start + 128].astype(F32).T
            tiles_ref[b, 16 * k : 16 * k + 16] = turned.reshape(16, 8, CH)
    emit_faces(tiles_ref, table_ref, (ym_ref, yp_ref, xm_ref, xp_ref))


def prep(field, table):
    face = jax.ShapeDtypeStruct((272, CH), BF16)
    return pl.pallas_call(
        prep_kernel,
        out_shape=[jax.ShapeDtypeStruct((BR, 64, 8, CH), F32)] + [face] * 4,
        in_specs=[VMEM] * 2,
        out_specs=[VMEM] * 5,
        compiler_params=PARAMS,
    )(field, table)


def exchange(faces):
    ym, yp, xm, xp = faces
    from_low = shifted(yp, 1)
    from_high = shifted(ym, -1)

    def column(plane, p):
        rows = [plane[64 * b + 8 * p : 64 * b + 8 * p + 8] for b in range(BR)]
        return rows + [plane[256:272]]

    up = jnp.concatenate([xp] + column(from_low, 7) + column(from_high, 7), axis=0)
    down = jnp.concatenate([xm] + column(from_low, 0) + column(from_high, 0), axis=0)
    return from_low, from_high, shifted(up, ROWS), shifted(down, -ROWS)


def pool_index(neighbours, halo):
    low, high, left, right = halo
    tables = {
        (-1, -1): left[304:320],
        (-1, 0): left[256:272],
        (-1, 1): left[352:368],
        (0, -1): low[256:272],
        (0, 1): high[256:272],
        (1, -1): right[304:320],
        (1, 0): right[256:272],
        (1, 1): right[352:368],
    }
    rows = []
    for d, facing in enumerate(compass):
        rows.append(tables[facing][7 - d, :SLOTS].astype(jnp.int32) + BASE[facing])
    values = jnp.concatenate(rows)
    entry = neighbours - 1
    hit = entry[:, :, None] == jnp.arange(8 * SLOTS, dtype=jnp.int32)
    remote = jnp.sum(jnp.where(hit, values, 0), axis=2)
    found = jnp.where(entry >= 8 * SLOTS, entry - 8 * SLOTS, remote)
    return jnp.where(neighbours == 0, ZERO, found)


def fill_pool(pool, tiles_ref, halo_refs):
    low_ref, high_ref, left_ref, right_ref = halo_refs

    def plane(ref, start):
        return ref[start : start + 64].astype(F32).reshape(8, 8, CH)

    for b in range(BR):
        pool[b] = tiles_ref[b]
        pool[ZERO, 16 * b : 16 * b + 16] = jnp.zeros((16, 8, CH), F32)
        low = plane(low_ref, 64 * b)
        high = plane(high_ref, 64 * b)
        for p in range(8):
            pool[BASE[0, -1] + b, 8 * p + 7] = low[p]
            pool[BASE[0, 1] + b, 8 * p] = high[p]
        pool[BASE[-1, 0] + b, 56:64] = plane(left_ref, 64 * b)
        pool[BASE[1, 0] + b, 0:8] = plane(right_ref, 64 * b)
    for ref, ex, p in ((left_ref, -1, 7), (right_ref, 1, 0)):
        for ey, q, start in ((-1, 7, 272), (1, 0, 320)):
            rows = ref[start : start + 32].astype(F32).reshape(BR, 8, CH)
            for b in range(BR):
                pool[BASE[ex, ey] + b, 8 * p + q] = rows[b]


def build_windows(index_ref, pool, windows):
    row = lax.broadcasted_iota(jnp.int32, (8, CH), 0)
    first, last = row == 0, row == 7

    def place(entries, p, q, at_p, at_q):
        shifted_rows = ([], [], [])
        for b in range(BR):
            below = pool[entries[b][0], 8 * p + q]
            centre = pool[entries[b][1], 8 * p + q]
            above = pool[entries[b][2], 8 * p + q]
            shifted_rows[0].append(pltpu.roll(jnp.where(last, below, centre), 1, 0))
            shifted_rows[1].append(centre)
            shifted_rows[2].append(pltpu.roll(jnp.where(first, above, centre), 7, 0))
        for k in range(3):
            windows[k, at_p, at_q] = jnp.concatenate(shifted_rows[k], axis=0).astype(BF16)

    for ox in (-1, 0, 1):
        for oy in (-1, 0, 1):
            column = 9 * (ox + 1) + 3 * (oy + 1)
            entries = [[index_ref[b, column + k] for k in range(3)] for b in range(BR)]
            p_edge = 7 if ox < 0 else 0
            q_edge = 7 if oy < 0 else 0
            p_at = 0 if ox < 0 else 9
            q_at = 0 if oy < 0 else 9
            if ox == 0 and oy == 0:

                def plane_body(p, carry, entries=entries):
                    for q in range(8):
                        place(entries, p, q, p + 1, q + 1)
                    return carry

                lax.fori_loop(0, 8, plane_body, 0)
            elif ox == 0:

                def p_body(p, carry, entries=entries, q_edge=q_edge, q_at=q_at):
                    place(entries, p, q_edge, p + 1, q_at)
                    return carry

                lax.fori_loop(0, 8, p_body, 0)
            elif oy == 0:

                def q_body(q, carry, entries=entries, p_edge=p_edge, p_at=p_at):
                    place(entries, p_edge, q, p_at, q + 1)
                    return carry

                lax.fori_loop(0, 8, q_body, 0)
            else:
                place(entries, p_edge, q_edge, p_at, q_at)


def window(windows, k, at_p, j):
    return windows[k, at_p, j : j + 8].reshape(256, CH)


def forward_kernel(
    index_ref,
    chan_ref,
    tiles_ref,
    low_ref,
    high_ref,
    left_ref,
    right_ref,
    weight_ref,
    cotangent_ref,
    table_ref,
    output_ref,
    gradh_ref,
    ym_ref,
    yp_ref,
    xm_ref,
    xp_ref,
    kernel_grad_ref,
    pool,
    windows,
    cot_tiles,
    out_tiles,
    out_turned,
    grad_rows,
    narrow,
    sums,
):
    fill_pool(pool, tiles_ref, (low_ref, high_ref, left_ref, right_ref))
    build_windows(index_ref, pool, windows)
    for b in range(BR):
        for k in range(4):
            start = VOX * b + 128 * k
            turned = cotangent_ref[:, start : start + 128].astype(F32).T
            cot_tiles[b, 16 * k : 16 * k + 16] = turned.reshape(16, 8, CH)

    def tap_weight(tap):
        return jnp.concatenate([weight_ref[s, tap] for s in range(4)], axis=0)

    def conv_body(p, carry):
        total = None
        for first in range(0, TAPS, 2):
            taps = range(first, min(first + 2, TAPS))
            left = [window(windows, t % 3, p + t // 9, t // 3 % 3) for t in taps]
            right = [tap_weight(t) for t in taps]
            term = jnp.dot(
                jnp.concatenate(left, axis=1), jnp.concatenate(right, axis=0), preferred_element_type=F32
            )
            total = term if total is None else total + term
        hidden = total.reshape(8, BR, 8, CH)
        for b in range(BR):
            h = hidden[:, b]
            feat = tiles_ref[b, pl.ds(8 * p, 8)]
            cot = cot_tiles[b, pl.ds(8 * p, 8)]
            sig = jax.nn.sigmoid(h)
            out_tiles[b, pl.ds(8 * p, 8)] = feat + h * sig
            grad = (cot * sig * (1.0 + h * (1.0 - sig))).astype(BF16).astype(F32)
            gradh_ref[b, pl.ds(8 * p, 8)] = grad
        return carry

    lax.fori_loop(0, 8, conv_body, 0)

    for b in range(BR):
        for k in range(4):
            start = VOX * b + 128 * k
            block = out_tiles[b, 16 * k : 16 * k + 16].reshape(128, CH)
            out_turned[:, start : start + 128] = block.T
    own = pl.multiple_of(chan_ref[0] * 32, 32)
    output_ref[...] = out_turned[pl.ds(own, 32), :].astype(BF16)
    emit_faces(gradh_ref, table_ref, (ym_ref, yp_ref, xm_ref, xp_ref))

    lane = lax.broadcasted_iota(jnp.int32, (CH, CH), 1)
    channel = lax.broadcasted_iota(jnp.int32, (CH, CH), 0)
    pick = [
        jnp.where((lane - 32 * k == channel - own) & (lane >= 32 * k) & (lane < 32 * k + 32), 1.0, 0.0).astype(BF16)
        for k in range(3)
    ]
    picks = jnp.concatenate(pick, axis=0)

    def narrow_body(p, carry):
        rows = [windows[k, p].reshape(320, CH) for k in range(3)]
        small = jnp.dot(jnp.concatenate(rows, axis=1), picks, preferred_element_type=F32)
        narrow[p] = small.astype(BF16).reshape(10, 32, CH)
        return carry

    lax.fori_loop(0, 10, narrow_body, 0)

    def turn_body(p, carry):
        parts = [gradh_ref[b, pl.ds(8 * p, 8)] for b in range(BR)]
        rows = jnp.stack(parts, axis=1).reshape(256, CH)
        for k in range(2):
            grad_rows[p, :, 128 * k : 128 * k + 128] = rows[128 * k : 128 * k + 128].T.astype(BF16)
        return carry

    lax.fori_loop(0, 8, turn_body, 0)

    sums[...] = jnp.zeros_like(sums)

    def sum_body(p, carry):
        left = grad_rows[p]
        for pair in range(9):
            i, j = pair // 3, pair % 3
            right = narrow[p + i, j : j + 8].reshape(256, CH)
            sums[pair] += jnp.dot(left, right, preferred_element_type=F32)
        return carry

    lax.fori_loop(0, 8, sum_body, 0)
    for pair in range(9):
        kernel_grad_ref[96 * pair : 96 * pair + 96] = sums[pair].T[:96]
    kernel_grad_ref[864:896] = jnp.zeros((32, CH), F32)


def forward(index, chan, tiles, halo, weight, cotangent, table):
    face = jax.ShapeDtypeStruct((272, CH), BF16)
    return pl.pallas_call(
        forward_kernel,
        out_shape=[
            jax.ShapeDtypeStruct((32, BR * VOX), BF16),
            jax.ShapeDtypeStruct((BR, 64, 8, CH), F32),
            face,
            face,
            face,
            face,
            jax.ShapeDtypeStruct((896, CH), F32),
        ],
        in_specs=[SMEM] * 2 + [VMEM] * 8,
        out_specs=[VMEM] * 7,
        scratch_shapes=[
            pltpu.VMEM((37, 64, 8, CH), F32),
            pltpu.VMEM((3, 10, 10, 32, CH), BF16),
            pltpu.VMEM((BR, 64, 8, CH), F32),
            pltpu.VMEM((BR, 64, 8, CH), F32),
            pltpu.VMEM((CH, BR * VOX), F32),
            pltpu.VMEM((8, CH, 256), BF16),
            pltpu.VMEM((10, 10, 32, CH), BF16),
            pltpu.VMEM((9, CH, CH), F32),
        ],
        compiler_params=PARAMS,
    )(index, chan, tiles, *halo, weight, cotangent, table)


def backward_kernel(
    index_ref,
    tiles_ref,
    low_ref,
    high_ref,
    left_ref,
    right_ref,
    weight_ref,
    cotangent_ref,
    grad_ref,
    pool,
    windows,
    result,
):
    fill_pool(pool, tiles_ref, (low_ref, high_ref, left_ref, right_ref))
    build_windows(index_ref, pool, windows)

    def conv_body(p, carry):
        total = None
        for first in range(0, TAPS, 2):
            taps = range(first, min(first + 2, TAPS))
            left = [window(windows, 2 - t % 3, p + 2 - t // 9, 2 - t // 3 % 3) for t in taps]
            right = [weight_ref[t] for t in taps]
            term = lax.dot_general(
                jnp.concatenate(left, axis=1),
                jnp.concatenate(right, axis=1),
                (((1,), (1,)), ((), ())),
                preferred_element_type=F32,
            )
            total = term if total is None else total + term
        rows = total.reshape(8, BR, 8, 32)
        for b in range(BR):
            result[b, pl.ds(8 * p, 8)] = rows[:, b]
        return carry

    lax.fori_loop(0, 8, conv_body, 0)
    for b in range(BR):
        for k in range(4):
            start = VOX * b + 128 * k
            block = result[b, 16 * k : 16 * k + 16].reshape(128, 32)
            summed = cotangent_ref[:, start : start + 128].astype(F32) + block.T
            grad_ref[:, start : start + 128] = summed.astype(BF16)


def backward(index, tiles, halo, weight, cotangent):
    return pl.pallas_call(
        backward_kernel,
        out_shape=jax.ShapeDtypeStruct((32, BR * VOX), BF16),
        in_specs=[SMEM] + [VMEM] * 7,
        out_specs=VMEM,
        scratch_shapes=[
            pltpu.VMEM((37, 64, 8, CH), F32),
            pltpu.VMEM((3, 10, 10, 32, CH), BF16),
            pltpu.VMEM((BR, 64, 8, 32), F32),
        ],
        compiler_params=PARAMS,
    )(index, tiles, *halo, weight, cotangent)


def ring_gather(value, axis):
    count = lax.axis_size(axis)
    blocks = [value]
    for step in range(1, count):
        blocks.append(lax.ppermute(value, axis, [(i, (i + step) % count) for i in range(count)]))
    return blocks


def spread(value, axis):
    count = lax.axis_size(axis)
    copies = jnp.broadcast_to(value[None], (count,) + value.shape)
    return lax.all_to_all(copies, axis, split_axis=0, concat_axis=0, tiled=True)


def reduce_space(partial):
    pieces = lax.all_to_all(partial.reshape(8, 112, CH), XC, split_axis=0, concat_axis=0, tiled=True)
    mine = jnp.sum(pieces, axis=0)
    column = jnp.sum(spread(mine, "z"), axis=0)
    return spread(column, XC).reshape(896, CH)[:864]


def per_device(features, weight, cotangent, neighbours, send_slots):
    feat_own = features.reshape(32, BR * VOX)
    cot_own = cotangent.reshape(32, BR * VOX)
    table = jnp.pad(send_slots.astype(BF16), ((0, 8), (0, CH - SLOTS)))
    feat_all = lax.all_gather(feat_own, "chan", axis=0, tiled=True)
    weight_all = lax.all_gather(weight, "chan", axis=0, tiled=False)
    cot_all = lax.all_gather(cot_own, "chan", axis=0, tiled=True)
    chan = lax.axis_index("chan").astype(jnp.int32).reshape(1)
    tiles, *faces = prep(feat_all, table)
    halo = exchange(faces)
    index = pool_index(neighbours, halo)
    out, grad_tiles, *rest = forward(index, chan, tiles, halo, weight_all, cot_all, table)
    grad_faces, partial = rest[:4], rest[4]
    grad_halo = exchange(grad_faces)
    grad_weight = reduce_space(partial)
    grad_input = backward(index, grad_tiles, grad_halo, weight, cot_own)
    return (
        out.reshape(32, BR, VOX),
        grad_input.reshape(32, BR, VOX),
        grad_weight.reshape(TAPS, 32, CH),
    )


def solution(mesh):
    fine = Mesh(mesh.devices.reshape(4, 8, 2, 4), ("x", "z", "core", "chan"))
    return jax.shard_map(
        per_device,
        mesh=fine,
        in_specs=(
            P("chan", SPACE, None),
            P(None, "chan", None),
            P("chan", SPACE, None),
            P(SPACE, None),
            P(SPACE, None),
        ),
        out_specs=(P("chan", SPACE, None), P("chan", SPACE, None), P(None, "chan", None)),
        check_vma=False,
    )
```

time: 1140 us -> 154 us (0.14); the launches traced: 1120 us -> 151 us
  local copies, waits for them, and re-layouts: 703 us -> 9.05 us
  waiting for transfers between devices: 209 us -> 31.6 us
  other arithmetic: 101 us -> 1.99 us
  blocking collectives: 10.8 us -> 37.3 us
  Pallas kernels: 0 us -> 25.4 us
  starting transfers between devices: 64.8 us -> 44.5 us
  between operations: 18.4 us -> 0.99 us
  matrix products: 15.1 us -> 0 us
    unnamed x1029 -> x63, local copies, waits for them, and re-layouts: 294 us -> 3.4 us
    psum x1 -> x0, waiting for transfers between devices: 182 us -> none  [per_device(): grad_weight = lax.psum(partial_grad, 'space')]
    slice x139 -> x1, local copies, waits for them, and re-layouts: 162 us -> 0.79 us  [reduce_space(): return spread(column, XC).reshape(896, CH)[:864]]
    concatenate x58 -> x5, local copies, waits for them, and re-layouts: 118 us -> 0.12 us  [the longest x1 0.08 us: pool_index(): values = jnp.concatenate(rows)]
    gather x68 -> x0, local copies, waits for them, and re-layouts: 80.4 us -> none  [the longest x52 67.6 us: brick_margin(): jnp.take(slab_pool, lookup[:, 9 * i + 3 * j + k], axis=1)]
    select_n x82 -> x1, other arithmetic: 42.5 us -> 0.59 us  [pool_index(): return jnp.where(neighbours == 0, ZERO, found)]
    ppermute x16 -> x8, starting transfers between devices: 60.5 us -> 20.4 us  [shifted(): lax.ppermute(value, SPACE, [(i, i + steps) for i in range(first, last)])]
    ppermute x16 -> x0, local copies, waits for them, and re-layouts: 30 us -> none  [shifted(): lax.ppermute(value, axis, [(source, source + steps) for source in range(f...]
  transfers between devices with their start and end apart: 20 -> 11, of which waited for: 5 -> 6; matrix products, arithmetic and copies ran while one was open for 15% -> 2% of each run, Pallas kernels for 0% -> 5%
where the time goes in v1:
time: 154 us; the launch traced here: 151 us
  starting transfers between devices  44.5 us (29%)
  blocking collectives  37.3 us (24%)
  waiting for transfers between devices  31.6 us (21%)
  Pallas kernels  25.4 us (16%)
  local copies, waits for them, and re-layouts  9.05 us (6%)
  other arithmetic  1.99 us (1%)
    ppermute x8, starting transfers between devices, shifted(): lax.ppermute(value, SPACE, [(i, i + steps) for i in range(first, last)])  20.4 us
    all_to_all x2, waiting for transfers between devices, spread(): return lax.all_to_all(copies, axis, split_axis=0, concat_axis=0, tiled=True)  15.4 us
    pallas_call x1, Pallas kernels, forward(): pl.pallas_call(forward_kernel, out_shape=[jax.ShapeDtypeStruct((32, BR *...  15 us
    all_to_all x1, starting transfers between devices, reduce_space(): lax.all_to_all(partial.reshape(8, 112, CH), XC, split_axis=0, concat_axis...  13.8 us
    all_gather x1, blocking collectives, per_device(): feat_all = lax.all_gather(feat_own, 'chan', axis=0, tiled=True)  13 us
    ppermute x8, waiting for transfers between devices, shifted(): lax.ppermute(value, SPACE, [(i, i + steps) for i in range(first, last)])  12.8 us
    all_gather x1, blocking collectives, per_device(): cot_all = lax.all_gather(cot_own, 'chan', axis=0, tiled=True)  12.3 us
    all_gather x1, blocking collectives, per_device(): weight_all = lax.all_gather(weight, 'chan', axis=0, tiled=False)  11.9 us
  transfers between devices with their start and end apart: 11, of which 6 were waited for; matrix products, arithmetic and copies ran while one was open for 2% of the time, Pallas kernels for 5%

profile of v1, /device:TPU:1, one launch (start us, length us, event | category | flops | bytes accessed | tf_op | source)
XLA Modules:
  0.0 150.8 jit_solution(5188125404666149090)
XLA Ops:
  1.3 0.9 copy.10
  2.3 13.0 %all_gather.12.field_ref = bf16[128,2048]{1,0:T(8,128)(2,1)} all-gather(bf16[32,2048]{1,0:T(8,128)(2,1)S(1)} %bitcast.29), channel_id=1, replica_groups=mesh['x'=4,'z'=8,'core'=2,'chan'=4] {'chan'}, dimensions={0}, use_global_device_ids=true | all-gather | bytes 655360 | tf_op jit(solution)/shard_map/all_gather | solution.py:402
  15.8 2.3 %shard_map.76 = (f32[4,64,8,128]{3,2,1,0:T(8,128)}, bf16[272,128]{1,0:T(8,128)(2,1)}, bf16[272,128]{1,0:T(8,128)(2,1)}, bf16[272,128]{1,0:T(8,128)(2,1)}, bf16[272,128]{1,0:T(8,128)(2,1)}) custom-call(bf16[128,2048]{1,0:T(8,128)(2,1)} %all_gather.12.field_ref, bf16[16,128]{1,0:T(8,128)(2,1)} %pad.4.table_ref), custom_call_target="tpu_custom_call" | custom-call | tf_op jit(solution)/shard_map/pallas_call | solution.py:55
  18.1 6.0 %collective-permute-start = (bf16[272,128]{1,0:T(8,128)(2,1)}, bf16[272,128]{1,0:T(8,128)(2,1)S(1)}, u32[]{:S(2)}, u32[]{:S(2)}) collective-permute-start(bf16[272,128]{1,0:T(8,128)(2,1)} %get-tuple-element.16), channel_id=1, source_target_pairs={{0,4},{4,8},{8,12},{12,16},{16,20},{20,24},{24,28},{28,32},{32,36}... | collective-permute-start | bytes 208904 | tf_op jit(solution)/shard_map/ppermute | solution.py:30
  24.1 1.9 %collective-permute-start.1 = (bf16[272,128]{1,0:T(8,128)(2,1)}, bf16[272,128]{1,0:T(8,128)(2,1)S(1)}, u32[]{:S(2)}, u32[]{:S(2)}) collective-permute-start(bf16[272,128]{1,0:T(8,128)(2,1)} %get-tuple-element.17), channel_id=1, source_target_pairs={{4,0},{8,4},{12,8},{16,12},{20,16},{24,20},{28,24},{32,28},{36,32}... | collective-permute-start | bytes 208904 | tf_op jit(solution)/shard_map/ppermute | solution.py:30
  26.9 12.3 %all_gather.15.cotangent_ref = bf16[128,2048]{1,0:T(8,128)(2,1)} all-gather(bf16[32,2048]{1,0:T(8,128)(2,1)S(1)} %bitcast.27), channel_id=1, replica_groups=mesh['x'=4,'z'=8,'core'=2,'chan'=4] {'chan'}, dimensions={0}, use_global_device_ids=true | all-gather | bytes 655360 | tf_op jit(solution)/shard_map/all_gather | solution.py:404
  39.3 11.9 %all-gather = bf16[108,32,128]{2,1,0:T(8,128)(2,1)} all-gather(bf16[27,32,128]{2,1,0:T(8,128)(2,1)S(1)} %copy-done.1), channel_id=2, replica_groups=mesh['x'=4,'z'=8,'core'=2,'chan'=4] {'chan'}, dimensions={0}, use_global_device_ids=true | all-gather | bytes 1105920 | tf_op jit(solution)/shard_map/all_gather | solution.py:403
  51.4 4.3 %collective-permute-start.2 = (bf16[368,128]{1,0:T(8,128)(2,1)S(1)}, bf16[368,128]{1,0:T(8,128)(2,1)S(1)}, u32[]{:S(2)}, u32[]{:S(2)}) collective-permute-start(bf16[368,128]{1,0:T(8,128)(2,1)S(1)} %constant_dynamic-update-slice_fusion), channel_id=1, source_target_pairs={{0,16},{4,20},{8,24},{12,28},{16,32},{20,36},{24,40},{28,44},{32,4... | collective-permute-start | bytes 282632 | tf_op jit(solution)/shard_map/ppermute | solution.py:30
  55.7 1.3 collective-permute-start.3
  57.3 5.4 %collective-permute-done.3.right_ref = bf16[368,128]{1,0:T(8,128)(2,1)S(1)} collective-permute-done((bf16[368,128]{1,0:T(8,128)(2,1)S(1)}, bf16[368,128]{1,0:T(8,128)(2,1)S(1)}, u32[]{:S(2)}, u32[]{:S(2)}) %collective-permute-start.3) | collective-permute-done | bytes 94240 | tf_op jit(solution)/shard_map/ppermute | solution.py:30
  64.1 15.0 %shard_map.77 = (bf16[32,2048]{1,0:T(8,128)(2,1)}, f32[4,64,8,128]{3,2,1,0:T(8,128)}, bf16[272,128]{1,0:T(8,128)(2,1)}, bf16[272,128]{1,0:T(8,128)(2,1)}, bf16[2...) custom-call(s32[4,27]{1,0:T(4,128)} %select_select_fusion.index_ref, s32[1]{0:T(128)} %bitcast.8.chan_ref, ...), custom_call_target="tpu_custom_call" | custom-call | tf_op jit(solution)/shard_map/pallas_call | solution.py:291
  79.1 13.8 %all-to-all-start = ((f32[8,112,128]{2,1,0:T(8,128)}), f32[8,112,128]{2,1,0:T(8,128)S(1)}, u32[]{:S(2)}, u32[]{:S(2)}) async-start(f32[8,112,128]{2,1,0:T(8,128)} %bitcast.30), calls=%async_computation | async-start | bytes 917504 | tf_op jit(solution)/shard_map/all_to_all | solution.py:392
  93.0 1.9 %collective-permute-start.4 = (bf16[272,128]{1,0:T(8,128)(2,1)S(1)}, bf16[272,128]{1,0:T(8,128)(2,1)S(1)}, u32[]{:S(2)}, u32[]{:S(2)}) collective-permute-start(bf16[272,128]{1,0:T(8,128)(2,1)S(1)} %copy-done.18), channel_id=1, source_target_pairs={{0,4},{4,8},{8,12},{12,16},{16,20},{20,24},{24,28},{28,32},{32,36}... | collective-permute-start | bytes 208904 | tf_op jit(solution)/shard_map/ppermute | solution.py:30
  94.9 2.4 %collective-permute-start.5 = (bf16[272,128]{1,0:T(8,128)(2,1)S(1)}, bf16[272,128]{1,0:T(8,128)(2,1)S(1)}, u32[]{:S(2)}, u32[]{:S(2)}) collective-permute-start(bf16[272,128]{1,0:T(8,128)(2,1)S(1)} %copy-done.17), channel_id=1, source_target_pairs={{4,0},{8,4},{12,8},{16,12},{20,16},{24,20},{28,24},{32,28},{36,32}... | collective-permute-start | bytes 208904 | tf_op jit(solution)/shard_map/ppermute | solution.py:30
  97.4 0.9 copy-done.12
  98.3 3.4 %all-to-all-done = f32[8,112,128]{2,1,0:T(8,128)S(1)} async-done(((f32[8,112,128]{2,1,0:T(8,128)}), f32[8,112,128]{2,1,0:T(8,128)S(1)}, u32[]{:S(2)}, u32[]{:S(2)}) %all-to-all-start) | async-done | bytes 458784 | tf_op jit(solution)/shard_map/all_to_all | solution.py:392
  102.6 5.1 %all-to-all-start.1 = ((f32[8,112,128]{2,1,0:T(8,128)}), f32[8,112,128]{2,1,0:T(8,128)S(1)}, u32[]{:S(2)}, u32[]{:S(2)}) async-start(f32[8,112,128]{2,1,0:T(8,128)} %broadcast_in_dim.29), calls=%async_computation.1 | async-start | bytes 917504 | tf_op jit(solution)/shard_map/all_to_all | solution.py:388
  107.8 15.4 %all-to-all-done.1 = f32[8,112,128]{2,1,0:T(8,128)S(1)} async-done(((f32[8,112,128]{2,1,0:T(8,128)}), f32[8,112,128]{2,1,0:T(8,128)S(1)}, u32[]{:S(2)}, u32[]{:S(2)}) %all-to-all-start.1) | async-done | bytes 458784 | tf_op jit(solution)/shard_map/all_to_all | solution.py:388
  124.0 5.1 %all-to-all-start.2 = ((f32[8,112,128]{2,1,0:T(8,128)}), f32[8,112,128]{2,1,0:T(8,128)S(1)}, u32[]{:S(2)}, u32[]{:S(2)}) async-start(f32[8,112,128]{2,1,0:T(8,128)} %broadcast_in_dim.30), calls=%async_computation.2 | async-start | bytes 917504 | tf_op jit(solution)/shard_map/all_to_all | solution.py:388
  129.1 1.3 collective-permute-start.6
  130.4 1.3 collective-permute-start.7
  132.6 7.0 %collective-permute-done.7.right_ref = bf16[368,128]{1,0:T(8,128)(2,1)S(1)} collective-permute-done((bf16[368,128]{1,0:T(8,128)(2,1)S(1)}, bf16[368,128]{1,0:T(8,128)(2,1)S(1)}, u32[]{:S(2)}, u32[]{:S(2)}) %collective-permute-start.7) | collective-permute-done | bytes 94240 | tf_op jit(solution)/shard_map/ppermute | solution.py:30
  140.3 8.1 %shard_map.78 = bf16[32,2048]{1,0:T(8,128)(2,1)} custom-call(s32[4,27]{1,0:T(4,128)} %select_select_fusion.index_ref, f32[4,64,8,128]{3,2,1,0:T(8,128)} %get-tuple-element.21.tiles_ref, bf16[272,128]{1,0:T(8,128)(2,1)} %copy-done.4, bf16[272,128]{1,0:T(8,128)(2,1)} %copy-done.5, bf16[368,128]{1,0:T(8,128)(2,1)} %copy-done.10, bf16[368,128]{1,0:T(8,128)(2,1)} %copy-done.11, ...), custom_call_target="tpu_custom_call" | custom-call | tf_op jit(solution)/shard_map/pallas_call | solution.py:363
  148.4 1.6 %reshape.61 = bf16[32,4,512]{2,1,0:T(4,128)(2,1)} reshape(bf16[32,2048]{1,0:T(8,128)(2,1)} %shard_map.78) | data formatting | bytes 262144 | tf_op jit(solution)/shard_map/reshape | solution.py:416
  (90 shorter events, 8.0 us)
Async XLA Ops:
  15.8 11.0 %copy-start.2 = (bf16[32,4,512]{2,1,0:T(4,128)(2,1)S(1)}, bf16[32,4,512]{2,1,0:T(4,128)(2,1)}, u32[]{:S(2)}) copy-start(bf16[32,4,512]{2,1,0:T(4,128)(2,1)} %param.7) | copy-start | bytes 393220
  18.1 33.1 %collective-permute-start = (bf16[272,128]{1,0:T(8,128)(2,1)}, bf16[272,128]{1,0:T(8,128)(2,1)S(1)}, u32[]{:S(2)}, u32[]{:S(2)}) collective-permute-start(bf16[272,128]{1,0:T(8,128)(2,1)} %get-tuple-element.16), channel_id=1, source_target_pairs={{0,4},{4,8},{8,12},{12,16},{16,20},{20,24},{24,28},{28,32},{32,36}... | collective-permute-start | bytes 208904 | tf_op jit(solution)/shard_map/ppermute | solution.py:30
  24.1 27.2 %collective-permute-start.1 = (bf16[272,128]{1,0:T(8,128)(2,1)}, bf16[272,128]{1,0:T(8,128)(2,1)S(1)}, u32[]{:S(2)}, u32[]{:S(2)}) collective-permute-start(bf16[272,128]{1,0:T(8,128)(2,1)} %get-tuple-element.17), channel_id=1, source_target_pairs={{4,0},{8,4},{12,8},{16,12},{20,16},{24,20},{28,24},{32,28},{36,32}... | collective-permute-start | bytes 208904 | tf_op jit(solution)/shard_map/ppermute | solution.py:30
  26.9 12.4 %copy-start = (bf16[4,8,4,512]{3,1,2,0:T(8,128)(2,1)}, bf16[4,8,4,512]{3,1,2,0:T(8,128)(2,1)S(1)}, u32[]{:S(2)}) copy-start(bf16[4,8,4,512]{3,1,2,0:T(8,128)(2,1)S(1)} %copy.11) | copy-start | bytes 393220
  26.9 12.4 %copy-start.1 = (bf16[27,32,128]{2,1,0:T(8,128)(2,1)S(1)}, bf16[27,32,128]{2,1,0:T(8,128)(2,1)}, u32[]{:S(2)}) copy-start(bf16[27,32,128]{2,1,0:T(8,128)(2,1)} %weight_ref.1) | copy-start | bytes 663556
  39.3 12.0 %copy-start.14 = (bf16[272,128]{1,0:T(8,128)(2,1)S(1)}, bf16[272,128]{1,0:T(8,128)(2,1)}, u32[]{:S(2)}) copy-start(bf16[272,128]{1,0:T(8,128)(2,1)} %get-tuple-element.18) | copy-start | bytes 208900
  39.3 11.9 %copy-start.15 = (bf16[272,128]{1,0:T(8,128)(2,1)S(1)}, bf16[272,128]{1,0:T(8,128)(2,1)}, u32[]{:S(2)}) copy-start(bf16[272,128]{1,0:T(8,128)(2,1)} %get-tuple-element.15) | copy-start | bytes 208900
  51.2 11.5 %copy-start.6 = (bf16[272,128]{1,0:T(8,128)(2,1)}, bf16[272,128]{1,0:T(8,128)(2,1)S(1)}, u32[]{:S(2)}) copy-start(bf16[272,128]{1,0:T(8,128)(2,1)S(1)} %collective-permute-done.low_ref) | copy-start | bytes 208900
  51.3 12.8 %copy-start.7 = (bf16[272,128]{1,0:T(8,128)(2,1)}, bf16[272,128]{1,0:T(8,128)(2,1)S(1)}, u32[]{:S(2)}) copy-start(bf16[272,128]{1,0:T(8,128)(2,1)S(1)} %collective-permute-done.1.high_ref) | copy-start | bytes 208900
  51.4 5.9 %collective-permute-start.2 = (bf16[368,128]{1,0:T(8,128)(2,1)S(1)}, bf16[368,128]{1,0:T(8,128)(2,1)S(1)}, u32[]{:S(2)}, u32[]{:S(2)}) collective-permute-start(bf16[368,128]{1,0:T(8,128)(2,1)S(1)} %constant_dynamic-update-slice_fusion), channel_id=1, source_target_pairs={{0,16},{4,20},{8,24},{12,28},{16,32},{20,36},{24,40},{28,44},{32,4... | collective-permute-start | bytes 282632 | tf_op jit(solution)/shard_map/ppermute | solution.py:30
  55.7 7.0 %collective-permute-start.3 = (bf16[368,128]{1,0:T(8,128)(2,1)S(1)}, bf16[368,128]{1,0:T(8,128)(2,1)S(1)}, u32[]{:S(2)}, u32[]{:S(2)}) collective-permute-start(bf16[368,128]{1,0:T(8,128)(2,1)S(1)} %constant_dynamic-update-slice_fusion.9), channel_id=1, source_target_pairs={{16,0},{20,4},{24,8},{28,12},{32,16},{36,20},{40,24},{44,28},{48,3... | collective-permute-start | bytes 282632 | tf_op jit(solution)/shard_map/ppermute | solution.py:30
  79.1 13.9 %copy-start.18 = (bf16[272,128]{1,0:T(8,128)(2,1)S(1)}, bf16[272,128]{1,0:T(8,128)(2,1)}, u32[]{:S(2)}) copy-start(bf16[272,128]{1,0:T(8,128)(2,1)} %get-tuple-element.22) | copy-start | bytes 208900
  79.1 15.8 %copy-start.17 = (bf16[272,128]{1,0:T(8,128)(2,1)S(1)}, bf16[272,128]{1,0:T(8,128)(2,1)}, u32[]{:S(2)}) copy-start(bf16[272,128]{1,0:T(8,128)(2,1)} %get-tuple-element.23) | copy-start | bytes 208900
  79.1 18.2 %copy-start.13 = (bf16[272,128]{1,0:T(8,128)(2,1)S(1)}, bf16[272,128]{1,0:T(8,128)(2,1)}, u32[]{:S(2)}) copy-start(bf16[272,128]{1,0:T(8,128)(2,1)} %get-tuple-element.24) | copy-start | bytes 208900
  79.1 22.6 %all-to-all-start = ((f32[8,112,128]{2,1,0:T(8,128)}), f32[8,112,128]{2,1,0:T(8,128)S(1)}, u32[]{:S(2)}, u32[]{:S(2)}) async-start(f32[8,112,128]{2,1,0:T(8,128)} %bitcast.30), calls=%async_computation | async-start | bytes 917504 | tf_op jit(solution)/shard_map/all_to_all | solution.py:392
  93.0 5.2 %collective-permute-start.4 = (bf16[272,128]{1,0:T(8,128)(2,1)S(1)}, bf16[272,128]{1,0:T(8,128)(2,1)S(1)}, u32[]{:S(2)}, u32[]{:S(2)}) collective-permute-start(bf16[272,128]{1,0:T(8,128)(2,1)S(1)} %copy-done.18), channel_id=1, source_target_pairs={{0,4},{4,8},{8,12},{12,16},{16,20},{20,24},{24,28},{28,32},{32,36}... | collective-permute-start | bytes 208904 | tf_op jit(solution)/shard_map/ppermute | solution.py:30
  94.9 12.8 %collective-permute-start.5 = (bf16[272,128]{1,0:T(8,128)(2,1)S(1)}, bf16[272,128]{1,0:T(8,128)(2,1)S(1)}, u32[]{:S(2)}, u32[]{:S(2)}) collective-permute-start(bf16[272,128]{1,0:T(8,128)(2,1)S(1)} %copy-done.17), channel_id=1, source_target_pairs={{4,0},{8,4},{12,8},{16,12},{20,16},{24,20},{28,24},{32,28},{36,32}... | collective-permute-start | bytes 208904 | tf_op jit(solution)/shard_map/ppermute | solution.py:30
  102.6 20.6 %all-to-all-start.1 = ((f32[8,112,128]{2,1,0:T(8,128)}), f32[8,112,128]{2,1,0:T(8,128)S(1)}, u32[]{:S(2)}, u32[]{:S(2)}) async-start(f32[8,112,128]{2,1,0:T(8,128)} %broadcast_in_dim.29), calls=%async_computation.1 | async-start | bytes 917504 | tf_op jit(solution)/shard_map/all_to_all | solution.py:388
  107.7 22.7 %copy-start.5 = (bf16[272,128]{1,0:T(8,128)(2,1)}, bf16[272,128]{1,0:T(8,128)(2,1)S(1)}, u32[]{:S(2)}) copy-start(bf16[272,128]{1,0:T(8,128)(2,1)S(1)} %collective-permute-done.5.high_ref) | copy-start | bytes 208900
  124.0 7.7 %copy-start.3 = (bf16[32,2048]{1,0:T(8,128)(2,1)S(1)}, bf16[32,2048]{1,0:T(8,128)(2,1)}, u32[]{:S(2)}) copy-start(bf16[32,2048]{1,0:T(8,128)(2,1)} %get-tuple-element.20) | copy-start | bytes 393220
  124.0 26.0 %all-to-all-start.2 = ((f32[8,112,128]{2,1,0:T(8,128)}), f32[8,112,128]{2,1,0:T(8,128)S(1)}, u32[]{:S(2)}, u32[]{:S(2)}) async-start(f32[8,112,128]{2,1,0:T(8,128)} %broadcast_in_dim.30), calls=%async_computation.2 | async-start | bytes 917504 | tf_op jit(solution)/shard_map/all_to_all | solution.py:388
  129.1 3.5 %collective-permute-start.6 = (bf16[368,128]{1,0:T(8,128)(2,1)S(1)}, bf16[368,128]{1,0:T(8,128)(2,1)S(1)}, u32[]{:S(2)}, u32[]{:S(2)}) collective-permute-start(bf16[368,128]{1,0:T(8,128)(2,1)S(1)} %constant_dynamic-update-slice_fusion.20), channel_id=1, source_target_pairs={{0,16},{4,20},{8,24},{12,28},{16,32},{20,36},{24,40},{28,44},{32,4... | collective-permute-start | bytes 282632 | tf_op jit(solution)/shard_map/ppermute | solution.py:30
  130.4 9.2 %collective-permute-start.7 = (bf16[368,128]{1,0:T(8,128)(2,1)S(1)}, bf16[368,128]{1,0:T(8,128)(2,1)S(1)}, u32[]{:S(2)}, u32[]{:S(2)}) collective-permute-start(bf16[368,128]{1,0:T(8,128)(2,1)S(1)} %constant_dynamic-update-slice_fusion.29), channel_id=1, source_target_pairs={{16,0},{20,4},{24,8},{28,12},{32,16},{36,20},{40,24},{44,28},{48,3... | collective-permute-start | bytes 282632 | tf_op jit(solution)/shard_map/ppermute | solution.py:30
  132.6 7.0 %copy-start.10 = (bf16[368,128]{1,0:T(8,128)(2,1)}, bf16[368,128]{1,0:T(8,128)(2,1)S(1)}, u32[]{:S(2)}) copy-start(bf16[368,128]{1,0:T(8,128)(2,1)S(1)} %collective-permute-done.6.left_ref) | copy-start | bytes 282628
  (6 other events, 14.0 us)

commit v2 on v0

v2 whole, which is shorter than its diff:
```python
import jax
import jax.numpy as jnp
from jax import lax
from jax.experimental import pallas as pl
from jax.experimental.pallas import tpu as pltpu
from jax.sharding import Mesh, PartitionSpec as P

ROWS = 4
CH = 128
OWN = 32
BR = 4
VOX = 512
TAPS = 27
SLOTS = 8
F32 = jnp.float32
BF16 = jnp.bfloat16
SPACE = ("x", "z", "core")
VMEM = pl.BlockSpec(memory_space=pltpu.VMEM)
SMEM = pl.BlockSpec(memory_space=pltpu.SMEM)
LIMIT = 56 * 2**20

compass = ((-1, -1), (-1, 0), (-1, 1), (0, -1), (0, 1), (1, -1), (1, 0), (1, 1))
SIDE_M, SIDE_N, SIDE_L, SIDE_R, SIDE_LM, SIDE_LN, SIDE_RM, SIDE_RN, ZERO = range(4, 40, 4)


def params():
    return pltpu.CompilerParams(vmem_limit_bytes=LIMIT)


def cost(flops, moved):
    return pl.CostEstimate(flops=flops, bytes_accessed=moved, transcendentals=0)


def shifted(value, steps):
    count = lax.axis_size(SPACE)
    first, last = max(0, -steps), min(count, count - steps)
    return lax.ppermute(value, SPACE, [(i, i + steps) for i in range(first, last)])


def emit_faces(core, tiles, table_ref, face_refs):
    for index, ref in enumerate(face_refs):
        for b in range(BR):
            if index == 0:
                rows = [tiles[b, 8 * p + 7 * (1 - core)] for p in range(8)]
            elif index == 1:
                rows = [tiles[b, 8 * p + 7 * core] for p in range(8)]
            else:
                rows = [tiles[b, 56 * (index - 2) + q] for q in range(8)]
            ref[64 * b : 64 * b + 64] = jnp.concatenate(rows, axis=0).astype(BF16)
        ref[256:272] = jnp.zeros((16, CH), BF16) if table_ref is None else table_ref[...]


def prep_kernel(core_ref, own_ref, ring1_ref, ring2_ref, ring3_ref, table_ref, tiles_ref, *face_refs):
    for b in range(BR):
        for k in range(4):
            start = VOX * b + 128 * k
            parts = [ref[:, start : start + 128] for ref in (own_ref, ring1_ref, ring2_ref, ring3_ref)]
            turned = jnp.concatenate(parts, axis=0).astype(F32).T
            tiles_ref[b, 16 * k : 16 * k + 16] = turned.reshape(16, 8, CH)
    emit_faces(core_ref[0], tiles_ref, table_ref, face_refs)


def prep(core, blocks, table):
    face = jax.ShapeDtypeStruct((272, CH), BF16)
    return pl.pallas_call(
        prep_kernel,
        out_shape=[jax.ShapeDtypeStruct((BR, 64, 8, CH), F32)] + [face] * 4,
        in_specs=[SMEM] + [VMEM] * 5,
        out_specs=[VMEM] * 5,
        compiler_params=params(),
        cost_estimate=cost(0, 2**22),
    )(core, *blocks, table)


def turn_kernel(chan_ref, own_ref, ring1_ref, ring2_ref, ring3_ref, tiles_ref, whole):
    for step, ref in enumerate((own_ref, ring1_ref, ring2_ref, ring3_ref)):
        block = lax.rem(chan_ref[0] + 4 - step, 4)
        whole[pl.ds(pl.multiple_of(block * OWN, OWN), OWN), :] = ref[...].astype(F32)
    for b in range(BR):
        for k in range(4):
            start = VOX * b + 128 * k
            tiles_ref[b, 16 * k : 16 * k + 16] = whole[:, start : start + 128].T.reshape(16, 8, CH)


def turn(chan, blocks):
    return pl.pallas_call(
        turn_kernel,
        out_shape=jax.ShapeDtypeStruct((BR, 64, 8, CH), F32),
        in_specs=[SMEM] + [VMEM] * 4,
        out_specs=VMEM,
        scratch_shapes=[pltpu.VMEM((CH, BR * VOX), F32)],
        compiler_params=params(),
        cost_estimate=cost(0, 2**22),
    )(chan, *blocks)


def column(plane, p):
    rows = [plane[64 * b + 8 * p : 64 * b + 8 * p + 8] for b in range(BR)]
    return rows + [plane[256:272]]


def exchange(faces):
    face_m, face_n, low, high = faces
    count = lax.axis_size(SPACE)
    across = [(s, s + 1) for s in range(count) if s % 4 == 1] + [(s, s - 1) for s in range(count) if s % 4 == 2]
    side_n = lax.ppermute(face_n, SPACE, across)
    side_m = lax.ppermute(face_m, "core", [(0, 1), (1, 0)])
    up = jnp.concatenate([high] + column(side_m, 7) + column(side_n, 7), axis=0)
    down = jnp.concatenate([low] + column(side_m, 0) + column(side_n, 0), axis=0)
    return side_m, side_n, shifted(up, ROWS), shifted(down, -ROWS)


def pool_index(neighbours, core, halo):
    side_m, side_n, left, right = halo
    tables = {
        SIDE_M: side_m[256:272],
        SIDE_N: side_n[256:272],
        SIDE_L: left[256:272],
        SIDE_R: right[256:272],
        SIDE_LM: left[304:320],
        SIDE_LN: left[352:368],
        SIDE_RM: right[304:320],
        SIDE_RN: right[352:368],
    }
    ends = {-1: (SIDE_LM, SIDE_LN), 0: (SIDE_M, SIDE_N), 1: (SIDE_RM, SIDE_RN)}

    def row(side, d):
        return tables[side][7 - d, :SLOTS].astype(jnp.int32) + side

    rows = []
    for d, (ex, ey) in enumerate(compass):
        if ey == 0:
            rows.append(row(SIDE_L if ex < 0 else SIDE_R, d))
        else:
            near, far = ends[ex] if ey > 0 else ends[ex][::-1]
            rows.append(jnp.where(core == 0, row(near, d), row(far, d)))
    values = jnp.concatenate(rows)
    entry = neighbours - 1
    hit = entry[:, :, None] == jnp.arange(8 * SLOTS, dtype=jnp.int32)
    remote = jnp.sum(jnp.where(hit, values, 0), axis=2)
    found = jnp.where(entry >= 8 * SLOTS, entry - 8 * SLOTS, remote)
    return jnp.where(neighbours == 0, ZERO, found)


def fill_pool(core, pool, tiles_ref, halo_refs):
    side_m, side_n, left, right = halo_refs
    q_m, q_n = 7 * core, 7 * (1 - core)

    def plane(ref, start):
        return ref[start : start + 64].astype(F32).reshape(8, 8, CH)

    for b in range(BR):
        for first in range(0, 64, 8):
            pool[b, first : first + 8] = tiles_ref[b, first : first + 8]
            pool[ZERO, first : first + 8] = jnp.zeros((8, 8, CH), F32)
        for ref, side, q in ((side_m, SIDE_M, q_m), (side_n, SIDE_N, q_n)):
            rows = plane(ref, 64 * b)
            for p in range(8):
                pool[side + b, 8 * p + q] = rows[p]
        pool[SIDE_L + b, 56:64] = plane(left, 64 * b)
        pool[SIDE_R + b, 0:8] = plane(right, 64 * b)
    for ref, sides, p in ((left, (SIDE_LM, SIDE_LN), 7), (right, (SIDE_RM, SIDE_RN), 0)):
        for side, q, start in ((sides[0], q_m, 272), (sides[1], q_n, 320)):
            rows = ref[start : start + 32].astype(F32).reshape(BR, 8, CH)
            for b in range(BR):
                pool[side + b, 8 * p + q] = rows[b]


def three_shifts(entries, pool, p, q):
    row = lax.broadcasted_iota(jnp.int32, (8, CH), 0)
    first, last = row == 0, row == 7
    shifts = ([], [], [])
    for b in range(BR):
        below = pool[entries[b][0], 8 * p + q]
        centre = pool[entries[b][1], 8 * p + q]
        above = pool[entries[b][2], 8 * p + q]
        shifts[0].append(pltpu.roll(jnp.where(last, below, centre), 1, 0))
        shifts[1].append(centre)
        shifts[2].append(pltpu.roll(jnp.where(first, above, centre), 7, 0))
    return [jnp.concatenate(rows, axis=0).astype(BF16) for rows in shifts]


def inner_windows(neighbours_ref, tiles_ref, zero, windows):
    zero[...] = jnp.zeros_like(zero)
    blank = jnp.zeros((10, 32, CH), BF16)
    for k in range(3):
        windows[k, 0] = blank
        windows[k, 9] = blank
        for p in range(1, 9):
            windows[k, p, 0] = blank[0]
            windows[k, p, 9] = blank[0]
    for b in range(BR):
        zero[b] = tiles_ref[b]
    entries = []
    for b in range(BR):
        found = [neighbours_ref[b, 12 + k] for k in range(3)]
        entries.append([jnp.where(e > 64, e - 65, 4) for e in found])

    def body(p, carry):
        for q in range(8):
            for k, rows in enumerate(three_shifts(entries, zero, p, q)):
                windows[k, p + 1, q + 1] = rows
        return carry

    lax.fori_loop(0, 8, body, 0)


def margin_windows(index_ref, pool, ends, strips):
    blank = jnp.zeros((32, CH), BF16)
    for ox in (-1, 0, 1):
        for oy in (-1, 0, 1):
            if ox == 0 and oy == 0:
                continue
            start = 9 * (ox + 1) + 3 * (oy + 1)
            entries = [[index_ref[b, start + k] for k in range(3)] for b in range(BR)]
            for i in range(8):
                p = i if ox == 0 else (7 if ox < 0 else 0)
                q = i if oy == 0 else (7 if oy < 0 else 0)
                for k, rows in enumerate(three_shifts(entries, pool, p, q)):
                    if ox == 0:
                        strips[(oy + 1) // 2, k, p + 1] = rows
                    else:
                        ends[(ox + 1) // 2, k, q + 1 if oy == 0 else (0 if oy < 0 else 9)] = rows
                if ox != 0 and oy != 0:
                    break
    for side in range(2):
        for k in range(3):
            strips[side, k, 0] = blank
            strips[side, k, 9] = blank


def conv_sum(pairs):
    total = None
    for first in range(0, len(pairs), 2):
        group = pairs[first : first + 2]
        left = jnp.concatenate([rows for rows, _ in group], axis=1)
        right = jnp.concatenate([tap for _, tap in group], axis=0)
        term = jnp.dot(left, right, preferred_element_type=F32)
        total = term if total is None else total + term
    return total


def turned_sum(pairs):
    total = None
    for first in range(0, len(pairs), 2):
        group = pairs[first : first + 2]
        left = jnp.concatenate([rows for rows, _ in group], axis=1)
        right = jnp.concatenate([tap for _, tap in group], axis=1)
        term = lax.dot_general(left, right, (((1,), (1,)), ((), ())), preferred_element_type=F32)
        total = term if total is None else total + term
    return total


def inner_sum(windows, summed, tap_weight, sign, p):
    pairs = []
    for t in range(TAPS):
        ox, oy, oz = (sign * (v - 1) for v in (t // 9, t // 3 % 3, t % 3))
        rows = windows[oz + 1, p + ox + 1, oy + 1 : oy + 9].reshape(256, CH)
        pairs.append((rows, tap_weight(t)))
    return summed(pairs)


def margin_sums(ends, strips, summed, tap_weight, sign):
    added = []
    for side in range(2):
        along_x, along_y = [], []
        for t in range(TAPS):
            ox, oy, oz = (sign * (v - 1) for v in (t // 9, t // 3 % 3, t % 3))
            if ox == 2 * side - 1:
                along_x.append((ends[side, oz + 1, oy + 1 : oy + 9].reshape(256, CH), tap_weight(t)))
            if oy == 2 * side - 1:
                along_y.append((strips[side, oz + 1, ox + 1 : ox + 9].reshape(256, CH), tap_weight(t)))
        added.append((summed(along_x), summed(along_y)))
    return added


def picks():
    lane = lax.broadcasted_iota(jnp.int32, (CH, CH), 1)
    channel = lax.broadcasted_iota(jnp.int32, (CH, CH), 0)
    parts = [
        jnp.where((lane - OWN * k == channel) & (channel < OWN), 1.0, 0.0).astype(BF16) for k in range(3)
    ]
    return jnp.concatenate(parts, axis=0)


def narrowed(rows):
    return jnp.dot(jnp.concatenate(rows, axis=1), picks(), preferred_element_type=F32).astype(BF16)


def inner_kernel(nb_ref, tiles_ref, w0_ref, w1_ref, w2_ref, w3_ref, hidden_ref, narrow_ref, zero, windows):
    inner_windows(nb_ref, tiles_ref, zero, windows)
    weights = (w0_ref, w1_ref, w2_ref, w3_ref)

    def tap_weight(t):
        return jnp.concatenate([ref[t] for ref in weights], axis=0)

    def body(p, carry):
        hidden_ref[p] = inner_sum(windows, conv_sum, tap_weight, 1, p).reshape(8, 32, CH)
        rows = [windows[k, p + 1, 1:9].reshape(256, CH) for k in range(3)]
        narrow_ref[p] = narrowed(rows).reshape(8, 32, CH)
        return carry

    lax.fori_loop(0, 8, body, 0)


def inner(neighbours, tiles, weights):
    return pl.pallas_call(
        inner_kernel,
        out_shape=[jax.ShapeDtypeStruct((8, 8, 32, CH), F32), jax.ShapeDtypeStruct((8, 8, 32, CH), BF16)],
        in_specs=[SMEM] + [VMEM] * 5,
        out_specs=[VMEM] * 2,
        scratch_shapes=[
            pltpu.VMEM((5, 64, 8, CH), F32),
            pltpu.VMEM((3, 10, 10, 32, CH), BF16),
        ],
        compiler_params=params(),
        cost_estimate=cost(2 * 27 * CH * CH * 2048, 2**24),
    )(neighbours, tiles, *weights)


def gate_kernel(
    index_ref,
    place_ref,
    tiles_ref,
    cot_ref,
    inner_ref,
    inner_narrow_ref,
    side_m_ref,
    side_n_ref,
    left_ref,
    right_ref,
    w0_ref,
    w1_ref,
    w2_ref,
    w3_ref,
    gated_ref,
    grad_ref,
    face_m_ref,
    face_n_ref,
    low_ref,
    high_ref,
    keep_ref,
    send_ref,
    pool,
    ends,
    strips,
    hidden,
    narrow,
    grad_rows,
    sums,
):
    core = place_ref[0]
    weights = (w0_ref, w1_ref, w2_ref, w3_ref)
    fill_pool(core, pool, tiles_ref, (side_m_ref, side_n_ref, left_ref, right_ref))
    margin_windows(index_ref, pool, ends, strips)

    def tap_weight(t):
        return jnp.concatenate([ref[t] for ref in weights], axis=0)

    for p in range(8):
        hidden[p] = inner_ref[p]
        narrow[p + 1, 1:9] = inner_narrow_ref[p]
    for side, (along_x, along_y) in enumerate(margin_sums(ends, strips, conv_sum, tap_weight, 1)):
        hidden[7 * side] += along_x.reshape(8, 32, CH)
        for p in range(8):
            hidden[p, 7 * side] += along_y[32 * p : 32 * p + 32]
        rows = [ends[side, k].reshape(320, CH) for k in range(3)]
        narrow[9 * side] = narrowed(rows).reshape(10, 32, CH)
        rows = [strips[side, k, 1:9].reshape(256, CH) for k in range(3)]
        small = narrowed(rows)
        for p in range(8):
            narrow[p + 1, 9 * side] = small[32 * p : 32 * p + 32]

    def gate_body(p, carry):
        h = hidden[p].reshape(8, BR, 8, CH)
        grads = []
        for b in range(BR):
            part = h[:, b]
            cot = cot_ref[b, pl.ds(8 * p, 8)]
            sig = jax.nn.sigmoid(part)
            gated_ref[b, pl.ds(8 * p, 8)] = part * sig
            grad = (cot * sig * (1.0 + part * (1.0 - sig))).astype(BF16).astype(F32)
            grad_ref[b, pl.ds(8 * p, 8)] = grad
            grads.append(grad)
        rows = jnp.stack(grads, axis=1).reshape(256, CH)
        for k in range(2):
            grad_rows[p, :, 128 * k : 128 * k + 128] = rows[128 * k : 128 * k + 128].T.astype(BF16)
        return carry

    lax.fori_loop(0, 8, gate_body, 0)
    emit_faces(core, grad_ref, None, (face_m_ref, face_n_ref, low_ref, high_ref))

    for i in range(3):

        def sum_body(p, carry, i=i):
            left = grad_rows[p]
            right = [narrow[p + i, j : j + 8].reshape(256, CH) for j in range(3)]
            return carry + jnp.dot(left, jnp.concatenate(right, axis=1), preferred_element_type=F32)

        total = lax.fori_loop(0, 8, sum_body, jnp.zeros((CH, 3 * CH), F32))
        for j in range(3):
            start = 96 * (3 * i + j)
            sums[start : start + 96] = total[:, CH * j : CH * j + CH].T[:96]
    sums[864:896] = jnp.zeros((32, CH), F32)
    keep_ref[...] = sums[pl.ds(pl.multiple_of(448 * core, 8), 448), :]
    send_ref[...] = sums[pl.ds(pl.multiple_of(448 * (1 - core), 8), 448), :]


def gate(index, core, tiles, cot, hidden, narrow, halo, weights):
    face = jax.ShapeDtypeStruct((272, CH), BF16)
    half = jax.ShapeDtypeStruct((448, CH), F32)
    field = jax.ShapeDtypeStruct((BR, 64, 8, CH), F32)
    return pl.pallas_call(
        gate_kernel,
        out_shape=[field, field, face, face, face, face, half, half],
        in_specs=[SMEM] * 2 + [VMEM] * 12,
        out_specs=[VMEM] * 8,
        scratch_shapes=[
            pltpu.VMEM((40, 64, 8, CH), F32),
            pltpu.VMEM((2, 3, 10, 32, CH), BF16),
            pltpu.VMEM((2, 3, 10, 32, CH), BF16),
            pltpu.VMEM((8, 8, 32, CH), F32),
            pltpu.VMEM((10, 10, 32, CH), BF16),
            pltpu.VMEM((8, CH, 256), BF16),
            pltpu.VMEM((896, CH), F32),
        ],
        compiler_params=params(),
        cost_estimate=cost(2 * 27 * CH * CH * 1024, 2**24),
    )(index, core, tiles, cot, hidden, narrow, *halo, *weights)


def back_inner_kernel(nb_ref, chan_ref, tiles_ref, weight_ref, gated_ref, feat_ref, part_ref, out_ref, zero, windows, turned):
    inner_windows(nb_ref, tiles_ref, zero, windows)

    def body(p, carry):
        part_ref[p] = inner_sum(windows, turned_sum, lambda t: weight_ref[t], -1, p).reshape(8, 32, OWN)
        return carry

    lax.fori_loop(0, 8, body, 0)
    own = pl.multiple_of(chan_ref[0] * OWN, OWN)
    for b in range(BR):
        for k in range(4):
            start = VOX * b + 128 * k
            turned[:, start : start + 128] = gated_ref[b, 16 * k : 16 * k + 16].reshape(128, CH).T
    out_ref[...] = (feat_ref[...].astype(F32) + turned[pl.ds(own, OWN), :]).astype(BF16)


def back_inner(neighbours, chan, tiles, weight, gated, features):
    return pl.pallas_call(
        back_inner_kernel,
        out_shape=[
            jax.ShapeDtypeStruct((8, 8, 32, OWN), F32),
            jax.ShapeDtypeStruct((OWN, BR * VOX), BF16),
        ],
        in_specs=[SMEM] * 2 + [VMEM] * 4,
        out_specs=[VMEM] * 2,
        scratch_shapes=[
            pltpu.VMEM((5, 64, 8, CH), F32),
            pltpu.VMEM((3, 10, 10, 32, CH), BF16),
            pltpu.VMEM((CH, BR * VOX), F32),
        ],
        compiler_params=params(),
        cost_estimate=cost(2 * 27 * CH * CH * 2048, 2**24),
    )(neighbours, chan, tiles, weight, gated, features)


def back_margin_kernel(
    index_ref,
    place_ref,
    tiles_ref,
    side_m_ref,
    side_n_ref,
    left_ref,
    right_ref,
    weight_ref,
    part_ref,
    cot_ref,
    grad_ref,
    pool,
    ends,
    strips,
    result,
):
    fill_pool(place_ref[0], pool, tiles_ref, (side_m_ref, side_n_ref, left_ref, right_ref))
    margin_windows(index_ref, pool, ends, strips)
    for p in range(8):
        result[p] = part_ref[p]
    for side, (along_x, along_y) in enumerate(margin_sums(ends, strips, turned_sum, lambda t: weight_ref[t], -1)):
        result[7 * side] += along_x.reshape(8, 32, OWN)
        for p in range(8):
            result[p, 7 * side] += along_y[32 * p : 32 * p + 32]
    for b in range(BR):
        for k in range(4):
            start = VOX * b + 128 * k
            block = result[2 * k : 2 * k + 2, :, 8 * b : 8 * b + 8, :].reshape(128, OWN)
            summed = cot_ref[:, start : start + 128].astype(F32) + block.T
            grad_ref[:, start : start + 128] = summed.astype(BF16)


def back_margin(index, core, tiles, halo, weight, part, cotangent):
    return pl.pallas_call(
        back_margin_kernel,
        out_shape=jax.ShapeDtypeStruct((OWN, BR * VOX), BF16),
        in_specs=[SMEM] * 2 + [VMEM] * 8,
        out_specs=VMEM,
        scratch_shapes=[
            pltpu.VMEM((40, 64, 8, CH), F32),
            pltpu.VMEM((2, 3, 10, 32, CH), BF16),
            pltpu.VMEM((2, 3, 10, 32, CH), BF16),
            pltpu.VMEM((8, 8, 32, OWN), F32),
        ],
        compiler_params=params(),
        cost_estimate=cost(2 * 27 * CH * CH * 512, 2**23),
    )(index, core, tiles, *halo, weight, part, cotangent)


def ring_gather(value, axis):
    count = lax.axis_size(axis)
    blocks = [value]
    for step in range(1, count):
        blocks.append(lax.ppermute(value, axis, [(i, (i + step) % count) for i in range(count)]))
    return blocks


def swapped(value, axis, partner):
    return lax.ppermute(value, axis, list(enumerate(partner)))


X_NEAR, X_FAR = (1, 0, 3, 2), (3, 2, 1, 0)
Z_PAIRS = ((1, 0, 3, 2, 5, 4, 7, 6), (2, 3, 0, 1, 6, 7, 4, 5), (6, 7, 4, 5, 2, 3, 0, 1))


def halve(value, bit, partner):
    halves = value.reshape(2, value.shape[0] // 2, CH)
    keep = lax.dynamic_index_in_dim(halves, bit, 0, keepdims=False)
    send = lax.dynamic_index_in_dim(halves, 1 - bit, 0, keepdims=False)
    return keep + swapped(send, "x", partner)


def place_kernel(me_ref, one_ref, two_ref, four_ref, eight_ref, out_ref):
    for t in range(8):
        if t < 1:
            rows = one_ref[...]
        elif t < 2:
            rows = two_ref[...]
        elif t < 4:
            rows = four_ref[112 * (t - 2) : 112 * (t - 1)]
        else:
            rows = eight_ref[112 * (t - 4) : 112 * (t - 3)]
        at = me_ref[t]
        start = pl.multiple_of(112 * at, 8)

        @pl.when(at < 7)
        def _():
            out_ref[pl.ds(start, 112), :] = rows

        @pl.when(at == 7)
        def _():
            out_ref[pl.ds(start, 80), :] = rows[:80]


def after(value, *others):
    return lax.optimization_barrier((value,) + others)[0]


def reduce_space(keep, send, beside):
    x = lax.axis_index("x")
    core = lax.axis_index("core")
    high = x // 2
    low = (x ^ (x // 2)) & 1
    value = keep + swapped(send, "core", (1, 0))
    value = halve(value, high, X_FAR)
    value = halve(after(value, *beside[0]), low, X_NEAR)
    for step, partner in enumerate(Z_PAIRS):
        value = after(value, *beside[step + 1])
        value = value + swapped(value, "z", partner)
    value = after(value, *beside[4])
    two = swapped(value, "x", X_NEAR)
    pair = jnp.concatenate([value, two], axis=0)
    four = swapped(pair, "x", X_FAR)
    quad = jnp.concatenate([pair, four], axis=0)
    eight = swapped(quad, "core", (1, 0))
    me = 4 * core + 2 * high + low
    return pl.pallas_call(
        place_kernel,
        out_shape=jax.ShapeDtypeStruct((864, CH), F32),
        in_specs=[SMEM] + [VMEM] * 4,
        out_specs=VMEM,
        compiler_params=params(),
        cost_estimate=cost(0, 2**20),
    )(me ^ jnp.arange(8, dtype=jnp.int32), value, two, four, eight)


def per_device(features, weight, cotangent, neighbours, send_slots):
    core = lax.axis_index("core").astype(jnp.int32)
    chan = lax.axis_index("chan").astype(jnp.int32).reshape(1)
    core_at = core.reshape(1)
    feat_own = features.reshape(OWN, BR * VOX)
    cot_own = cotangent.reshape(OWN, BR * VOX)
    table = jnp.pad(send_slots.astype(BF16), ((0, 8), (0, CH - SLOTS)))
    feat_blocks = ring_gather(feat_own, "chan")
    weights = ring_gather(weight, "chan")

    tiles, *faces = prep(core_at, feat_blocks, table)
    halo = exchange(faces)
    cot_blocks = ring_gather(after(cot_own, *halo[:2]), "chan")
    hidden, narrow = inner(neighbours, tiles, weights)
    cot = turn(chan, cot_blocks)
    index = pool_index(neighbours, core, halo)
    gated, grads, face_m, face_n, low, high, keep, send = gate(index, core_at, tiles, cot, hidden, narrow, halo, weights)
    grad_halo = exchange((face_m, face_n, low, high))
    part, out = back_inner(neighbours, chan, grads, weight, gated, feat_own)
    grad_input = back_margin(index, core_at, grads, grad_halo, weight, part, cot_own)
    grad_weight = reduce_space(keep, send, (grad_halo[:2], (part,), grad_halo[2:], (grad_input,), ()))
    return (
        out.reshape(OWN, BR, VOX),
        grad_input.reshape(OWN, BR, VOX),
        grad_weight.reshape(TAPS, OWN, CH),
    )


def solution(mesh):
    fine = Mesh(mesh.devices.reshape(4, 8, 2, 4), ("x", "z", "core", "chan"))
    return jax.shard_map(
        per_device,
        mesh=fine,
        in_specs=(
            P("chan", SPACE, None),
            P(None, "chan", None),
            P("chan", SPACE, None),
            P(SPACE, None),
            P(SPACE, None),
        ),
        out_specs=(P("chan", SPACE, None), P("chan", SPACE, None), P(None, "chan", None)),
        check_vma=False,
    )
```

time: 1140 us -> 123 us (0.11); the launches traced: 1120 us -> 121 us
  local copies, waits for them, and re-layouts: 703 us -> 12 us
  waiting for transfers between devices: 209 us -> 14.3 us
  other arithmetic: 101 us -> 1.89 us
  Pallas kernels: 0 us -> 37.8 us
  between operations: 18.4 us -> 1.18 us
  matrix products: 15.1 us -> 0 us
    unnamed x1029 -> x87, local copies, waits for them, and re-layouts: 294 us -> 9.6 us
    psum x1 -> x0, waiting for transfers between devices: 182 us -> none  [per_device(): grad_weight = lax.psum(partial_grad, 'space')]
    slice x139 -> x0, local copies, waits for them, and re-layouts: 162 us -> none  [the longest x75 101 us: brick_margin(): cube[:, :, layer_cuts[i][0]:layer_cuts[i][1], layer_cuts[j][0]:layer_cuts...]
    concatenate x58 -> x5, local copies, waits for them, and re-layouts: 118 us -> 0.11 us  [the longest x1 0.08 us: pool_index(): values = jnp.concatenate(rows)]
    gather x68 -> x0, local copies, waits for them, and re-layouts: 80.4 us -> none  [the longest x52 67.6 us: brick_margin(): jnp.take(slab_pool, lookup[:, 9 * i + 3 * j + k], axis=1)]
    select_n x82 -> x4, other arithmetic: 42.5 us -> 0.63 us  [the longest x1 0.59 us: pool_index(): return jnp.where(neighbours == 0, ZERO, found)]
    pallas_call x0 -> x7, Pallas kernels: none -> 37.8 us  [the longest x1 11 us: gate(): pl.pallas_call(gate_kernel, out_shape=[field, field, face, face, face, fa...]
    ppermute x16 -> x0, local copies, waits for them, and re-layouts: 30 us -> none  [shifted(): lax.ppermute(value, axis, [(source, source + steps) for source in range(f...]
  transfers between devices with their start and end apart: 20 -> 26, of which waited for: 5 -> 7; matrix products, arithmetic and copies ran while one was open for 15% -> 6% of each run, Pallas kernels for 0% -> 18%
where the time goes in v2:
time: 123 us; the launch traced here: 121 us
  starting transfers between devices  54.1 us (44%)
  Pallas kernels  37.8 us (31%)
  waiting for transfers between devices  14.3 us (12%)
  local copies, waits for them, and re-layouts  12 us (10%)
  other arithmetic  1.89 us (2%)
    ppermute x9, starting transfers between devices, swapped(): return lax.ppermute(value, axis, list(enumerate(partner)))  22.4 us
    ppermute x9, starting transfers between devices, ring_gather(): lax.ppermute(value, axis, [(i, (i + step) % count) for i in range(count)])  12 us
    ppermute x9, waiting for transfers between devices, swapped(): return lax.ppermute(value, axis, list(enumerate(partner)))  11.2 us
    pallas_call x1, Pallas kernels, gate(): pl.pallas_call(gate_kernel, out_shape=[field, field, face, face, face, fa...  11 us
    unnamed x87, local copies, waits for them, and re-layouts  9.6 us
    ppermute x4, starting transfers between devices, shifted(): lax.ppermute(value, SPACE, [(i, i + steps) for i in range(first, last)])  9.37 us
    pallas_call x1, Pallas kernels, inner(): pl.pallas_call(inner_kernel, out_shape=[jax.ShapeDtypeStruct((8, 8, 32, C...  8.43 us
    pallas_call x1, Pallas kernels, back_inner(): pl.pallas_call(back_inner_kernel, out_shape=[jax.ShapeDtypeStruct((8, 8,...  7.9 us
  transfers between devices with their start and end apart: 26, of which 7 were waited for; matrix products, arithmetic and copies ran while one was open for 6% of the time, Pallas kernels for 18%

profile of v2, /device:TPU:1, one launch (start us, length us, event | category | flops | bytes accessed | tf_op | source)
XLA Modules:
  0.0 121.3 jit_solution(13411208487909439046)
XLA Ops:
  1.6 2.2 %collective-permute-start = (bf16[32,2048]{1,0:T(8,128)(2,1)S(1)}, bf16[32,2048]{1,0:T(8,128)(2,1)S(1)}, u32[]{:S(2)}, u32[]{:S(2)}) collective-permute-start(bf16[32,2048]{1,0:T(8,128)(2,1)S(1)} %bitcast.40), channel_id=1, source_target_pairs={{0,1},{1,2},{2,3},{3,0},{4,5},{5,6},{6,7},{7,4},{8,9},{9,10},{10,1... | collective-permute-start | bytes 393224 | tf_op jit(solution)/shard_map/ppermute | solution.py:521
  3.8 2.6 %collective-permute-start.1 = (bf16[32,2048]{1,0:T(8,128)(2,1)S(1)}, bf16[32,2048]{1,0:T(8,128)(2,1)S(1)}, u32[]{:S(2)}, u32[]{:S(2)}) collective-permute-start(bf16[32,2048]{1,0:T(8,128)(2,1)S(1)} %bitcast.41), channel_id=1, source_target_pairs={{0,2},{1,3},{2,0},{3,1},{4,6},{5,7},{6,4},{7,5},{8,10},{9,11},{10,... | collective-permute-start | bytes 393224 | tf_op jit(solution)/shard_map/ppermute | solution.py:521
  14.1 2.4 %shard_map.76 = (f32[4,64,8,128]{3,2,1,0:T(8,128)}, bf16[272,128]{1,0:T(8,128)(2,1)}, bf16[272,128]{1,0:T(8,128)(2,1)}, bf16[272,128]{1,0:T(8,128)(2,1)}, bf16[272,128]{1,0:T(8,128)(2,1)}) custom-call(s32[1]{0:T(128)} %bitcast.1.core_ref.place_ref, bf16[32,2048]{1,0:T(8,128)(2,1)} %bitcast.43, bf16[32,2048]{1,0:T(8,128)(2,1)} %copy-done.13, ...), custom_call_target="tpu_custom_call" | custom-call | bytes 4194304 | tf_op jit(solution)/shard_map/pallas_call | solution.py:65
  16.5 3.4 %collective-permute-start.3 = (bf16[272,128]{1,0:T(8,128)(2,1)}, bf16[272,128]{1,0:T(8,128)(2,1)S(1)}, u32[]{:S(2)}, u32[]{:S(2)}) collective-permute-start(bf16[272,128]{1,0:T(8,128)(2,1)} %get-tuple-element.26), channel_id=1, source_target_pairs={{0,4},{4,0},{1,5},{5,1},{2,6},{6,2},{3,7},{7,3},{8,12},{12,8},{9,1... | collective-permute-start | bytes 208904 | tf_op jit(solution)/shard_map/ppermute | solution.py:107
  19.9 2.1 %collective-permute-start.4 = (bf16[272,128]{1,0:T(8,128)(2,1)}, bf16[272,128]{1,0:T(8,128)(2,1)S(1)}, u32[]{:S(2)}, u32[]{:S(2)}) collective-permute-start(bf16[272,128]{1,0:T(8,128)(2,1)} %get-tuple-element.27), channel_id=1, source_target_pairs={{4,8},{20,24},{36,40},{52,56},{68,72},{84,88},{100,104},{116,120},... | collective-permute-start | bytes 208904 | tf_op jit(solution)/shard_map/ppermute | solution.py:106
  22.9 3.1 %collective-permute-done.4.side_n_ref = bf16[272,128]{1,0:T(8,128)(2,1)S(1)} collective-permute-done((bf16[272,128]{1,0:T(8,128)(2,1)}, bf16[272,128]{1,0:T(8,128)(2,1)S(1)}, u32[]{:S(2)}, u32[]{:S(2)}) %collective-permute-start.4) | collective-permute-done | bytes 69664 | tf_op jit(solution)/shard_map/ppermute | solution.py:106
  30.8 5.5 %collective-permute-start.5 = (bf16[368,128]{1,0:T(8,128)(2,1)S(1)}, bf16[368,128]{1,0:T(8,128)(2,1)S(1)}, u32[]{:S(2)}, u32[]{:S(2)}) collective-permute-start(bf16[368,128]{1,0:T(8,128)(2,1)S(1)} %constant_dynamic-update-slice_fusion), channel_id=1, source_target_pairs={{0,16},{4,20},{8,24},{12,28},{16,32},{20,36},{24,40},{28,44},{32,4... | collective-permute-start | bytes 282632 | tf_op jit(solution)/shard_map/ppermute | solution.py:37
  36.4 8.4 %shard_map.78 = (f32[8,8,32,128]{3,2,1,0:T(8,128)}, bf16[8,8,32,128]{3,2,1,0:T(8,128)(2,1)}) custom-call(s32[4,27]{1,0:T(4,128)} %nb_ref.3, f32[4,64,8,128]{3,2,1,0:T(8,128)} %get-tuple-element.29.tiles_ref, bf16[27,32,128]{2,1,0:T(8,128)(2,1)} %weight_ref.3, bf16[27,32,128]{2,1,0:T(8,128)(2,1)} %copy-done.9, bf16[27,32,128]{2,1,0:T(8,128)(2,1)} %copy-done.10, ...), custom_call_target="tpu_custom_call" | custom-call | flops 1811939328 | bytes 16777216 | tf_op jit(solution)/shard_map/pallas_call | solution.py:307
  47.6 2.5 %shard_map.77.cot_ref = f32[4,64,8,128]{3,2,1,0:T(8,128)} custom-call(s32[1]{0:T(128)} %bitcast.chan_ref, bf16[32,2048]{1,0:T(8,128)(2,1)} %bitcast.36, bf16[32,2048]{1,0:T(8,128)(2,1)} %copy-done.12, bf16[32,2048]{1,0:T(8,128)(2,1)} %copy-done.14, bf16[32,2048]{1,0:T(8,128)(2,1)} %copy-done.17), custom_call_target="tpu_custom_call" | custom-call | bytes 4194304 | tf_op jit(solution)/shard_map/pallas_call | solution.py:86
  50.1 11.0 %shard_map.79 = (f32[4,64,8,128]{3,2,1,0:T(8,128)}, f32[4,64,8,128]{3,2,1,0:T(8,128)}, bf16[272,128]{1,0:T(8,128)(2,1)}, bf16[272,128]{1,0:T(8,128)(2,1)}, bf16[...) custom-call(s32[4,27]{1,0:T(4,128)} %select_select_fusion.index_ref, ...), custom_call_target="tpu_custom_call" | custom-call | flops 905969664 | bytes 16777216 | tf_op jit(solution)/shard_map/pallas_call | solution.py:413
  61.6 4.2 %collective-permute-start.14 = (bf16[272,128]{1,0:T(8,128)(2,1)}, bf16[272,128]{1,0:T(8,128)(2,1)S(1)}, u32[]{:S(2)}, u32[]{:S(2)}) collective-permute-start(bf16[272,128]{1,0:T(8,128)(2,1)} %get-tuple-element.37), channel_id=1, source_target_pairs={{4,8},{20,24},{36,40},{52,56},{68,72},{84,88},{100,104},{116,120},... | collective-permute-start | bytes 208904 | tf_op jit(solution)/shard_map/ppermute | solution.py:106
  66.7 7.9 %shard_map.80 = (f32[8,8,32,32]{3,2,1,0:T(8,128)}, bf16[32,2048]{1,0:T(8,128)(2,1)}) custom-call(s32[4,27]{1,0:T(4,128)} %nb_ref.3, s32[1]{0:T(128)} %bitcast.chan_ref, f32[4,64,8,128]{3,2,1,0:T(8,128)} %get-tuple-element.33.tiles_ref, bf16[27,32,128]{2,1,0:T(8,128)(2,1)} %weight_ref.3, f32[4,64,8,128]{3,2,1,0:T(8,128)} %get-tuple-element.34.gated_ref, ...), custom_call_target="tpu_custom_call" | custom-call | flops 1811939328 | bytes 16777216 | tf_op jit(solution)/shard_map/pallas_call | solution.py:449
  75.7 5.0 %collective-permute-start.18 = (f32[224,128]{1,0:T(8,128)S(1)}, f32[224,128]{1,0:T(8,128)S(1)}, u32[]{:S(2)}, u32[]{:S(2)}) collective-permute-start(f32[224,128]{1,0:T(8,128)S(1)} %dynamic-slice_bitcast_fusion), channel_id=1, source_target_pairs={{0,192},{64,128},{128,64},{192,0},{1,193},{65,129},{129,65},{193,1... | collective-permute-start | bytes 344072 | tf_op jit(solution)/shard_map/ppermute | solution.py:526
  82.8 3.0 %collective-permute-start.19 = (f32[112,128]{1,0:T(8,128)S(1)}, f32[112,128]{1,0:T(8,128)S(1)}, u32[]{:S(2)}, u32[]{:S(2)}) collective-permute-start(f32[112,128]{1,0:T(8,128)S(1)} %dynamic-slice_bitcast_fusion.1), channel_id=1, source_target_pairs={{0,64},{64,0},{128,192},{192,128},{1,65},{65,1},{129,193},{193,129... | collective-permute-start | bytes 172040 | tf_op jit(solution)/shard_map/ppermute | solution.py:526
  87.6 3.9 %collective-permute-done.20 = f32[112,128]{1,0:T(8,128)S(1)} collective-permute-done((f32[112,128]{1,0:T(8,128)S(1)}, f32[112,128]{1,0:T(8,128)S(1)}, u32[]{:S(2)}, u32[]{:S(2)}) %collective-permute-start.20) | collective-permute-done | bytes 57376 | tf_op jit(solution)/shard_map/ppermute | solution.py:526
  91.5 2.0 %collective-permute-start.21 = (f32[112,128]{1,0:T(8,128)S(1)}, f32[112,128]{1,0:T(8,128)S(1)}, u32[]{:S(2)}, u32[]{:S(2)}) collective-permute-start(f32[112,128]{1,0:T(8,128)S(1)} %add.132), channel_id=1, source_target_pairs={{0,16},{8,24},{16,0},{24,8},{32,48},{40,56},{48,32},{56,40},{1,17}... | collective-permute-start | bytes 172040 | tf_op jit(solution)/shard_map/ppermute | solution.py:526
  93.6 3.7 %shard_map.81 = bf16[32,2048]{1,0:T(8,128)(2,1)} custom-call(s32[4,27]{1,0:T(4,128)} %select_select_fusion.index_ref, s32[1]{0:T(128)} %bitcast.1.core_ref.place_ref, f32[4,64,8,128]{3,2,1,0:T(8,128)} %get-tuple-element.33.tiles_ref, bf16[272,128]{1,0:T(8,128)(2,1)} %copy-done.21, bf16[272,128]{1,0:T(8,128)(2,1)} %copy-done.22, bf16[368,128]{1,0:T(8,128)(2,1)} %copy-done.26, ...), custom_call_target="tpu_custom_call" | custom-call | flops 452984832 | bytes 8388608 | tf_op jit(solution)/shard_map/pallas_call | solution.py:501
  97.3 2.8 %collective-permute-start.22 = (f32[112,128]{1,0:T(8,128)S(1)}, f32[112,128]{1,0:T(8,128)S(1)}, u32[]{:S(2)}, u32[]{:S(2)}) collective-permute-start(f32[112,128]{1,0:T(8,128)S(1)} %add.133), channel_id=1, source_target_pairs={{0,48},{8,56},{16,32},{24,40},{32,16},{40,24},{48,0},{56,8},{1,49}... | collective-permute-start | bytes 172040 | tf_op jit(solution)/shard_map/ppermute | solution.py:526
  100.1 2.4 %collective-permute-done.22 = f32[112,128]{1,0:T(8,128)S(1)} collective-permute-done((f32[112,128]{1,0:T(8,128)S(1)}, f32[112,128]{1,0:T(8,128)S(1)}, u32[]{:S(2)}, u32[]{:S(2)}) %collective-permute-start.22) | collective-permute-done | bytes 57376 | tf_op jit(solution)/shard_map/ppermute | solution.py:526
  102.6 2.5 %collective-permute-start.23 = (f32[112,128]{1,0:T(8,128)S(1)}, f32[112,128]{1,0:T(8,128)S(1)}, u32[]{:S(2)}, u32[]{:S(2)}) collective-permute-start(f32[112,128]{1,0:T(8,128)S(1)} %add.134.one_ref), channel_id=1, source_target_pairs={{0,64},{64,0},{128,192},{192,128},{1,65},{65,1},{129,193},{193,129... | collective-permute-start | bytes 172040 | tf_op jit(solution)/shard_map/ppermute | solution.py:526
  106.6 4.6 %collective-permute-start.24 = (f32[224,128]{1,0:T(8,128)S(1)}, f32[224,128]{1,0:T(8,128)S(1)}, u32[]{:S(2)}, u32[]{:S(2)}) collective-permute-start(f32[224,128]{1,0:T(8,128)S(1)} %pad_maximum_fusion.1), channel_id=1, source_target_pairs={{0,192},{64,128},{128,64},{192,0},{1,193},{65,129},{129,65},{193,1... | collective-permute-start | bytes 344072 | tf_op jit(solution)/shard_map/ppermute | solution.py:526
  111.2 2.2 %collective-permute-done.24.four_ref = f32[224,128]{1,0:T(8,128)S(1)} collective-permute-done((f32[224,128]{1,0:T(8,128)S(1)}, f32[224,128]{1,0:T(8,128)S(1)}, u32[]{:S(2)}, u32[]{:S(2)}) %collective-permute-start.24) | collective-permute-done | bytes 114720 | tf_op jit(solution)/shard_map/ppermute | solution.py:526
  114.0 2.4 %collective-permute-start.25 = (f32[448,128]{1,0:T(8,128)S(1)}, f32[448,128]{1,0:T(8,128)S(1)}, u32[]{:S(2)}, u32[]{:S(2)}) collective-permute-start(f32[448,128]{1,0:T(8,128)S(1)} %pad_maximum_fusion), channel_id=1, source_target_pairs={{0,4},{4,0},{1,5},{5,1},{2,6},{6,2},{3,7},{7,3},{8,12},{12,8},{9,1... | collective-permute-start | bytes 688136 | tf_op jit(solution)/shard_map/ppermute | solution.py:526
  119.3 1.9 %shard_map.82 = f32[864,128]{1,0:T(8,128)} custom-call(s32[8]{0:T(128)} %iota_xor_fusion.me_ref, f32[112,128]{1,0:T(8,128)} %copy-done.1, f32[112,128]{1,0:T(8,128)} %copy-done.5, f32[224,128]{1,0:T(8,128)} %copy-done.6, f32[448,128]{1,0:T(8,128)} %copy-done.7), custom_call_target="tpu_custom_call" | custom-call | bytes 1048576 | tf_op jit(solution)/shard_map/pallas_call | solution.py:584
  (150 shorter events, 28.3 us)
Async XLA Ops:
  1.6 10.1 %collective-permute-start = (bf16[32,2048]{1,0:T(8,128)(2,1)S(1)}, bf16[32,2048]{1,0:T(8,128)(2,1)S(1)}, u32[]{:S(2)}, u32[]{:S(2)}) collective-permute-start(bf16[32,2048]{1,0:T(8,128)(2,1)S(1)} %bitcast.40), channel_id=1, source_target_pairs={{0,1},{1,2},{2,3},{3,0},{4,5},{5,6},{6,7},{7,4},{8,9},{9,10},{10,1... | collective-permute-start | bytes 393224 | tf_op jit(solution)/shard_map/ppermute | solution.py:521
  3.8 9.6 %collective-permute-start.1 = (bf16[32,2048]{1,0:T(8,128)(2,1)S(1)}, bf16[32,2048]{1,0:T(8,128)(2,1)S(1)}, u32[]{:S(2)}, u32[]{:S(2)}) collective-permute-start(bf16[32,2048]{1,0:T(8,128)(2,1)S(1)} %bitcast.41), channel_id=1, source_target_pairs={{0,2},{1,3},{2,0},{3,1},{4,6},{5,7},{6,4},{7,5},{8,10},{9,11},{10,... | collective-permute-start | bytes 393224 | tf_op jit(solution)/shard_map/ppermute | solution.py:521
  6.5 6.9 %collective-permute-start.2 = (bf16[32,2048]{1,0:T(8,128)(2,1)S(1)}, bf16[32,2048]{1,0:T(8,128)(2,1)S(1)}, u32[]{:S(2)}, u32[]{:S(2)}) collective-permute-start(bf16[32,2048]{1,0:T(8,128)(2,1)S(1)} %bitcast.42), channel_id=1, source_target_pairs={{0,3},{1,0},{2,1},{3,2},{4,7},{5,4},{6,5},{7,6},{8,11},{9,8},{10,9... | collective-permute-start | bytes 393224 | tf_op jit(solution)/shard_map/ppermute | solution.py:521
  7.5 20.2 %collective-permute-start.10 = (bf16[27,32,128]{2,1,0:T(8,128)(2,1)S(1)}, bf16[27,32,128]{2,1,0:T(8,128)(2,1)S(1)}, u32[]{:S(2)}, u32[]{:S(2)}) collective-permute-start(bf16[27,32,128]{2,1,0:T(8,128)(2,1)S(1)} %copy-done.2), channel_id=1, source_target_pairs={{0,1},{1,2},{2,3},{3,0},{4,5},{5,6},{6,7},{7,4},{8,9},{9,10},{10,1... | collective-permute-start | bytes 663560 | tf_op jit(solution)/shard_map/ppermute | solution.py:521
  7.9 21.6 %collective-permute-start.11 = (bf16[27,32,128]{2,1,0:T(8,128)(2,1)S(1)}, bf16[27,32,128]{2,1,0:T(8,128)(2,1)S(1)}, u32[]{:S(2)}, u32[]{:S(2)}) collective-permute-start(bf16[27,32,128]{2,1,0:T(8,128)(2,1)S(1)} %copy-done.2), channel_id=1, source_target_pairs={{0,2},{1,3},{2,0},{3,1},{4,6},{5,7},{6,4},{7,5},{8,10},{9,11},{10,... | collective-permute-start | bytes 663560 | tf_op jit(solution)/shard_map/ppermute | solution.py:521
  11.8 19.1 %collective-permute-start.12 = (bf16[27,32,128]{2,1,0:T(8,128)(2,1)S(1)}, bf16[27,32,128]{2,1,0:T(8,128)(2,1)S(1)}, u32[]{:S(2)}, u32[]{:S(2)}) collective-permute-start(bf16[27,32,128]{2,1,0:T(8,128)(2,1)S(1)} %copy-done.2), channel_id=1, source_target_pairs={{0,3},{1,0},{2,1},{3,2},{4,7},{5,4},{6,5},{7,6},{8,11},{9,8},{10,9... | collective-permute-start | bytes 663560 | tf_op jit(solution)/shard_map/ppermute | solution.py:521
  16.5 6.4 %collective-permute-start.3 = (bf16[272,128]{1,0:T(8,128)(2,1)}, bf16[272,128]{1,0:T(8,128)(2,1)S(1)}, u32[]{:S(2)}, u32[]{:S(2)}) collective-permute-start(bf16[272,128]{1,0:T(8,128)(2,1)} %get-tuple-element.26), channel_id=1, source_target_pairs={{0,4},{4,0},{1,5},{5,1},{2,6},{6,2},{3,7},{7,3},{8,12},{12,8},{9,1... | collective-permute-start | bytes 208904 | tf_op jit(solution)/shard_map/ppermute | solution.py:107
  19.9 6.1 %collective-permute-start.4 = (bf16[272,128]{1,0:T(8,128)(2,1)}, bf16[272,128]{1,0:T(8,128)(2,1)S(1)}, u32[]{:S(2)}, u32[]{:S(2)}) collective-permute-start(bf16[272,128]{1,0:T(8,128)(2,1)} %get-tuple-element.27), channel_id=1, source_target_pairs={{4,8},{20,24},{36,40},{52,56},{68,72},{84,88},{100,104},{116,120},... | collective-permute-start | bytes 208904 | tf_op jit(solution)/shard_map/ppermute | solution.py:106
  26.0 20.9 %collective-permute-start.7 = (bf16[32,2048]{1,0:T(8,128)(2,1)S(1)}, bf16[32,2048]{1,0:T(8,128)(2,1)S(1)}, u32[]{:S(2)}, u32[]{:S(2)}) collective-permute-start(bf16[32,2048]{1,0:T(8,128)(2,1)S(1)} %bitcast.33), channel_id=1, source_target_pairs={{0,1},{1,2},{2,3},{3,0},{4,5},{5,6},{6,7},{7,4},{8,9},{9,10},{10,1... | collective-permute-start | bytes 393224 | tf_op jit(solution)/shard_map/ppermute | solution.py:521
  26.0 20.9 %collective-permute-start.8 = (bf16[32,2048]{1,0:T(8,128)(2,1)S(1)}, bf16[32,2048]{1,0:T(8,128)(2,1)S(1)}, u32[]{:S(2)}, u32[]{:S(2)}) collective-permute-start(bf16[32,2048]{1,0:T(8,128)(2,1)S(1)} %bitcast.34), channel_id=1, source_target_pairs={{0,2},{1,3},{2,0},{3,1},{4,6},{5,7},{6,4},{7,5},{8,10},{9,11},{10,... | collective-permute-start | bytes 393224 | tf_op jit(solution)/shard_map/ppermute | solution.py:521
  27.8 19.2 %collective-permute-start.9 = (bf16[32,2048]{1,0:T(8,128)(2,1)S(1)}, bf16[32,2048]{1,0:T(8,128)(2,1)S(1)}, u32[]{:S(2)}, u32[]{:S(2)}) collective-permute-start(bf16[32,2048]{1,0:T(8,128)(2,1)S(1)} %bitcast.35), channel_id=1, source_target_pairs={{0,3},{1,0},{2,1},{3,2},{4,7},{5,4},{6,5},{7,6},{8,11},{9,8},{10,9... | collective-permute-start | bytes 393224 | tf_op jit(solution)/shard_map/ppermute | solution.py:521
  29.5 15.3 %collective-permute-start.6 = (bf16[368,128]{1,0:T(8,128)(2,1)S(1)}, bf16[368,128]{1,0:T(8,128)(2,1)S(1)}, u32[]{:S(2)}, u32[]{:S(2)}) collective-permute-start(bf16[368,128]{1,0:T(8,128)(2,1)S(1)} %constant_dynamic-update-slice_fusion.9), channel_id=1, source_target_pairs={{16,0},{20,4},{24,8},{28,12},{32,16},{36,20},{40,24},{44,28},{48,3... | collective-permute-start | bytes 282632 | tf_op jit(solution)/shard_map/ppermute | solution.py:37
  30.8 14.0 %collective-permute-start.5 = (bf16[368,128]{1,0:T(8,128)(2,1)S(1)}, bf16[368,128]{1,0:T(8,128)(2,1)S(1)}, u32[]{:S(2)}, u32[]{:S(2)}) collective-permute-start(bf16[368,128]{1,0:T(8,128)(2,1)S(1)} %constant_dynamic-update-slice_fusion), channel_id=1, source_target_pairs={{0,16},{4,20},{8,24},{12,28},{16,32},{20,36},{24,40},{28,44},{32,4... | collective-permute-start | bytes 282632 | tf_op jit(solution)/shard_map/ppermute | solution.py:37
  61.1 13.8 %collective-permute-start.17 = (f32[448,128]{1,0:T(8,128)}, f32[448,128]{1,0:T(8,128)S(1)}, u32[]{:S(2)}, u32[]{:S(2)}) collective-permute-start(f32[448,128]{1,0:T(8,128)} %get-tuple-element.42), channel_id=1, source_target_pairs={{0,4},{4,0},{1,5},{5,1},{2,6},{6,2},{3,7},{7,3},{8,12},{12,8},{9,1... | collective-permute-start | bytes 688136 | tf_op jit(solution)/shard_map/ppermute | solution.py:526
  61.1 13.6 %collective-permute-start.13 = (bf16[272,128]{1,0:T(8,128)(2,1)}, bf16[272,128]{1,0:T(8,128)(2,1)S(1)}, u32[]{:S(2)}, u32[]{:S(2)}) collective-permute-start(bf16[272,128]{1,0:T(8,128)(2,1)} %get-tuple-element.36), channel_id=1, source_target_pairs={{0,4},{4,0},{1,5},{5,1},{2,6},{6,2},{3,7},{7,3},{8,12},{12,8},{9,1... | collective-permute-start | bytes 208904 | tf_op jit(solution)/shard_map/ppermute | solution.py:107
  61.6 13.2 %collective-permute-start.14 = (bf16[272,128]{1,0:T(8,128)(2,1)}, bf16[272,128]{1,0:T(8,128)(2,1)S(1)}, u32[]{:S(2)}, u32[]{:S(2)}) collective-permute-start(bf16[272,128]{1,0:T(8,128)(2,1)} %get-tuple-element.37), channel_id=1, source_target_pairs={{4,8},{20,24},{36,40},{52,56},{68,72},{84,88},{100,104},{116,120},... | collective-permute-start | bytes 208904 | tf_op jit(solution)/shard_map/ppermute | solution.py:106
  75.7 7.1 %collective-permute-start.18 = (f32[224,128]{1,0:T(8,128)S(1)}, f32[224,128]{1,0:T(8,128)S(1)}, u32[]{:S(2)}, u32[]{:S(2)}) collective-permute-start(f32[224,128]{1,0:T(8,128)S(1)} %dynamic-slice_bitcast_fusion), channel_id=1, source_target_pairs={{0,192},{64,128},{128,64},{192,0},{1,193},{65,129},{129,65},{193,1... | collective-permute-start | bytes 344072 | tf_op jit(solution)/shard_map/ppermute | solution.py:526
  80.6 10.9 %collective-permute-start.16 = (bf16[368,128]{1,0:T(8,128)(2,1)S(1)}, bf16[368,128]{1,0:T(8,128)(2,1)S(1)}, u32[]{:S(2)}, u32[]{:S(2)}) collective-permute-start(bf16[368,128]{1,0:T(8,128)(2,1)S(1)} %constant_dynamic-update-slice_fusion.29), channel_id=1, source_target_pairs={{16,0},{20,4},{24,8},{28,12},{32,16},{36,20},{40,24},{44,28},{48,3... | collective-permute-start | bytes 282632 | tf_op jit(solution)/shard_map/ppermute | solution.py:37
  82.8 4.6 %collective-permute-start.19 = (f32[112,128]{1,0:T(8,128)S(1)}, f32[112,128]{1,0:T(8,128)S(1)}, u32[]{:S(2)}, u32[]{:S(2)}) collective-permute-start(f32[112,128]{1,0:T(8,128)S(1)} %dynamic-slice_bitcast_fusion.1), channel_id=1, source_target_pairs={{0,64},{64,0},{128,192},{192,128},{1,65},{65,1},{129,193},{193,129... | collective-permute-start | bytes 172040 | tf_op jit(solution)/shard_map/ppermute | solution.py:526
  85.9 5.6 %collective-permute-start.15 = (bf16[368,128]{1,0:T(8,128)(2,1)S(1)}, bf16[368,128]{1,0:T(8,128)(2,1)S(1)}, u32[]{:S(2)}, u32[]{:S(2)}) collective-permute-start(bf16[368,128]{1,0:T(8,128)(2,1)S(1)} %constant_dynamic-update-slice_fusion.20), channel_id=1, source_target_pairs={{0,16},{4,20},{8,24},{12,28},{16,32},{20,36},{24,40},{28,44},{32,4... | collective-permute-start | bytes 282632 | tf_op jit(solution)/shard_map/ppermute | solution.py:37
  91.5 5.8 %collective-permute-start.21 = (f32[112,128]{1,0:T(8,128)S(1)}, f32[112,128]{1,0:T(8,128)S(1)}, u32[]{:S(2)}, u32[]{:S(2)}) collective-permute-start(f32[112,128]{1,0:T(8,128)S(1)} %add.132), channel_id=1, source_target_pairs={{0,16},{8,24},{16,0},{24,8},{32,48},{40,56},{48,32},{56,40},{1,17}... | collective-permute-start | bytes 172040 | tf_op jit(solution)/shard_map/ppermute | solution.py:526
  97.3 5.2 %collective-permute-start.22 = (f32[112,128]{1,0:T(8,128)S(1)}, f32[112,128]{1,0:T(8,128)S(1)}, u32[]{:S(2)}, u32[]{:S(2)}) collective-permute-start(f32[112,128]{1,0:T(8,128)S(1)} %add.133), channel_id=1, source_target_pairs={{0,48},{8,56},{16,32},{24,40},{32,16},{40,24},{48,0},{56,8},{1,49}... | collective-permute-start | bytes 172040 | tf_op jit(solution)/shard_map/ppermute | solution.py:526
  106.6 6.7 %collective-permute-start.24 = (f32[224,128]{1,0:T(8,128)S(1)}, f32[224,128]{1,0:T(8,128)S(1)}, u32[]{:S(2)}, u32[]{:S(2)}) collective-permute-start(f32[224,128]{1,0:T(8,128)S(1)} %pad_maximum_fusion.1), channel_id=1, source_target_pairs={{0,192},{64,128},{128,64},{192,0},{1,193},{65,129},{129,65},{193,1... | collective-permute-start | bytes 344072 | tf_op jit(solution)/shard_map/ppermute | solution.py:526
  114.0 4.6 %collective-permute-start.25 = (f32[448,128]{1,0:T(8,128)S(1)}, f32[448,128]{1,0:T(8,128)S(1)}, u32[]{:S(2)}, u32[]{:S(2)}) collective-permute-start(f32[448,128]{1,0:T(8,128)S(1)} %pad_maximum_fusion), channel_id=1, source_target_pairs={{0,4},{4,0},{1,5},{5,1},{2,6},{6,2},{3,7},{7,3},{8,12},{12,8},{9,1... | collective-permute-start | bytes 688136 | tf_op jit(solution)/shard_map/ppermute | solution.py:526
  (33 other events, 175.8 us)

commit v3 on v2

--- a/solution.py
+++ b/solution.py
@@ -17,14 +17,13 @@
 SPACE = ("x", "z", "core")
 VMEM = pl.BlockSpec(memory_space=pltpu.VMEM)
 SMEM = pl.BlockSpec(memory_space=pltpu.SMEM)
-LIMIT = 56 * 2**20
 
 compass = ((-1, -1), (-1, 0), (-1, 1), (0, -1), (0, 1), (1, -1), (1, 0), (1, 1))
 SIDE_M, SIDE_N, SIDE_L, SIDE_R, SIDE_LM, SIDE_LN, SIDE_RM, SIDE_RN, ZERO = range(4, 40, 4)
 
 
-def params():
-    return pltpu.CompilerParams(vmem_limit_bytes=LIMIT)
+def params(mib):
+    return pltpu.CompilerParams(vmem_limit_bytes=mib * 2**20)
 
 
 def cost(flops, moved):
@@ -53,8 +52,8 @@
 def prep_kernel(core_ref, own_ref, ring1_ref, ring2_ref, ring3_ref, table_ref, tiles_ref, *face_refs):
     for b in range(BR):
         for k in range(4):
-            start = VOX * b + 128 * k
-            parts = [ref[:, start : start + 128] for ref in (own_ref, ring1_ref, ring2_ref, ring3_ref)]
+            start = OWN * (4 * b + k)
+            parts = [ref[start : start + OWN] for ref in (own_ref, ring1_ref, ring2_ref, ring3_ref)]
             turned = jnp.concatenate(parts, axis=0).astype(F32).T
             tiles_ref[b, 16 * k : 16 * k + 16] = turned.reshape(16, 8, CH)
     emit_faces(core_ref[0], tiles_ref, table_ref, face_refs)
@@ -67,31 +66,39 @@
         out_shape=[jax.ShapeDtypeStruct((BR, 64, 8, CH), F32)] + [face] * 4,
         in_specs=[SMEM] + [VMEM] * 5,
         out_specs=[VMEM] * 5,
-        compiler_params=params(),
+        compiler_params=params(6),
         cost_estimate=cost(0, 2**22),
     )(core, *blocks, table)
 
 
-def turn_kernel(chan_ref, own_ref, ring1_ref, ring2_ref, ring3_ref, tiles_ref, whole):
-    for step, ref in enumerate((own_ref, ring1_ref, ring2_ref, ring3_ref)):
-        block = lax.rem(chan_ref[0] + 4 - step, 4)
-        whole[pl.ds(pl.multiple_of(block * OWN, OWN), OWN), :] = ref[...].astype(F32)
+def turn_kernel(weight_ref, turned_ref):
+    blank = jnp.zeros((OWN, CH), BF16)
+    for t in range(9):
+        block = jnp.concatenate([weight_ref[9 * i + t] for i in range(3)] + [blank], axis=0)
+        turned_ref[CH * t : CH * t + CH] = block.astype(F32).T.astype(BF16)
+
+
+def turn_weight(weight):
+    return pl.pallas_call(
+        turn_kernel,
+        out_shape=jax.ShapeDtypeStruct((9 * CH, CH), BF16),
+        in_specs=[VMEM],
+        out_specs=VMEM,
+        compiler_params=params(4),
+        cost_estimate=cost(0, 2**20),
+    )(weight)
+
+
+def turn_field(chan, blocks, start, whole, tiles_ref):
+    for step, ref in enumerate(blocks):
+        block = lax.rem(chan + 4 - step, 4)
+        for k in range(16):
+            rows = ref[start + OWN * k : start + OWN * k + OWN]
+            whole[pl.ds(pl.multiple_of(block * OWN, OWN), OWN), CH * k : CH * k + CH] = rows.astype(F32)
     for b in range(BR):
         for k in range(4):
-            start = VOX * b + 128 * k
-            tiles_ref[b, 16 * k : 16 * k + 16] = whole[:, start : start + 128].T.reshape(16, 8, CH)
-
-
-def turn(chan, blocks):
-    return pl.pallas_call(
-        turn_kernel,
-        out_shape=jax.ShapeDtypeStruct((BR, 64, 8, CH), F32),
-        in_specs=[SMEM] + [VMEM] * 4,
-        out_specs=VMEM,
-        scratch_shapes=[pltpu.VMEM((CH, BR * VOX), F32)],
-        compiler_params=params(),
-        cost_estimate=cost(0, 2**22),
-    )(chan, *blocks)
+            at = VOX * b + CH * k
+            tiles_ref[b, 16 * k : 16 * k + 16] = whole[:, at : at + CH].T.reshape(16, 8, CH)
 
 
 def column(plane, p):
@@ -110,7 +117,7 @@
     return side_m, side_n, shifted(up, ROWS), shifted(down, -ROWS)
 
 
-def pool_index(neighbours, core, halo):
+def pool_index(entry, core, halo):
     side_m, side_n, left, right = halo
     tables = {
         SIDE_M: side_m[256:272],
@@ -122,24 +129,22 @@
         SIDE_RM: right[304:320],
         SIDE_RN: right[352:368],
     }
+    tables = {side: table.astype(F32).astype(jnp.int32) for side, table in tables.items()}
     ends = {-1: (SIDE_LM, SIDE_LN), 0: (SIDE_M, SIDE_N), 1: (SIDE_RM, SIDE_RN)}
 
     def row(side, d):
-        return tables[side][7 - d, :SLOTS].astype(jnp.int32) + side
-
-    rows = []
+        return tables[side][7 - d : 8 - d] + side
+
+    found = jnp.where(entry == 0, ZERO, entry - 65)
     for d, (ex, ey) in enumerate(compass):
         if ey == 0:
-            rows.append(row(SIDE_L if ex < 0 else SIDE_R, d))
+            values = row(SIDE_L if ex < 0 else SIDE_R, d)
         else:
             near, far = ends[ex] if ey > 0 else ends[ex][::-1]
-            rows.append(jnp.where(core == 0, row(near, d), row(far, d)))
-    values = jnp.concatenate(rows)
-    entry = neighbours - 1
-    hit = entry[:, :, None] == jnp.arange(8 * SLOTS, dtype=jnp.int32)
-    remote = jnp.sum(jnp.where(hit, values, 0), axis=2)
-    found = jnp.where(entry >= 8 * SLOTS, entry - 8 * SLOTS, remote)
-    return jnp.where(neighbours == 0, ZERO, found)
+            values = jnp.where(core == 0, row(near, d), row(far, d))
+        for j in range(SLOTS):
+            found = jnp.where(entry == 1 + SLOTS * d + j, values[:, j : j + 1], found)
+    return jnp.clip(found, 0, ZERO)
 
 
 def fill_pool(core, pool, tiles_ref, halo_refs):
@@ -240,26 +245,6 @@
     return total
 
 
-def turned_sum(pairs):
-    total = None
-    for first in range(0, len(pairs), 2):
-        group = pairs[first : first + 2]
-        left = jnp.concatenate([rows for rows, _ in group], axis=1)
-        right = jnp.concatenate([tap for _, tap in group], axis=1)
-        term = lax.dot_general(left, right, (((1,), (1,)), ((), ())), preferred_element_type=F32)
-        total = term if total is None else total + term
-    return total
-
-
-def inner_sum(windows, summed, tap_weight, sign, p):
-    pairs = []
-    for t in range(TAPS):
-        ox, oy, oz = (sign * (v - 1) for v in (t // 9, t // 3 % 3, t % 3))
-        rows = windows[oz + 1, p + ox + 1, oy + 1 : oy + 9].reshape(256, CH)
-        pairs.append((rows, tap_weight(t)))
-    return summed(pairs)
-
-
 def margin_sums(ends, strips, summed, tap_weight, sign):
     added = []
     for side in range(2):
@@ -283,44 +268,63 @@
     return jnp.concatenate(parts, axis=0)
 
 
-def narrowed(rows):
-    return jnp.dot(jnp.concatenate(rows, axis=1), picks(), preferred_element_type=F32).astype(BF16)
-
-
-def inner_kernel(nb_ref, tiles_ref, w0_ref, w1_ref, w2_ref, w3_ref, hidden_ref, narrow_ref, zero, windows):
+def narrowed(rows, picked):
+    return jnp.dot(jnp.concatenate(rows, axis=1), picked, preferred_element_type=F32).astype(BF16)
+
+
+def inner_kernel(
+    nb_ref, chan_ref, tiles_ref, w0_ref, w1_ref, w2_ref, w3_ref, hidden_ref, narrow_ref, cot_ref, zero, windows, wide, padded, whole
+):
     inner_windows(nb_ref, tiles_ref, zero, windows)
-    weights = (w0_ref, w1_ref, w2_ref, w3_ref)
-
-    def tap_weight(t):
-        return jnp.concatenate([ref[t] for ref in weights], axis=0)
+    blocks = (w0_ref, w1_ref, w2_ref, w3_ref)
+    for t in range(TAPS):
+        row, lane = CH * (t % 9), CH * (t // 9)
+        for s, ref in enumerate(blocks):
+            wide[row + OWN * s : row + OWN * s + OWN, lane : lane + CH] = ref[OWN * t : OWN * t + OWN]
+    for p in range(10):
+        padded[p] = jnp.zeros((8, 32, CH), F32)
+    picked = picks()
 
     def body(p, carry):
-        hidden_ref[p] = inner_sum(windows, conv_sum, tap_weight, 1, p).reshape(8, 32, CH)
+        left = [windows[t % 3, p + 1, t // 3 : t // 3 + 8].reshape(256, CH) for t in range(9)]
+        total = jnp.dot(jnp.concatenate(left, axis=1), wide[...], preferred_element_type=F32)
+        for i in range(3):
+            padded[p + 2 - i] += total[:, CH * i : CH * i + CH].reshape(8, 32, CH)
         rows = [windows[k, p + 1, 1:9].reshape(256, CH) for k in range(3)]
-        narrow_ref[p] = narrowed(rows).reshape(8, 32, CH)
+        narrow_ref[p] = narrowed(rows, picked).reshape(8, 32, CH)
         return carry
 
     lax.fori_loop(0, 8, body, 0)
-
-
-def inner(neighbours, tiles, weights):
+    for p in range(8):
+        hidden_ref[p] = padded[p + 1]
+    turn_field(chan_ref[0], blocks, TAPS * OWN, whole, cot_ref)
+
+
+def inner(neighbours, chan, tiles, blocks):
     return pl.pallas_call(
         inner_kernel,
-        out_shape=[jax.ShapeDtypeStruct((8, 8, 32, CH), F32), jax.ShapeDtypeStruct((8, 8, 32, CH), BF16)],
-        in_specs=[SMEM] + [VMEM] * 5,
-        out_specs=[VMEM] * 2,
+        out_shape=[
+            jax.ShapeDtypeStruct((8, 8, 32, CH), F32),
+            jax.ShapeDtypeStruct((8, 8, 32, CH), BF16),
+            jax.ShapeDtypeStruct((BR, 64, 8, CH), F32),
+        ],
+        in_specs=[SMEM] * 2 + [VMEM] * 5,
+        out_specs=[VMEM] * 3,
         scratch_shapes=[
             pltpu.VMEM((5, 64, 8, CH), F32),
             pltpu.VMEM((3, 10, 10, 32, CH), BF16),
+            pltpu.VMEM((9 * CH, 3 * CH), BF16),
+            pltpu.VMEM((10, 8, 32, CH), F32),
+            pltpu.VMEM((CH, BR * VOX), F32),
         ],
-        compiler_params=params(),
+        compiler_params=params(20),
         cost_estimate=cost(2 * 27 * CH * CH * 2048, 2**24),
-    )(neighbours, tiles, *weights)
+    )(neighbours, chan, tiles, *blocks)
 
 
 def gate_kernel(
-    index_ref,
     place_ref,
+    entry_ref,
     tiles_ref,
     cot_ref,
     inner_ref,
@@ -341,6 +345,8 @@
     high_ref,
     keep_ref,
     send_ref,
+    index_out_ref,
+    index_ref,
     pool,
     ends,
     strips,
@@ -350,12 +356,15 @@
     sums,
 ):
     core = place_ref[0]
+    index_out_ref[...] = pool_index(entry_ref[...], core, (side_m_ref, side_n_ref, left_ref, right_ref))
+    pltpu.sync_copy(index_out_ref, index_ref)
     weights = (w0_ref, w1_ref, w2_ref, w3_ref)
+    picked = picks()
     fill_pool(core, pool, tiles_ref, (side_m_ref, side_n_ref, left_ref, right_ref))
     margin_windows(index_ref, pool, ends, strips)
 
     def tap_weight(t):
-        return jnp.concatenate([ref[t] for ref in weights], axis=0)
+        return jnp.concatenate([ref[OWN * t : OWN * t + OWN] for ref in weights], axis=0)
 
     for p in range(8):
         hidden[p] = inner_ref[p]
@@ -365,9 +374,9 @@
         for p in range(8):
             hidden[p, 7 * side] += along_y[32 * p : 32 * p + 32]
         rows = [ends[side, k].reshape(320, CH) for k in range(3)]
-        narrow[9 * side] = narrowed(rows).reshape(10, 32, CH)
+        narrow[9 * side] = narrowed(rows, picked).reshape(10, 32, CH)
         rows = [strips[side, k, 1:9].reshape(256, CH) for k in range(3)]
-        small = narrowed(rows)
+        small = narrowed(rows, picked)
         for p in range(8):
             narrow[p + 1, 9 * side] = small[32 * p : 32 * p + 32]
 
@@ -390,32 +399,29 @@
     lax.fori_loop(0, 8, gate_body, 0)
     emit_faces(core, grad_ref, None, (face_m_ref, face_n_ref, low_ref, high_ref))
 
-    for i in range(3):
-
-        def sum_body(p, carry, i=i):
-            left = grad_rows[p]
-            right = [narrow[p + i, j : j + 8].reshape(256, CH) for j in range(3)]
-            return carry + jnp.dot(left, jnp.concatenate(right, axis=1), preferred_element_type=F32)
-
-        total = lax.fori_loop(0, 8, sum_body, jnp.zeros((CH, 3 * CH), F32))
-        for j in range(3):
-            start = 96 * (3 * i + j)
-            sums[start : start + 96] = total[:, CH * j : CH * j + CH].T[:96]
+    left = jnp.concatenate([grad_rows[p] for p in range(8)], axis=1)
+    for first in range(0, 9, 2):
+        group = range(first, min(first + 2, 9))
+        right = [narrow[t // 3 : t // 3 + 8, t % 3 : t % 3 + 8].reshape(2048, CH) for t in group]
+        total = jnp.dot(left, jnp.concatenate(right, axis=1), preferred_element_type=F32)
+        for k, t in enumerate(group):
+            sums[96 * t : 96 * t + 96] = total[:, CH * k : CH * k + CH].T[:96]
     sums[864:896] = jnp.zeros((32, CH), F32)
     keep_ref[...] = sums[pl.ds(pl.multiple_of(448 * core, 8), 448), :]
     send_ref[...] = sums[pl.ds(pl.multiple_of(448 * (1 - core), 8), 448), :]
 
 
-def gate(index, core, tiles, cot, hidden, narrow, halo, weights):
+def gate(core, entries, tiles, cot, hidden, narrow, halo, weights):
     face = jax.ShapeDtypeStruct((272, CH), BF16)
     half = jax.ShapeDtypeStruct((448, CH), F32)
     field = jax.ShapeDtypeStruct((BR, 64, 8, CH), F32)
     return pl.pallas_call(
         gate_kernel,
-        out_shape=[field, field, face, face, face, face, half, half],
-        in_specs=[SMEM] * 2 + [VMEM] * 12,
-        out_specs=[VMEM] * 8,
+        out_shape=[field, field, face, face, face, face, half, half, jax.ShapeDtypeStruct((8, CH), jnp.int32)],
+        in_specs=[SMEM] + [VMEM] * 13,
+        out_specs=[VMEM] * 9,
         scratch_shapes=[
+            pltpu.SMEM((8, CH), jnp.int32),
             pltpu.VMEM((40, 64, 8, CH), F32),
             pltpu.VMEM((2, 3, 10, 32, CH), BF16),
             pltpu.VMEM((2, 3, 10, 32, CH), BF16),
@@ -424,94 +430,131 @@
             pltpu.VMEM((8, CH, 256), BF16),
             pltpu.VMEM((896, CH), F32),
         ],
-        compiler_params=params(),
+        compiler_params=params(28),
         cost_estimate=cost(2 * 27 * CH * CH * 1024, 2**24),
-    )(index, core, tiles, cot, hidden, narrow, *halo, *weights)
-
-
-def back_inner_kernel(nb_ref, chan_ref, tiles_ref, weight_ref, gated_ref, feat_ref, part_ref, out_ref, zero, windows, turned):
+    )(core, entries, tiles, cot, hidden, narrow, *halo, *weights)
+
+
+def back_inner_kernel(nb_ref, tiles_ref, turned_ref, part_ref, zero, windows, planes):
     inner_windows(nb_ref, tiles_ref, zero, windows)
+    planes[0] = jnp.zeros((256, CH), F32)
+    planes[9] = jnp.zeros((256, CH), F32)
 
     def body(p, carry):
-        part_ref[p] = inner_sum(windows, turned_sum, lambda t: weight_ref[t], -1, p).reshape(8, 32, OWN)
+        left = [windows[2 - t % 3, p + 1, 2 - t // 3 : 10 - t // 3].reshape(256, CH) for t in range(9)]
+        planes[p + 1] = jnp.dot(jnp.concatenate(left, axis=1), turned_ref[...], preferred_element_type=F32)
         return carry
 
     lax.fori_loop(0, 8, body, 0)
-    own = pl.multiple_of(chan_ref[0] * OWN, OWN)
-    for b in range(BR):
-        for k in range(4):
-            start = VOX * b + 128 * k
-            turned[:, start : start + 128] = gated_ref[b, 16 * k : 16 * k + 16].reshape(128, CH).T
-    out_ref[...] = (feat_ref[...].astype(F32) + turned[pl.ds(own, OWN), :]).astype(BF16)
-
-
-def back_inner(neighbours, chan, tiles, weight, gated, features):
+    for p in range(8):
+        summed = planes[p + 2] + pltpu.roll(planes[p + 1], CH - OWN, 1) + pltpu.roll(planes[p], CH - 2 * OWN, 1)
+        part_ref[p] = summed.reshape(8, 32, CH)
+
+
+def back_inner(neighbours, tiles, turned):
     return pl.pallas_call(
         back_inner_kernel,
-        out_shape=[
-            jax.ShapeDtypeStruct((8, 8, 32, OWN), F32),
-            jax.ShapeDtypeStruct((OWN, BR * VOX), BF16),
-        ],
-        in_specs=[SMEM] * 2 + [VMEM] * 4,
-        out_specs=[VMEM] * 2,
+        out_shape=jax.ShapeDtypeStruct((8, 8, 32, CH), F32),
+        in_specs=[SMEM] + [VMEM] * 2,
+        out_specs=VMEM,
         scratch_shapes=[
             pltpu.VMEM((5, 64, 8, CH), F32),
             pltpu.VMEM((3, 10, 10, 32, CH), BF16),
-            pltpu.VMEM((CH, BR * VOX), F32),
+            pltpu.VMEM((10, 256, CH), F32),
         ],
-        compiler_params=params(),
-        cost_estimate=cost(2 * 27 * CH * CH * 2048, 2**24),
-    )(neighbours, chan, tiles, weight, gated, features)
+        compiler_params=params(14),
+        cost_estimate=cost(2 * 27 * CH * CH * 1024, 2**23),
+    )(neighbours, tiles, turned)
+
+
+def output_kernel(chan_ref, gated_ref, feat_ref, out_ref, turned):
+    own = pl.multiple_of(chan_ref[0] * OWN, OWN)
+    for k in range(16):
+        turned[k] = gated_ref[k // 4, 16 * (k % 4) : 16 * (k % 4) + 16].reshape(128, CH).T
+        rows = feat_ref[OWN * k : OWN * k + OWN].astype(F32) + turned[k, pl.ds(own, OWN), :]
+        out_ref[OWN * k : OWN * k + OWN] = rows.astype(BF16)
+
+
+def output_of(chan, gated, features):
+    return pl.pallas_call(
+        output_kernel,
+        out_shape=jax.ShapeDtypeStruct((16 * OWN, CH), BF16),
+        in_specs=[SMEM] + [VMEM] * 2,
+        out_specs=VMEM,
+        scratch_shapes=[pltpu.VMEM((16, CH, CH), F32)],
+        compiler_params=params(6),
+        cost_estimate=cost(0, 2**22),
+    )(chan, gated, features)
 
 
 def back_margin_kernel(
-    index_ref,
     place_ref,
+    index_in_ref,
     tiles_ref,
     side_m_ref,
     side_n_ref,
     left_ref,
     right_ref,
-    weight_ref,
+    turned_ref,
     part_ref,
     cot_ref,
     grad_ref,
+    index_ref,
     pool,
     ends,
     strips,
     result,
 ):
+    pltpu.sync_copy(index_in_ref, index_ref)
     fill_pool(place_ref[0], pool, tiles_ref, (side_m_ref, side_n_ref, left_ref, right_ref))
     margin_windows(index_ref, pool, ends, strips)
     for p in range(8):
         result[p] = part_ref[p]
-    for side, (along_x, along_y) in enumerate(margin_sums(ends, strips, turned_sum, lambda t: weight_ref[t], -1)):
-        result[7 * side] += along_x.reshape(8, 32, OWN)
+    blank = jnp.zeros((32, CH), F32)
+    for side in range(2):
+        left = [ends[side, 2 - t % 3, 2 - t // 3 : 10 - t // 3].reshape(256, CH) for t in range(9)]
+        along_x = jnp.dot(jnp.concatenate(left, axis=1), turned_ref[...], preferred_element_type=F32)
+        if side == 0:
+            along_x = pltpu.roll(along_x, CH - 2 * OWN, 1)
+        result[7 * side] += along_x.reshape(8, 32, CH)
+        j = 2 - 2 * side
+        left = [strips[side, 2 - k, 1:9].reshape(256, CH) for k in range(3)]
+        along_y = jnp.dot(
+            jnp.concatenate(left, axis=1), turned_ref[3 * CH * j : 3 * CH * (j + 1)], preferred_element_type=F32
+        )
+        here = pltpu.roll(along_y, CH - OWN, 1)
+        before = pltpu.roll(along_y, CH - 2 * OWN, 1)
         for p in range(8):
-            result[p, 7 * side] += along_y[32 * p : 32 * p + 32]
+            rows = here[32 * p : 32 * p + 32]
+            if p < 7:
+                rows = rows + along_y[32 * p + 32 : 32 * p + 64]
+            if p > 0:
+                rows = rows + before[32 * p - 32 : 32 * p]
+            result[p, 7 * side] += rows
     for b in range(BR):
         for k in range(4):
-            start = VOX * b + 128 * k
-            block = result[2 * k : 2 * k + 2, :, 8 * b : 8 * b + 8, :].reshape(128, OWN)
-            summed = cot_ref[:, start : start + 128].astype(F32) + block.T
-            grad_ref[:, start : start + 128] = summed.astype(BF16)
-
-
-def back_margin(index, core, tiles, halo, weight, part, cotangent):
+            at = OWN * (4 * b + k)
+            block = result[2 * k : 2 * k + 2, :, 8 * b : 8 * b + 8, :].reshape(128, CH)
+            summed = cot_ref[at : at + OWN].astype(F32) + block.T[:OWN]
+            grad_ref[at : at + OWN] = summed.astype(BF16)
+
+
+def back_margin(core, index, tiles, halo, turned, part, cotangent):
     return pl.pallas_call(
         back_margin_kernel,
-        out_shape=jax.ShapeDtypeStruct((OWN, BR * VOX), BF16),
-        in_specs=[SMEM] * 2 + [VMEM] * 8,
+        out_shape=jax.ShapeDtypeStruct((16 * OWN, CH), BF16),
+        in_specs=[SMEM] + [VMEM] * 9,
         out_specs=VMEM,
         scratch_shapes=[
+            pltpu.SMEM((8, CH), jnp.int32),
             pltpu.VMEM((40, 64, 8, CH), F32),
             pltpu.VMEM((2, 3, 10, 32, CH), BF16),
             pltpu.VMEM((2, 3, 10, 32, CH), BF16),
-            pltpu.VMEM((8, 8, 32, OWN), F32),
+            pltpu.VMEM((8, 8, 32, CH), F32),
         ],
-        compiler_params=params(),
+        compiler_params=params(20),
         cost_estimate=cost(2 * 27 * CH * CH * 512, 2**23),
-    )(index, core, tiles, *halo, weight, part, cotangent)
+    )(core, index, tiles, *halo, turned, part, cotangent)
 
 
 def ring_gather(value, axis):
@@ -586,37 +629,43 @@
         out_shape=jax.ShapeDtypeStruct((864, CH), F32),
         in_specs=[SMEM] + [VMEM] * 4,
         out_specs=VMEM,
-        compiler_params=params(),
+        compiler_params=params(4),
         cost_estimate=cost(0, 2**20),
     )(me ^ jnp.arange(8, dtype=jnp.int32), value, two, four, eight)
 
 
+def to_rows(field):
+    return field.reshape(OWN, 16, CH).transpose(1, 0, 2).reshape(16 * OWN, CH)
+
+
+def from_rows(rows):
+    return rows.reshape(16, OWN, CH).transpose(1, 0, 2).reshape(OWN, BR, VOX)
+
+
 def per_device(features, weight, cotangent, neighbours, send_slots):
-    core = lax.axis_index("core").astype(jnp.int32)
+    core = lax.axis_index("core").astype(jnp.int32).reshape(1)
     chan = lax.axis_index("chan").astype(jnp.int32).reshape(1)
-    core_at = core.reshape(1)
-    feat_own = features.reshape(OWN, BR * VOX)
-    cot_own = cotangent.reshape(OWN, BR * VOX)
+    feat_own = to_rows(features)
+    cot_own = to_rows(cotangent)
     table = jnp.pad(send_slots.astype(BF16), ((0, 8), (0, CH - SLOTS)))
+    entries = jnp.pad(neighbours, ((0, 4), (0, CH - TAPS)))
     feat_blocks = ring_gather(feat_own, "chan")
-    weights = ring_gather(weight, "chan")
-
-    tiles, *faces = prep(core_at, feat_blocks, table)
+    both = jnp.concatenate([weight.reshape(TAPS * OWN, CH), cot_own], axis=0)
+    blocks = ring_gather(both, "chan")
+    turned = turn_weight(weight)
+    table = after(table, turned, entries)
+
+    tiles, *faces = prep(core, feat_blocks, table)
     halo = exchange(faces)
-    cot_blocks = ring_gather(after(cot_own, *halo[:2]), "chan")
-    hidden, narrow = inner(neighbours, tiles, weights)
-    cot = turn(chan, cot_blocks)
-    index = pool_index(neighbours, core, halo)
-    gated, grads, face_m, face_n, low, high, keep, send = gate(index, core_at, tiles, cot, hidden, narrow, halo, weights)
-    grad_halo = exchange((face_m, face_n, low, high))
-    part, out = back_inner(neighbours, chan, grads, weight, gated, feat_own)
-    grad_input = back_margin(index, core_at, grads, grad_halo, weight, part, cot_own)
-    grad_weight = reduce_space(keep, send, (grad_halo[:2], (part,), grad_halo[2:], (grad_input,), ()))
-    return (
-        out.reshape(OWN, BR, VOX),
-        grad_input.reshape(OWN, BR, VOX),
-        grad_weight.reshape(TAPS, OWN, CH),
-    )
+    hidden, narrow, cot = inner(neighbours, chan, tiles, blocks)
+    gated, grads, *rest = gate(core, entries, tiles, cot, hidden, narrow, halo, blocks)
+    grad_faces, keep, send, index = rest[:4], rest[4], rest[5], rest[6]
+    grad_halo = exchange(grad_faces)
+    part = back_inner(neighbours, grads, turned)
+    out = output_of(chan, gated, feat_own)
+    grad_input = back_margin(core, index, grads, grad_halo, turned, part, cot_own)
+    grad_weight = reduce_space(keep, send, ((part,), (out,), (), (grad_input,), ()))
+    return (from_rows(out), from_rows(grad_input), grad_weight.reshape(TAPS, OWN, CH))
 
 
 def solution(mesh):

time: 123 us -> 91.5 us (0.74); the launches traced: 121 us -> 91.2 us
  Pallas kernels: 37.8 us -> 18 us
  local copies, waits for them, and re-layouts: 12 us -> 3.6 us
  other arithmetic: 1.89 us -> 0.14 us
  starting transfers between devices: 54.1 us -> 52.6 us
  waiting for transfers between devices: 14.3 us -> 15.8 us
    unnamed x87 -> x31, local copies, waits for them, and re-layouts: 9.6 us -> 0.9 us
    pallas_call x3 -> x4, Pallas kernels: 14.1 us -> 6.39 us  [the longest x1 4.15 us: back_inner(): pl.pallas_call(back_inner_kernel, out_shape=jax.ShapeDtypeStruct((8, 8, 3...]
    pallas_call x1, Pallas kernels: 11 us -> 4.08 us  [gate(): pl.pallas_call(gate_kernel, out_shape=[field, field, face, face, face, fa...]
    ppermute x9 -> x6, starting transfers between devices: 12 us -> 8.94 us  [ring_gather(): lax.ppermute(value, axis, [(i, (i + step) % count) for i in range(count)])]
    pallas_call x1, Pallas kernels: 8.43 us -> 5.86 us  [inner(): pl.pallas_call(inner_kernel, out_shape=[jax.ShapeDtypeStruct((8, 8, 32, C...]
    pallas_call x1, Pallas kernels: 2.41 us -> 0.24 us  [prep(): pl.pallas_call(prep_kernel, out_shape=[jax.ShapeDtypeStruct((BR, 64, 8, C...]
    ppermute x9, waiting for transfers between devices: 11.2 us -> 12.8 us  [swapped(): return lax.ppermute(value, axis, list(enumerate(partner)))]
    reshape x2 -> x6, local copies, waits for them, and re-layouts: 1.46 us -> 2.51 us  [the longest x2 1.43 us: from_rows(): return rows.reshape(16, OWN, CH).transpose(1, 0, 2).reshape(OWN, BR, VOX)]
  transfers between devices with their start and end apart: 26 -> 23, of which waited for: 7 -> 8; matrix products, arithmetic and copies ran while one was open for 6% -> 2% of each run, Pallas kernels for 18% -> 14%
where the time goes in v3:
time: 91.5 us; the launch traced here: 91.2 us
  starting transfers between devices  52.6 us (57%)
  Pallas kernels  18 us (20%)
  waiting for transfers between devices  15.8 us (17%)
  local copies, waits for them, and re-layouts  3.6 us (4%)
  between operations  1.06 us (1%)
    ppermute x9, starting transfers between devices, swapped(): return lax.ppermute(value, axis, list(enumerate(partner)))  23.3 us
    ppermute x9, waiting for transfers between devices, swapped(): return lax.ppermute(value, axis, list(enumerate(partner)))  12.8 us
    ppermute x4, starting transfers between devices, shifted(): lax.ppermute(value, SPACE, [(i, i + steps) for i in range(first, last)])  10.3 us
    ppermute x6, starting transfers between devices, ring_gather(): lax.ppermute(value, axis, [(i, (i + step) % count) for i in range(count)])  8.94 us
    ppermute x2, starting transfers between devices, exchange(): side_n = lax.ppermute(face_n, SPACE, across)  7 us
    pallas_call x1, Pallas kernels, inner(): pl.pallas_call(inner_kernel, out_shape=[jax.ShapeDtypeStruct((8, 8, 32, C...  5.86 us
    pallas_call x1, Pallas kernels, back_inner(): pl.pallas_call(back_inner_kernel, out_shape=jax.ShapeDtypeStruct((8, 8, 3...  4.15 us
    pallas_call x1, Pallas kernels, gate(): pl.pallas_call(gate_kernel, out_shape=[field, field, face, face, face, fa...  4.08 us
  transfers between devices with their start and end apart: 23, of which 8 were waited for; matrix products, arithmetic and copies ran while one was open for 2% of the time, Pallas kernels for 14%

profile of v3, /device:TPU:1, one launch (start us, length us, event | category | flops | bytes accessed | tf_op | source)
XLA Modules:
  0.0 91.2 jit_solution(3637062455807295173)
XLA Ops:
  1.7 2.2 %collective-permute-start = (bf16[512,128]{1,0:T(8,128)(2,1)S(1)}, bf16[512,128]{1,0:T(8,128)(2,1)S(1)}, u32[]{:S(2)}, u32[]{:S(2)}) collective-permute-start(bf16[512,128]{1,0:T(8,128)(2,1)S(1)} %bitcast.26), channel_id=1, source_target_pairs={{0,1},{1,2},{2,3},{3,0},{4,5},{5,6},{6,7},{7,4},{8,9},{9,10},{10,1... | collective-permute-start | bytes 393224 | tf_op jit(solution)/shard_map/ppermute | solution.py:564
  3.9 2.6 %collective-permute-start.1 = (bf16[512,128]{1,0:T(8,128)(2,1)S(1)}, bf16[512,128]{1,0:T(8,128)(2,1)S(1)}, u32[]{:S(2)}, u32[]{:S(2)}) collective-permute-start(bf16[512,128]{1,0:T(8,128)(2,1)S(1)} %bitcast.27), channel_id=1, source_target_pairs={{0,2},{1,3},{2,0},{3,1},{4,6},{5,7},{6,4},{7,5},{8,10},{9,11},{10,... | collective-permute-start | bytes 393224 | tf_op jit(solution)/shard_map/ppermute | solution.py:564
  9.9 1.8 %collective-permute-start.5 = (bf16[1376,128]{1,0:T(8,128)(2,1)S(1)}, bf16[1376,128]{1,0:T(8,128)(2,1)S(1)}, u32[]{:S(2)}, u32[]{:S(2)}) collective-permute-start(bf16[1376,128]{1,0:T(8,128)(2,1)S(1)} %pad_maximum_fusion.w0_ref), channel_id=1, source_target_pairs={{0,3},{1,0},{2,1},{3,2},{4,7},{5,4},{6,5},{7,6},{8,11},{9,8},{10,9... | collective-permute-start | bytes 1056776 | tf_op jit(solution)/shard_map/ppermute | solution.py:564
  12.4 2.9 %collective-permute-start.6 = (bf16[272,128]{1,0:T(8,128)(2,1)S(1)}, bf16[272,128]{1,0:T(8,128)(2,1)S(1)}, u32[]{:S(2)}, u32[]{:S(2)}) collective-permute-start(bf16[272,128]{1,0:T(8,128)(2,1)S(1)} %get-tuple-element.29), channel_id=1, source_target_pairs={{0,4},{4,0},{1,5},{5,1},{2,6},{6,2},{3,7},{7,3},{8,12},{12,8},{9,1... | collective-permute-start | bytes 208904 | tf_op jit(solution)/shard_map/ppermute | solution.py:114
  15.3 3.3 %collective-permute-start.7 = (bf16[272,128]{1,0:T(8,128)(2,1)S(1)}, bf16[272,128]{1,0:T(8,128)(2,1)S(1)}, u32[]{:S(2)}, u32[]{:S(2)}) collective-permute-start(bf16[272,128]{1,0:T(8,128)(2,1)S(1)} %get-tuple-element.30), channel_id=1, source_target_pairs={{4,8},{20,24},{36,40},{52,56},{68,72},{84,88},{100,104},{116,120},... | collective-permute-start | bytes 208904 | tf_op jit(solution)/shard_map/ppermute | solution.py:113
  18.8 2.5 %collective-permute-done.7.side_n_ref = bf16[272,128]{1,0:T(8,128)(2,1)S(1)} collective-permute-done((bf16[272,128]{1,0:T(8,128)(2,1)S(1)}, bf16[272,128]{1,0:T(8,128)(2,1)S(1)}, u32[]{:S(2)}, u32[]{:S(2)}) %collective-permute-start.7) | collective-permute-done | bytes 69664 | tf_op jit(solution)/shard_map/ppermute | solution.py:113
  22.6 5.5 %collective-permute-start.8 = (bf16[368,128]{1,0:T(8,128)(2,1)S(1)}, bf16[368,128]{1,0:T(8,128)(2,1)S(1)}, u32[]{:S(2)}, u32[]{:S(2)}) collective-permute-start(bf16[368,128]{1,0:T(8,128)(2,1)S(1)} %constant_dynamic-update-slice_fusion), channel_id=1, source_target_pairs={{0,16},{4,20},{8,24},{12,28},{16,32},{20,36},{24,40},{28,44},{32,4... | collective-permute-start | bytes 282632 | tf_op jit(solution)/shard_map/ppermute | solution.py:36
  28.2 5.9 %shard_map.78 = (f32[8,8,32,128]{3,2,1,0:T(8,128)S(1)}, bf16[8,8,32,128]{3,2,1,0:T(8,128)(2,1)S(1)}, f32[4,64,8,128]{3,2,1,0:T(8,128)S(1)}) custom-call(s32[4,27]{1,0:T(4,128)S(1)} %copy-done.1, s32[1]{0:T(128)} %bitcast.chan_ref, f32[4,64,8,128]{3,2,1,0:T(8,128)S(1)} %get-tuple-element.25.tiles_ref, bf16[1376,128]{1,0:T(8,128)(2,1)S(1)} %pad_maximum_fusion.w0_ref, ...), custom_call_target="tpu_custom_call" | custom-call | flops 1811939328 | bytes 16777216 | tf_op jit(solution)/shard_map/pallas_call | solution.py:304
  34.1 4.1 %shard_map.79 = (f32[4,64,8,128]{3,2,1,0:T(8,128)S(1)}, f32[4,64,8,128]{3,2,1,0:T(8,128)S(1)}, bf16[272,128]{1,0:T(8,128)(2,1)S(1)}, bf16[272,128]{1,0:T(8,128)(...) custom-call(s32[1]{0:T(128)} %bitcast.1.core_ref.place_ref, ...), custom_call_target="tpu_custom_call" | custom-call | flops 905969664 | bytes 16777216 | tf_op jit(solution)/shard_map/pallas_call | solution.py:418
  39.6 3.7 %collective-permute-start.11 = (bf16[272,128]{1,0:T(8,128)(2,1)S(1)}, bf16[272,128]{1,0:T(8,128)(2,1)S(1)}, u32[]{:S(2)}, u32[]{:S(2)}) collective-permute-start(bf16[272,128]{1,0:T(8,128)(2,1)S(1)} %get-tuple-element.37), channel_id=1, source_target_pairs={{4,8},{20,24},{36,40},{52,56},{68,72},{84,88},{100,104},{116,120},... | collective-permute-start | bytes 208904 | tf_op jit(solution)/shard_map/ppermute | solution.py:113
  43.3 4.2 %shard_map.81.part_ref = f32[8,8,32,128]{3,2,1,0:T(8,128)S(1)} custom-call(s32[4,27]{1,0:T(4,128)S(1)} %copy-done.1, f32[4,64,8,128]{3,2,1,0:T(8,128)S(1)} %get-tuple-element.35.tiles_ref, bf16[1152,128]{1,0:T(8,128)(2,1)S(1)} %shard_map.76.turned_ref), custom_call_target="tpu_custom_call" | custom-call | flops 905969664 | bytes 8388608 | tf_op jit(solution)/shard_map/pallas_call | solution.py:455
  47.7 7.0 %collective-permute-start.15 = (f32[224,128]{1,0:T(8,128)S(1)}, f32[224,128]{1,0:T(8,128)S(1)}, u32[]{:S(2)}, u32[]{:S(2)}) collective-permute-start(f32[224,128]{1,0:T(8,128)S(1)} %dynamic-slice_bitcast_fusion), channel_id=1, source_target_pairs={{0,192},{64,128},{128,64},{192,0},{1,193},{65,129},{129,65},{193,1... | collective-permute-start | bytes 344072 | tf_op jit(solution)/shard_map/ppermute | solution.py:569
  56.9 1.9 %collective-permute-start.16 = (f32[112,128]{1,0:T(8,128)S(1)}, f32[112,128]{1,0:T(8,128)S(1)}, u32[]{:S(2)}, u32[]{:S(2)}) collective-permute-start(f32[112,128]{1,0:T(8,128)S(1)} %dynamic-slice_bitcast_fusion.1), channel_id=1, source_target_pairs={{0,64},{64,0},{128,192},{192,128},{1,65},{65,1},{129,193},{193,129... | collective-permute-start | bytes 172040 | tf_op jit(solution)/shard_map/ppermute | solution.py:569
  58.8 2.2 %collective-permute-start.12 = (bf16[368,128]{1,0:T(8,128)(2,1)S(1)}, bf16[368,128]{1,0:T(8,128)(2,1)S(1)}, u32[]{:S(2)}, u32[]{:S(2)}) collective-permute-start(bf16[368,128]{1,0:T(8,128)(2,1)S(1)} %constant_dynamic-update-slice_fusion.20), channel_id=1, source_target_pairs={{0,16},{4,20},{8,24},{12,28},{16,32},{20,36},{24,40},{28,44},{32,4... | collective-permute-start | bytes 282632 | tf_op jit(solution)/shard_map/ppermute | solution.py:36
  61.1 3.7 %collective-permute-done.17 = f32[112,128]{1,0:T(8,128)S(1)} collective-permute-done((f32[112,128]{1,0:T(8,128)S(1)}, f32[112,128]{1,0:T(8,128)S(1)}, u32[]{:S(2)}, u32[]{:S(2)}) %collective-permute-start.17) | collective-permute-done | bytes 57376 | tf_op jit(solution)/shard_map/ppermute | solution.py:569
  65.9 1.7 %shard_map.82 = bf16[512,128]{1,0:T(8,128)(2,1)S(1)} custom-call(s32[1]{0:T(128)} %bitcast.1.core_ref.place_ref, s32[8,128]{1,0:T(8,128)S(1)} %get-tuple-element.34.index_in_ref, f32[4,64,8,128]{3,2,1,0:T(8,128)S(1)} %get-tuple-element.35.tiles_ref, bf16[272,128]{1,0:T(8,128)(2,1)S(1)} %collective-permute-done.10.side_m_ref, ...), custom_call_target="tpu_custom_call" | custom-call | flops 452984832 | bytes 8388608 | tf_op jit(solution)/shard_map/pallas_call | solution.py:543
  68.9 3.3 %collective-permute-start.19 = (f32[112,128]{1,0:T(8,128)S(1)}, f32[112,128]{1,0:T(8,128)S(1)}, u32[]{:S(2)}, u32[]{:S(2)}) collective-permute-start(f32[112,128]{1,0:T(8,128)S(1)} %add.55), channel_id=1, source_target_pairs={{0,48},{8,56},{16,32},{24,40},{32,16},{40,24},{48,0},{56,8},{1,49}... | collective-permute-start | bytes 172040 | tf_op jit(solution)/shard_map/ppermute | solution.py:569
  72.2 2.1 %collective-permute-done.19 = f32[112,128]{1,0:T(8,128)S(1)} collective-permute-done((f32[112,128]{1,0:T(8,128)S(1)}, f32[112,128]{1,0:T(8,128)S(1)}, u32[]{:S(2)}, u32[]{:S(2)}) %collective-permute-start.19) | collective-permute-done | bytes 57376 | tf_op jit(solution)/shard_map/ppermute | solution.py:569
  74.3 1.4 %collective-permute-start.20 = (f32[112,128]{1,0:T(8,128)S(1)}, f32[112,128]{1,0:T(8,128)S(1)}, u32[]{:S(2)}, u32[]{:S(2)}) collective-permute-start(f32[112,128]{1,0:T(8,128)S(1)} %add.56.one_ref), channel_id=1, source_target_pairs={{0,64},{64,0},{128,192},{192,128},{1,65},{65,1},{129,193},{193,129... | collective-permute-start | bytes 172040 | tf_op jit(solution)/shard_map/ppermute | solution.py:569
  75.8 1.7 %collective-permute-done.20.two_ref = f32[112,128]{1,0:T(8,128)S(1)} collective-permute-done((f32[112,128]{1,0:T(8,128)S(1)}, f32[112,128]{1,0:T(8,128)S(1)}, u32[]{:S(2)}, u32[]{:S(2)}) %collective-permute-start.20) | collective-permute-done | bytes 57376 | tf_op jit(solution)/shard_map/ppermute | solution.py:569
  77.5 1.8 %collective-permute-start.21 = (f32[224,128]{1,0:T(8,128)S(1)}, f32[224,128]{1,0:T(8,128)S(1)}, u32[]{:S(2)}, u32[]{:S(2)}) collective-permute-start(f32[224,128]{1,0:T(8,128)S(1)} %pad_maximum_fusion.2), channel_id=1, source_target_pairs={{0,192},{64,128},{128,64},{192,0},{1,193},{65,129},{129,65},{193,1... | collective-permute-start | bytes 344072 | tf_op jit(solution)/shard_map/ppermute | solution.py:569
  79.3 3.1 %collective-permute-done.21.four_ref = f32[224,128]{1,0:T(8,128)S(1)} collective-permute-done((f32[224,128]{1,0:T(8,128)S(1)}, f32[224,128]{1,0:T(8,128)S(1)}, u32[]{:S(2)}, u32[]{:S(2)}) %collective-permute-start.21) | collective-permute-done | bytes 114720 | tf_op jit(solution)/shard_map/ppermute | solution.py:569
  82.4 5.8 %collective-permute-start.22 = (f32[448,128]{1,0:T(8,128)S(1)}, f32[448,128]{1,0:T(8,128)S(1)}, u32[]{:S(2)}, u32[]{:S(2)}) collective-permute-start(f32[448,128]{1,0:T(8,128)S(1)} %pad_maximum_fusion.1), channel_id=1, source_target_pairs={{0,4},{4,0},{1,5},{5,1},{2,6},{6,2},{3,7},{7,3},{8,12},{12,8},{9,1... | collective-permute-start | bytes 688136 | tf_op jit(solution)/shard_map/ppermute | solution.py:569
  89.8 1.4 %shard_map.83 = f32[864,128]{1,0:T(8,128)} custom-call(s32[8]{0:T(128)S(1)} %iota_xor_fusion.me_ref, f32[112,128]{1,0:T(8,128)S(1)} %add.56.one_ref, f32[112,128]{1,0:T(8,128)S(1)} %collective-permute-done.20.two_ref, f32[224,128]{1,0:T(8,128)S(1)} %collective-permute-done.21.four_ref, f32[448,128]{1,0:T(8,128)S(1)} %collective-permute-done.22.eight_ref), custom_call_target="tpu_custom_call" | custom-call | bytes 1048576 | tf_op jit(solution)/shard_map/pallas_call | solution.py:627
  (88 shorter events, 14.2 us)
Async XLA Ops:
  1.6 6.0 %copy-start = (bf16[27,32,128]{2,1,0:T(8,128)(2,1)S(1)}, bf16[27,32,128]{2,1,0:T(8,128)(2,1)}, u32[]{:S(2)}) copy-start(bf16[27,32,128]{2,1,0:T(8,128)(2,1)} %weight_ref.1) | copy-start | bytes 663556
  1.7 8.2 %collective-permute-start = (bf16[512,128]{1,0:T(8,128)(2,1)S(1)}, bf16[512,128]{1,0:T(8,128)(2,1)S(1)}, u32[]{:S(2)}, u32[]{:S(2)}) collective-permute-start(bf16[512,128]{1,0:T(8,128)(2,1)S(1)} %bitcast.26), channel_id=1, source_target_pairs={{0,1},{1,2},{2,3},{3,0},{4,5},{5,6},{6,7},{7,4},{8,9},{9,10},{10,1... | collective-permute-start | bytes 393224 | tf_op jit(solution)/shard_map/ppermute | solution.py:564
  3.9 8.3 %collective-permute-start.1 = (bf16[512,128]{1,0:T(8,128)(2,1)S(1)}, bf16[512,128]{1,0:T(8,128)(2,1)S(1)}, u32[]{:S(2)}, u32[]{:S(2)}) collective-permute-start(bf16[512,128]{1,0:T(8,128)(2,1)S(1)} %bitcast.27), channel_id=1, source_target_pairs={{0,2},{1,3},{2,0},{3,1},{4,6},{5,7},{6,4},{7,5},{8,10},{9,11},{10,... | collective-permute-start | bytes 393224 | tf_op jit(solution)/shard_map/ppermute | solution.py:564
  6.5 5.7 %collective-permute-start.2 = (bf16[512,128]{1,0:T(8,128)(2,1)S(1)}, bf16[512,128]{1,0:T(8,128)(2,1)S(1)}, u32[]{:S(2)}, u32[]{:S(2)}) collective-permute-start(bf16[512,128]{1,0:T(8,128)(2,1)S(1)} %bitcast.28), channel_id=1, source_target_pairs={{0,3},{1,0},{2,1},{3,2},{4,7},{5,4},{6,5},{7,6},{8,11},{9,8},{10,9... | collective-permute-start | bytes 393224 | tf_op jit(solution)/shard_map/ppermute | solution.py:564
  7.7 20.5 %collective-permute-start.3 = (bf16[1376,128]{1,0:T(8,128)(2,1)S(1)}, bf16[1376,128]{1,0:T(8,128)(2,1)S(1)}, u32[]{:S(2)}, u32[]{:S(2)}) collective-permute-start(bf16[1376,128]{1,0:T(8,128)(2,1)S(1)} %pad_maximum_fusion.w0_ref), channel_id=1, source_target_pairs={{0,1},{1,2},{2,3},{3,0},{4,5},{5,6},{6,7},{7,4},{8,9},{9,10},{10,1... | collective-permute-start | bytes 1056776 | tf_op jit(solution)/shard_map/ppermute | solution.py:564
  8.2 20.0 %collective-permute-start.4 = (bf16[1376,128]{1,0:T(8,128)(2,1)S(1)}, bf16[1376,128]{1,0:T(8,128)(2,1)S(1)}, u32[]{:S(2)}, u32[]{:S(2)}) collective-permute-start(bf16[1376,128]{1,0:T(8,128)(2,1)S(1)} %pad_maximum_fusion.w0_ref), channel_id=1, source_target_pairs={{0,2},{1,3},{2,0},{3,1},{4,6},{5,7},{6,4},{7,5},{8,10},{9,11},{10,... | collective-permute-start | bytes 1056776 | tf_op jit(solution)/shard_map/ppermute | solution.py:564
  9.9 18.3 %collective-permute-start.5 = (bf16[1376,128]{1,0:T(8,128)(2,1)S(1)}, bf16[1376,128]{1,0:T(8,128)(2,1)S(1)}, u32[]{:S(2)}, u32[]{:S(2)}) collective-permute-start(bf16[1376,128]{1,0:T(8,128)(2,1)S(1)} %pad_maximum_fusion.w0_ref), channel_id=1, source_target_pairs={{0,3},{1,0},{2,1},{3,2},{4,7},{5,4},{6,5},{7,6},{8,11},{9,8},{10,9... | collective-permute-start | bytes 1056776 | tf_op jit(solution)/shard_map/ppermute | solution.py:564
  12.4 6.3 %collective-permute-start.6 = (bf16[272,128]{1,0:T(8,128)(2,1)S(1)}, bf16[272,128]{1,0:T(8,128)(2,1)S(1)}, u32[]{:S(2)}, u32[]{:S(2)}) collective-permute-start(bf16[272,128]{1,0:T(8,128)(2,1)S(1)} %get-tuple-element.29), channel_id=1, source_target_pairs={{0,4},{4,0},{1,5},{5,1},{2,6},{6,2},{3,7},{7,3},{8,12},{12,8},{9,1... | collective-permute-start | bytes 208904 | tf_op jit(solution)/shard_map/ppermute | solution.py:114
  15.3 5.9 %collective-permute-start.7 = (bf16[272,128]{1,0:T(8,128)(2,1)S(1)}, bf16[272,128]{1,0:T(8,128)(2,1)S(1)}, u32[]{:S(2)}, u32[]{:S(2)}) collective-permute-start(bf16[272,128]{1,0:T(8,128)(2,1)S(1)} %get-tuple-element.30), channel_id=1, source_target_pairs={{4,8},{20,24},{36,40},{52,56},{68,72},{84,88},{100,104},{116,120},... | collective-permute-start | bytes 208904 | tf_op jit(solution)/shard_map/ppermute | solution.py:113
  21.3 12.8 %collective-permute-start.9 = (bf16[368,128]{1,0:T(8,128)(2,1)S(1)}, bf16[368,128]{1,0:T(8,128)(2,1)S(1)}, u32[]{:S(2)}, u32[]{:S(2)}) collective-permute-start(bf16[368,128]{1,0:T(8,128)(2,1)S(1)} %constant_dynamic-update-slice_fusion.9), channel_id=1, source_target_pairs={{16,0},{20,4},{24,8},{28,12},{32,16},{36,20},{40,24},{44,28},{48,3... | collective-permute-start | bytes 282632 | tf_op jit(solution)/shard_map/ppermute | solution.py:36
  22.6 11.5 %collective-permute-start.8 = (bf16[368,128]{1,0:T(8,128)(2,1)S(1)}, bf16[368,128]{1,0:T(8,128)(2,1)S(1)}, u32[]{:S(2)}, u32[]{:S(2)}) collective-permute-start(bf16[368,128]{1,0:T(8,128)(2,1)S(1)} %constant_dynamic-update-slice_fusion), channel_id=1, source_target_pairs={{0,16},{4,20},{8,24},{12,28},{16,32},{20,36},{24,40},{28,44},{32,4... | collective-permute-start | bytes 282632 | tf_op jit(solution)/shard_map/ppermute | solution.py:36
  38.2 9.4 %collective-permute-start.14 = (f32[448,128]{1,0:T(8,128)S(1)}, f32[448,128]{1,0:T(8,128)S(1)}, u32[]{:S(2)}, u32[]{:S(2)}) collective-permute-start(f32[448,128]{1,0:T(8,128)S(1)} %get-tuple-element.41), channel_id=1, source_target_pairs={{0,4},{4,0},{1,5},{5,1},{2,6},{6,2},{3,7},{7,3},{8,12},{12,8},{9,1... | collective-permute-start | bytes 688136 | tf_op jit(solution)/shard_map/ppermute | solution.py:569
  39.5 8.0 %collective-permute-start.10 = (bf16[272,128]{1,0:T(8,128)(2,1)S(1)}, bf16[272,128]{1,0:T(8,128)(2,1)S(1)}, u32[]{:S(2)}, u32[]{:S(2)}) collective-permute-start(bf16[272,128]{1,0:T(8,128)(2,1)S(1)} %get-tuple-element.36), channel_id=1, source_target_pairs={{0,4},{4,0},{1,5},{5,1},{2,6},{6,2},{3,7},{7,3},{8,12},{12,8},{9,1... | collective-permute-start | bytes 208904 | tf_op jit(solution)/shard_map/ppermute | solution.py:114
  39.6 7.9 %collective-permute-start.11 = (bf16[272,128]{1,0:T(8,128)(2,1)S(1)}, bf16[272,128]{1,0:T(8,128)(2,1)S(1)}, u32[]{:S(2)}, u32[]{:S(2)}) collective-permute-start(bf16[272,128]{1,0:T(8,128)(2,1)S(1)} %get-tuple-element.37), channel_id=1, source_target_pairs={{4,8},{20,24},{36,40},{52,56},{68,72},{84,88},{100,104},{116,120},... | collective-permute-start | bytes 208904 | tf_op jit(solution)/shard_map/ppermute | solution.py:113
  47.7 9.2 %collective-permute-start.15 = (f32[224,128]{1,0:T(8,128)S(1)}, f32[224,128]{1,0:T(8,128)S(1)}, u32[]{:S(2)}, u32[]{:S(2)}) collective-permute-start(f32[224,128]{1,0:T(8,128)S(1)} %dynamic-slice_bitcast_fusion), channel_id=1, source_target_pairs={{0,192},{64,128},{128,64},{192,0},{1,193},{65,129},{129,65},{193,1... | collective-permute-start | bytes 344072 | tf_op jit(solution)/shard_map/ppermute | solution.py:569
  54.6 11.2 %collective-permute-start.13 = (bf16[368,128]{1,0:T(8,128)(2,1)S(1)}, bf16[368,128]{1,0:T(8,128)(2,1)S(1)}, u32[]{:S(2)}, u32[]{:S(2)}) collective-permute-start(bf16[368,128]{1,0:T(8,128)(2,1)S(1)} %constant_dynamic-update-slice_fusion.29), channel_id=1, source_target_pairs={{16,0},{20,4},{24,8},{28,12},{32,16},{36,20},{40,24},{44,28},{48,3... | collective-permute-start | bytes 282632 | tf_op jit(solution)/shard_map/ppermute | solution.py:36
  56.9 4.1 %collective-permute-start.16 = (f32[112,128]{1,0:T(8,128)S(1)}, f32[112,128]{1,0:T(8,128)S(1)}, u32[]{:S(2)}, u32[]{:S(2)}) collective-permute-start(f32[112,128]{1,0:T(8,128)S(1)} %dynamic-slice_bitcast_fusion.1), channel_id=1, source_target_pairs={{0,64},{64,0},{128,192},{192,128},{1,65},{65,1},{129,193},{193,129... | collective-permute-start | bytes 172040 | tf_op jit(solution)/shard_map/ppermute | solution.py:569
  58.8 7.1 %collective-permute-start.12 = (bf16[368,128]{1,0:T(8,128)(2,1)S(1)}, bf16[368,128]{1,0:T(8,128)(2,1)S(1)}, u32[]{:S(2)}, u32[]{:S(2)}) collective-permute-start(bf16[368,128]{1,0:T(8,128)(2,1)S(1)} %constant_dynamic-update-slice_fusion.20), channel_id=1, source_target_pairs={{0,16},{4,20},{8,24},{12,28},{16,32},{20,36},{24,40},{28,44},{32,4... | collective-permute-start | bytes 282632 | tf_op jit(solution)/shard_map/ppermute | solution.py:36
  61.0 3.8 %collective-permute-start.17 = (f32[112,128]{1,0:T(8,128)S(1)}, f32[112,128]{1,0:T(8,128)S(1)}, u32[]{:S(2)}, u32[]{:S(2)}) collective-permute-start(f32[112,128]{1,0:T(8,128)S(1)} %bitcast_add_fusion.1), channel_id=1, source_target_pairs={{0,8},{8,0},{16,24},{24,16},{32,40},{40,32},{48,56},{56,48},{1,9},... | collective-permute-start | bytes 172040 | tf_op jit(solution)/shard_map/ppermute | solution.py:569
  64.9 4.0 %collective-permute-start.18 = (f32[112,128]{1,0:T(8,128)S(1)}, f32[112,128]{1,0:T(8,128)S(1)}, u32[]{:S(2)}, u32[]{:S(2)}) collective-permute-start(f32[112,128]{1,0:T(8,128)S(1)} %add.54), channel_id=1, source_target_pairs={{0,16},{8,24},{16,0},{24,8},{32,48},{40,56},{48,32},{56,40},{1,17}... | collective-permute-start | bytes 172040 | tf_op jit(solution)/shard_map/ppermute | solution.py:569
  68.9 5.5 %collective-permute-start.19 = (f32[112,128]{1,0:T(8,128)S(1)}, f32[112,128]{1,0:T(8,128)S(1)}, u32[]{:S(2)}, u32[]{:S(2)}) collective-permute-start(f32[112,128]{1,0:T(8,128)S(1)} %add.55), channel_id=1, source_target_pairs={{0,48},{8,56},{16,32},{24,40},{32,16},{40,24},{48,0},{56,8},{1,49}... | collective-permute-start | bytes 172040 | tf_op jit(solution)/shard_map/ppermute | solution.py:569
  74.3 3.1 %collective-permute-start.20 = (f32[112,128]{1,0:T(8,128)S(1)}, f32[112,128]{1,0:T(8,128)S(1)}, u32[]{:S(2)}, u32[]{:S(2)}) collective-permute-start(f32[112,128]{1,0:T(8,128)S(1)} %add.56.one_ref), channel_id=1, source_target_pairs={{0,64},{64,0},{128,192},{192,128},{1,65},{65,1},{129,193},{193,129... | collective-permute-start | bytes 172040 | tf_op jit(solution)/shard_map/ppermute | solution.py:569
  77.5 4.9 %collective-permute-start.21 = (f32[224,128]{1,0:T(8,128)S(1)}, f32[224,128]{1,0:T(8,128)S(1)}, u32[]{:S(2)}, u32[]{:S(2)}) collective-permute-start(f32[224,128]{1,0:T(8,128)S(1)} %pad_maximum_fusion.2), channel_id=1, source_target_pairs={{0,192},{64,128},{128,64},{192,0},{1,193},{65,129},{129,65},{193,1... | collective-permute-start | bytes 344072 | tf_op jit(solution)/shard_map/ppermute | solution.py:569
  82.4 7.3 %collective-permute-start.22 = (f32[448,128]{1,0:T(8,128)S(1)}, f32[448,128]{1,0:T(8,128)S(1)}, u32[]{:S(2)}, u32[]{:S(2)}) collective-permute-start(f32[448,128]{1,0:T(8,128)S(1)} %pad_maximum_fusion.1), channel_id=1, source_target_pairs={{0,4},{4,0},{1,5},{5,1},{2,6},{6,2},{3,7},{7,3},{8,12},{12,8},{9,1... | collective-permute-start | bytes 688136 | tf_op jit(solution)/shard_map/ppermute | solution.py:569
  (3 other events, 7.3 us)

commit v4 on v3

--- a/solution.py
+++ b/solution.py
@@ -66,7 +66,7 @@
         out_shape=[jax.ShapeDtypeStruct((BR, 64, 8, CH), F32)] + [face] * 4,
         in_specs=[SMEM] + [VMEM] * 5,
         out_specs=[VMEM] * 5,
-        compiler_params=params(6),
+        compiler_params=params(4),
         cost_estimate=cost(0, 2**22),
     )(core, *blocks, table)
 
@@ -84,7 +84,7 @@
         out_shape=jax.ShapeDtypeStruct((9 * CH, CH), BF16),
         in_specs=[VMEM],
         out_specs=VMEM,
-        compiler_params=params(4),
+        compiler_params=params(2),
         cost_estimate=cost(0, 2**20),
     )(weight)
 
@@ -147,6 +147,9 @@
     return jnp.clip(found, 0, ZERO)
 
 
+P_HIGH, P_LOW, Q_HIGH, Q_LOW = range(4)
+
+
 def fill_pool(core, pool, tiles_ref, halo_refs):
     side_m, side_n, left, right = halo_refs
     q_m, q_n = 7 * core, 7 * (1 - core)
@@ -154,31 +157,37 @@
     def plane(ref, start):
         return ref[start : start + 64].astype(F32).reshape(8, 8, CH)
 
+    for m in range(4):
+        pool[m, ZERO] = jnp.zeros((8, 8, CH), F32)
     for b in range(BR):
-        for first in range(0, 64, 8):
-            pool[b, first : first + 8] = tiles_ref[b, first : first + 8]
-            pool[ZERO, first : first + 8] = jnp.zeros((8, 8, CH), F32)
+        pool[P_HIGH, b] = tiles_ref[b, 56:64]
+        pool[P_LOW, b] = tiles_ref[b, 0:8]
+        for p in range(8):
+            pool[Q_HIGH, b, p] = tiles_ref[b, 8 * p + 7]
+            pool[Q_LOW, b, p] = tiles_ref[b, 8 * p]
         for ref, side, q in ((side_m, SIDE_M, q_m), (side_n, SIDE_N, q_n)):
             rows = plane(ref, 64 * b)
-            for p in range(8):
-                pool[side + b, 8 * p + q] = rows[p]
-        pool[SIDE_L + b, 56:64] = plane(left, 64 * b)
-        pool[SIDE_R + b, 0:8] = plane(right, 64 * b)
-    for ref, sides, p in ((left, (SIDE_LM, SIDE_LN), 7), (right, (SIDE_RM, SIDE_RN), 0)):
+            pool[Q_HIGH, side + b] = rows
+            pool[Q_LOW, side + b] = rows
+            pool[P_HIGH, side + b, q] = rows[7]
+            pool[P_LOW, side + b, q] = rows[0]
+        pool[P_HIGH, SIDE_L + b] = plane(left, 64 * b)
+        pool[P_LOW, SIDE_R + b] = plane(right, 64 * b)
+    for ref, sides, m in ((left, (SIDE_LM, SIDE_LN), P_HIGH), (right, (SIDE_RM, SIDE_RN), P_LOW)):
         for side, q, start in ((sides[0], q_m, 272), (sides[1], q_n, 320)):
             rows = ref[start : start + 32].astype(F32).reshape(BR, 8, CH)
             for b in range(BR):
-                pool[side + b, 8 * p + q] = rows[b]
-
-
-def three_shifts(entries, pool, p, q):
+                pool[m, side + b, q] = rows[b]
+
+
+def three_shifts(entries, tile):
     row = lax.broadcasted_iota(jnp.int32, (8, CH), 0)
     first, last = row == 0, row == 7
     shifts = ([], [], [])
     for b in range(BR):
-        below = pool[entries[b][0], 8 * p + q]
-        centre = pool[entries[b][1], 8 * p + q]
-        above = pool[entries[b][2], 8 * p + q]
+        below = tile(entries[b][0])
+        centre = tile(entries[b][1])
+        above = tile(entries[b][2])
         shifts[0].append(pltpu.roll(jnp.where(last, below, centre), 1, 0))
         shifts[1].append(centre)
         shifts[2].append(pltpu.roll(jnp.where(first, above, centre), 7, 0))
@@ -203,7 +212,7 @@
 
     def body(p, carry):
         for q in range(8):
-            for k, rows in enumerate(three_shifts(entries, zero, p, q)):
+            for k, rows in enumerate(three_shifts(entries, lambda e: zero[e, 8 * p + q])):
                 windows[k, p + 1, q + 1] = rows
         return carry
 
@@ -218,16 +227,17 @@
                 continue
             start = 9 * (ox + 1) + 3 * (oy + 1)
             entries = [[index_ref[b, start + k] for k in range(3)] for b in range(BR)]
-            for i in range(8):
-                p = i if ox == 0 else (7 if ox < 0 else 0)
-                q = i if oy == 0 else (7 if oy < 0 else 0)
-                for k, rows in enumerate(three_shifts(entries, pool, p, q)):
+            if ox == 0:
+                m = Q_HIGH if oy < 0 else Q_LOW
+            else:
+                m = P_HIGH if ox < 0 else P_LOW
+            corner = ox != 0 and oy != 0
+            for i in ((7 if oy < 0 else 0),) if corner else range(8):
+                for k, rows in enumerate(three_shifts(entries, lambda e: pool[m, e, i])):
                     if ox == 0:
-                        strips[(oy + 1) // 2, k, p + 1] = rows
+                        strips[(oy + 1) // 2, k, i + 1] = rows
                     else:
-                        ends[(ox + 1) // 2, k, q + 1 if oy == 0 else (0 if oy < 0 else 9)] = rows
-                if ox != 0 and oy != 0:
-                    break
+                        ends[(ox + 1) // 2, k, i + 1 if not corner else (0 if oy < 0 else 9)] = rows
     for side in range(2):
         for k in range(3):
             strips[side, k, 0] = blank
@@ -317,7 +327,7 @@
             pltpu.VMEM((10, 8, 32, CH), F32),
             pltpu.VMEM((CH, BR * VOX), F32),
         ],
-        compiler_params=params(20),
+        compiler_params=params(13),
         cost_estimate=cost(2 * 27 * CH * CH * 2048, 2**24),
     )(neighbours, chan, tiles, *blocks)
 
@@ -422,7 +432,7 @@
         out_specs=[VMEM] * 9,
         scratch_shapes=[
             pltpu.SMEM((8, CH), jnp.int32),
-            pltpu.VMEM((40, 64, 8, CH), F32),
+            pltpu.VMEM((4, 40, 8, 8, CH), F32),
             pltpu.VMEM((2, 3, 10, 32, CH), BF16),
             pltpu.VMEM((2, 3, 10, 32, CH), BF16),
             pltpu.VMEM((8, 8, 32, CH), F32),
@@ -430,7 +440,7 @@
             pltpu.VMEM((8, CH, 256), BF16),
             pltpu.VMEM((896, CH), F32),
         ],
-        compiler_params=params(28),
+        compiler_params=params(18),
         cost_estimate=cost(2 * 27 * CH * CH * 1024, 2**24),
     )(core, entries, tiles, cot, hidden, narrow, *halo, *weights)
 
@@ -462,7 +472,7 @@
             pltpu.VMEM((3, 10, 10, 32, CH), BF16),
             pltpu.VMEM((10, 256, CH), F32),
         ],
-        compiler_params=params(14),
+        compiler_params=params(8),
         cost_estimate=cost(2 * 27 * CH * CH * 1024, 2**23),
     )(neighbours, tiles, turned)
 
@@ -482,7 +492,7 @@
         in_specs=[SMEM] + [VMEM] * 2,
         out_specs=VMEM,
         scratch_shapes=[pltpu.VMEM((16, CH, CH), F32)],
-        compiler_params=params(6),
+        compiler_params=params(4),
         cost_estimate=cost(0, 2**22),
     )(chan, gated, features)
 
@@ -547,12 +557,12 @@
         out_specs=VMEM,
         scratch_shapes=[
             pltpu.SMEM((8, CH), jnp.int32),
-            pltpu.VMEM((40, 64, 8, CH), F32),
+            pltpu.VMEM((4, 40, 8, 8, CH), F32),
             pltpu.VMEM((2, 3, 10, 32, CH), BF16),
             pltpu.VMEM((2, 3, 10, 32, CH), BF16),
             pltpu.VMEM((8, 8, 32, CH), F32),
         ],
-        compiler_params=params(20),
+        compiler_params=params(12),
         cost_estimate=cost(2 * 27 * CH * CH * 512, 2**23),
     )(core, index, tiles, *halo, turned, part, cotangent)
 
@@ -569,15 +579,8 @@
     return lax.ppermute(value, axis, list(enumerate(partner)))
 
 
-X_NEAR, X_FAR = (1, 0, 3, 2), (3, 2, 1, 0)
+X_PARTNERS = ((1, 0, 3, 2), (3, 2, 1, 0), (2, 3, 0, 1))
 Z_PAIRS = ((1, 0, 3, 2, 5, 4, 7, 6), (2, 3, 0, 1, 6, 7, 4, 5), (6, 7, 4, 5, 2, 3, 0, 1))
-
-
-def halve(value, bit, partner):
-    halves = value.reshape(2, value.shape[0] // 2, CH)
-    keep = lax.dynamic_index_in_dim(halves, bit, 0, keepdims=False)
-    send = lax.dynamic_index_in_dim(halves, 1 - bit, 0, keepdims=False)
-    return keep + swapped(send, "x", partner)
 
 
 def place_kernel(me_ref, one_ref, two_ref, four_ref, eight_ref, out_ref):
@@ -606,30 +609,38 @@
     return lax.optimization_barrier((value,) + others)[0]
 
 
-def reduce_space(keep, send, beside):
+def reduce_space(keep, send, work):
     x = lax.axis_index("x")
     core = lax.axis_index("core")
-    high = x // 2
-    low = (x ^ (x // 2)) & 1
+    label = x ^ (x // 2)
+
+    def beside(step, value, got):
+        return after(got, *work[step](value)) if step in work else got
+
+    def halve(value, bit, partner):
+        halves = value.reshape(2, value.shape[0] // 2, CH)
+        kept = lax.dynamic_index_in_dim(halves, bit, 0, keepdims=False)
+        sent = lax.dynamic_index_in_dim(halves, 1 - bit, 0, keepdims=False)
+        return kept + swapped(sent, "x", partner)
+
     value = keep + swapped(send, "core", (1, 0))
-    value = halve(value, high, X_FAR)
-    value = halve(after(value, *beside[0]), low, X_NEAR)
+    value = halve(value, label // 2, X_PARTNERS[1])
+    value = halve(value, label % 2, X_PARTNERS[0])
     for step, partner in enumerate(Z_PAIRS):
-        value = after(value, *beside[step + 1])
-        value = value + swapped(value, "z", partner)
-    value = after(value, *beside[4])
-    two = swapped(value, "x", X_NEAR)
-    pair = jnp.concatenate([value, two], axis=0)
-    four = swapped(pair, "x", X_FAR)
-    quad = jnp.concatenate([pair, four], axis=0)
+        value = value + beside(step, value, swapped(value, "z", partner))
+    others = [swapped(value, "x", partner) for partner in X_PARTNERS]
+    others[0] = beside(3, value, others[0])
+    quad = jnp.concatenate([value] + others, axis=0)
     eight = swapped(quad, "core", (1, 0))
-    me = 4 * core + 2 * high + low
+    me = 4 * core + label
+    two = others[0]
+    four = jnp.concatenate(others[1:], axis=0)
     return pl.pallas_call(
         place_kernel,
         out_shape=jax.ShapeDtypeStruct((864, CH), F32),
         in_specs=[SMEM] + [VMEM] * 4,
         out_specs=VMEM,
-        compiler_params=params(4),
+        compiler_params=params(3),
         cost_estimate=cost(0, 2**20),
     )(me ^ jnp.arange(8, dtype=jnp.int32), value, two, four, eight)
 
@@ -661,11 +672,25 @@
     gated, grads, *rest = gate(core, entries, tiles, cot, hidden, narrow, halo, blocks)
     grad_faces, keep, send, index = rest[:4], rest[4], rest[5], rest[6]
     grad_halo = exchange(grad_faces)
-    part = back_inner(neighbours, grads, turned)
-    out = output_of(chan, gated, feat_own)
-    grad_input = back_margin(core, index, grads, grad_halo, turned, part, cot_own)
-    grad_weight = reduce_space(keep, send, ((part,), (out,), (), (grad_input,), ()))
-    return (from_rows(out), from_rows(grad_input), grad_weight.reshape(TAPS, OWN, CH))
+    made = {}
+
+    def inner_part(value):
+        made["part"] = back_inner(after(neighbours, value[:8]), grads, turned)
+        return (made["part"],)
+
+    def margin_part(value):
+        here = after(core, value[:8])
+        made["grad"] = from_rows(back_margin(here, index, grads, grad_halo, turned, made["part"], cot_own))
+        return (made["grad"],)
+
+    def output_part(value):
+        made["out"] = from_rows(output_of(after(chan, value[:8]), gated, feat_own))
+        return (made["out"],)
+
+    work = {0: inner_part, 2: margin_part, 3: output_part}
+    grad_weight = reduce_space(keep, send, work)
+    out, grad_input = made["out"], made["grad"]
+    return (out, grad_input, grad_weight.reshape(TAPS, OWN, CH))
 
 
 def solution(mesh):

time: 91.5 us -> 89.5 us (0.978)
  waiting for transfers between devices: 15.8 us -> 13.1 us
    ppermute x9 -> x10, waiting for transfers between devices: 12.8 us -> 7.98 us  [swapped(): return lax.ppermute(value, axis, list(enumerate(partner)))]
    ppermute x2, waiting for transfers between devices: 2.48 us -> 5.11 us  [exchange(): side_n = lax.ppermute(face_n, SPACE, across)]
    ppermute x9 -> x10, starting transfers between devices: 23.3 us -> 24.9 us  [swapped(): return lax.ppermute(value, axis, list(enumerate(partner)))]
    ppermute x4, starting transfers between devices: 10.3 us -> 9.27 us  [shifted(): lax.ppermute(value, SPACE, [(i, i + steps) for i in range(first, last)])]
  transfers between devices with their start and end apart: 23 -> 24, of which waited for: 8 -> 7; matrix products, arithmetic and copies ran while one was open for 2% -> 2% of each run, Pallas kernels for 14% -> 14%
where the time goes in v4:
time: 89.5 us; the launch traced here: 89.2 us
  starting transfers between devices  52.8 us (59%)
  Pallas kernels  17.8 us (20%)
  waiting for transfers between devices  13.1 us (15%)
  local copies, waits for them, and re-layouts  4.26 us (5%)
  between operations  1.09 us (1%)
    ppermute x10, starting transfers between devices, swapped(): return lax.ppermute(value, axis, list(enumerate(partner)))  24.9 us
    ppermute x4, starting transfers between devices, shifted(): lax.ppermute(value, SPACE, [(i, i + steps) for i in range(first, last)])  9.27 us
    ppermute x6, starting transfers between devices, ring_gather(): lax.ppermute(value, axis, [(i, (i + step) % count) for i in range(count)])  8.94 us
    ppermute x10, waiting for transfers between devices, swapped(): return lax.ppermute(value, axis, list(enumerate(partner)))  7.98 us
    ppermute x2, starting transfers between devices, exchange(): side_n = lax.ppermute(face_n, SPACE, across)  6.2 us
    pallas_call x1, Pallas kernels, inner(): pl.pallas_call(inner_kernel, out_shape=[jax.ShapeDtypeStruct((8, 8, 32, C...  5.86 us
    ppermute x2, waiting for transfers between devices, exchange(): side_n = lax.ppermute(face_n, SPACE, across)  5.11 us
    pallas_call x1, Pallas kernels, back_inner(): pl.pallas_call(back_inner_kernel, out_shape=jax.ShapeDtypeStruct((8, 8, 3...  4.15 us
  transfers between devices with their start and end apart: 24, of which 7 were waited for; matrix products, arithmetic and copies ran while one was open for 2% of the time, Pallas kernels for 14%

profile of v4, /device:TPU:1, one launch (start us, length us, event | category | flops | bytes accessed | tf_op | source)
XLA Modules:
  0.0 89.2 jit_solution(6895317334429933790)
XLA Ops:
  1.7 2.2 %collective-permute-start = (bf16[512,128]{1,0:T(8,128)(2,1)S(1)}, bf16[512,128]{1,0:T(8,128)(2,1)S(1)}, u32[]{:S(2)}, u32[]{:S(2)}) collective-permute-start(bf16[512,128]{1,0:T(8,128)(2,1)S(1)} %bitcast.26), channel_id=1, source_target_pairs={{0,1},{1,2},{2,3},{3,0},{4,5},{5,6},{6,7},{7,4},{8,9},{9,10},{10,1... | collective-permute-start | bytes 393224 | tf_op jit(solution)/shard_map/ppermute | solution.py:574
  3.9 2.6 %collective-permute-start.1 = (bf16[512,128]{1,0:T(8,128)(2,1)S(1)}, bf16[512,128]{1,0:T(8,128)(2,1)S(1)}, u32[]{:S(2)}, u32[]{:S(2)}) collective-permute-start(bf16[512,128]{1,0:T(8,128)(2,1)S(1)} %bitcast.27), channel_id=1, source_target_pairs={{0,2},{1,3},{2,0},{3,1},{4,6},{5,7},{6,4},{7,5},{8,10},{9,11},{10,... | collective-permute-start | bytes 393224 | tf_op jit(solution)/shard_map/ppermute | solution.py:574
  10.6 1.8 %collective-permute-start.5 = (bf16[1376,128]{1,0:T(8,128)(2,1)S(1)}, bf16[1376,128]{1,0:T(8,128)(2,1)S(1)}, u32[]{:S(2)}, u32[]{:S(2)}) collective-permute-start(bf16[1376,128]{1,0:T(8,128)(2,1)S(1)} %pad_maximum_fusion.w0_ref), channel_id=1, source_target_pairs={{0,3},{1,0},{2,1},{3,2},{4,7},{5,4},{6,5},{7,6},{8,11},{9,8},{10,9... | collective-permute-start | bytes 1056776 | tf_op jit(solution)/shard_map/ppermute | solution.py:574
  12.6 3.4 %collective-permute-start.6 = (bf16[272,128]{1,0:T(8,128)(2,1)S(1)}, bf16[272,128]{1,0:T(8,128)(2,1)S(1)}, u32[]{:S(2)}, u32[]{:S(2)}) collective-permute-start(bf16[272,128]{1,0:T(8,128)(2,1)S(1)} %get-tuple-element.29), channel_id=1, source_target_pairs={{0,4},{4,0},{1,5},{5,1},{2,6},{6,2},{3,7},{7,3},{8,12},{12,8},{9,1... | collective-permute-start | bytes 208904 | tf_op jit(solution)/shard_map/ppermute | solution.py:114
  16.1 2.6 %collective-permute-start.7 = (bf16[272,128]{1,0:T(8,128)(2,1)S(1)}, bf16[272,128]{1,0:T(8,128)(2,1)S(1)}, u32[]{:S(2)}, u32[]{:S(2)}) collective-permute-start(bf16[272,128]{1,0:T(8,128)(2,1)S(1)} %get-tuple-element.30), channel_id=1, source_target_pairs={{4,8},{20,24},{36,40},{52,56},{68,72},{84,88},{100,104},{116,120},... | collective-permute-start | bytes 208904 | tf_op jit(solution)/shard_map/ppermute | solution.py:113
  18.8 3.2 %collective-permute-done.7.side_n_ref = bf16[272,128]{1,0:T(8,128)(2,1)S(1)} collective-permute-done((bf16[272,128]{1,0:T(8,128)(2,1)S(1)}, bf16[272,128]{1,0:T(8,128)(2,1)S(1)}, u32[]{:S(2)}, u32[]{:S(2)}) %collective-permute-start.7) | collective-permute-done | bytes 69664 | tf_op jit(solution)/shard_map/ppermute | solution.py:113
  23.3 4.9 %collective-permute-start.8 = (bf16[368,128]{1,0:T(8,128)(2,1)S(1)}, bf16[368,128]{1,0:T(8,128)(2,1)S(1)}, u32[]{:S(2)}, u32[]{:S(2)}) collective-permute-start(bf16[368,128]{1,0:T(8,128)(2,1)S(1)} %constant_dynamic-update-slice_fusion), channel_id=1, source_target_pairs={{0,16},{4,20},{8,24},{12,28},{16,32},{20,36},{24,40},{28,44},{32,4... | collective-permute-start | bytes 282632 | tf_op jit(solution)/shard_map/ppermute | solution.py:36
  28.2 5.9 %shard_map.78 = (f32[8,8,32,128]{3,2,1,0:T(8,128)S(1)}, bf16[8,8,32,128]{3,2,1,0:T(8,128)(2,1)S(1)}, f32[4,64,8,128]{3,2,1,0:T(8,128)S(1)}) custom-call(s32[4,27]{1,0:T(4,128)S(1)} %copy-done.1, s32[1]{0:T(128)} %bitcast.chan_ref, f32[4,64,8,128]{3,2,1,0:T(8,128)S(1)} %get-tuple-element.25.tiles_ref, bf16[1376,128]{1,0:T(8,128)(2,1)S(1)} %pad_maximum_fusion.w0_ref, ...), custom_call_target="tpu_custom_call" | custom-call | flops 1811939328 | bytes 16777216 | tf_op jit(solution)/shard_map/pallas_call | solution.py:314
  34.1 4.0 %shard_map.79 = (f32[4,64,8,128]{3,2,1,0:T(8,128)S(1)}, f32[4,64,8,128]{3,2,1,0:T(8,128)S(1)}, bf16[272,128]{1,0:T(8,128)(2,1)S(1)}, bf16[272,128]{1,0:T(8,128)(...) custom-call(s32[1]{0:T(128)} %bitcast.1.core_ref.place_ref, ...), custom_call_target="tpu_custom_call" | custom-call | flops 905969664 | bytes 16777216 | tf_op jit(solution)/shard_map/pallas_call | solution.py:428
  39.2 3.6 %collective-permute-start.11 = (bf16[272,128]{1,0:T(8,128)(2,1)S(1)}, bf16[272,128]{1,0:T(8,128)(2,1)S(1)}, u32[]{:S(2)}, u32[]{:S(2)}) collective-permute-start(bf16[272,128]{1,0:T(8,128)(2,1)S(1)} %get-tuple-element.37), channel_id=1, source_target_pairs={{4,8},{20,24},{36,40},{52,56},{68,72},{84,88},{100,104},{116,120},... | collective-permute-start | bytes 208904 | tf_op jit(solution)/shard_map/ppermute | solution.py:113
  42.8 1.9 %collective-permute-done.11.side_n_ref = bf16[272,128]{1,0:T(8,128)(2,1)S(1)} collective-permute-done((bf16[272,128]{1,0:T(8,128)(2,1)S(1)}, bf16[272,128]{1,0:T(8,128)(2,1)S(1)}, u32[]{:S(2)}, u32[]{:S(2)}) %collective-permute-start.11) | collective-permute-done | bytes 69664 | tf_op jit(solution)/shard_map/ppermute | solution.py:113
  44.9 7.1 %collective-permute-start.15 = (f32[224,128]{1,0:T(8,128)S(1)}, f32[224,128]{1,0:T(8,128)S(1)}, u32[]{:S(2)}, u32[]{:S(2)}) collective-permute-start(f32[224,128]{1,0:T(8,128)S(1)} %dynamic-slice_bitcast_fusion), channel_id=1, source_target_pairs={{0,192},{64,128},{128,64},{192,0},{1,193},{65,129},{129,65},{193,1... | collective-permute-start | bytes 344072 | tf_op jit(solution)/shard_map/ppermute | solution.py:579
  54.1 2.3 %collective-permute-start.16 = (f32[112,128]{1,0:T(8,128)S(1)}, f32[112,128]{1,0:T(8,128)S(1)}, u32[]{:S(2)}, u32[]{:S(2)}) collective-permute-start(f32[112,128]{1,0:T(8,128)S(1)} %dynamic-slice_bitcast_fusion.1), channel_id=1, source_target_pairs={{0,64},{64,0},{128,192},{192,128},{1,65},{65,1},{129,193},{193,129... | collective-permute-start | bytes 172040 | tf_op jit(solution)/shard_map/ppermute | solution.py:579
  56.5 1.8 %collective-permute-start.12 = (bf16[368,128]{1,0:T(8,128)(2,1)S(1)}, bf16[368,128]{1,0:T(8,128)(2,1)S(1)}, u32[]{:S(2)}, u32[]{:S(2)}) collective-permute-start(bf16[368,128]{1,0:T(8,128)(2,1)S(1)} %constant_dynamic-update-slice_fusion.20), channel_id=1, source_target_pairs={{0,16},{4,20},{8,24},{12,28},{16,32},{20,36},{24,40},{28,44},{32,4... | collective-permute-start | bytes 282632 | tf_op jit(solution)/shard_map/ppermute | solution.py:36
  58.6 4.2 %shard_map.81.part_ref = f32[8,8,32,128]{3,2,1,0:T(8,128)S(1)} custom-call(s32[4,27]{1,0:T(4,128)S(1)} %copy-done.1, f32[4,64,8,128]{3,2,1,0:T(8,128)S(1)} %get-tuple-element.35.tiles_ref, bf16[1152,128]{1,0:T(8,128)(2,1)S(1)} %shard_map.76.turned_ref), custom_call_target="tpu_custom_call" | custom-call | flops 905969664 | bytes 8388608 | tf_op jit(solution)/shard_map/pallas_call | solution.py:465
  62.8 1.4 %collective-permute-start.18 = (f32[112,128]{1,0:T(8,128)S(1)}, f32[112,128]{1,0:T(8,128)S(1)}, u32[]{:S(2)}, u32[]{:S(2)}) collective-permute-start(f32[112,128]{1,0:T(8,128)S(1)} %add.56), channel_id=1, source_target_pairs={{0,16},{8,24},{16,0},{24,8},{32,48},{40,56},{48,32},{56,40},{1,17}... | collective-permute-start | bytes 172040 | tf_op jit(solution)/shard_map/ppermute | solution.py:579
  64.2 2.6 %collective-permute-done.18 = f32[112,128]{1,0:T(8,128)S(1)} collective-permute-done((f32[112,128]{1,0:T(8,128)S(1)}, f32[112,128]{1,0:T(8,128)S(1)}, u32[]{:S(2)}, u32[]{:S(2)}) %collective-permute-start.18) | collective-permute-done | bytes 57376 | tf_op jit(solution)/shard_map/ppermute | solution.py:579
  66.8 3.5 %collective-permute-start.19 = (f32[112,128]{1,0:T(8,128)S(1)}, f32[112,128]{1,0:T(8,128)S(1)}, u32[]{:S(2)}, u32[]{:S(2)}) collective-permute-start(f32[112,128]{1,0:T(8,128)S(1)} %add.57), channel_id=1, source_target_pairs={{0,48},{8,56},{16,32},{24,40},{32,16},{40,24},{48,0},{56,8},{1,49}... | collective-permute-start | bytes 172040 | tf_op jit(solution)/shard_map/ppermute | solution.py:579
  70.3 1.6 %shard_map.82 = bf16[512,128]{1,0:T(8,128)(2,1)S(1)} custom-call(s32[1]{0:T(128)} %bitcast.1.core_ref.place_ref, s32[8,128]{1,0:T(8,128)S(1)} %get-tuple-element.34.index_in_ref, f32[4,64,8,128]{3,2,1,0:T(8,128)S(1)} %get-tuple-element.35.tiles_ref, bf16[272,128]{1,0:T(8,128)(2,1)S(1)} %collective-permute-done.10.side_m_ref, ...), custom_call_target="tpu_custom_call" | custom-call | flops 452984832 | bytes 8388608 | tf_op jit(solution)/shard_map/pallas_call | solution.py:553
  72.8 1.6 %collective-permute-start.20 = (f32[112,128]{1,0:T(8,128)S(1)}, f32[112,128]{1,0:T(8,128)S(1)}, u32[]{:S(2)}, u32[]{:S(2)}) collective-permute-start(f32[112,128]{1,0:T(8,128)S(1)} %add.58.one_ref), channel_id=1, source_target_pairs={{0,64},{64,0},{128,192},{192,128},{1,65},{65,1},{129,193},{193,129... | collective-permute-start | bytes 172040 | tf_op jit(solution)/shard_map/ppermute | solution.py:579
  74.4 1.9 %collective-permute-start.21 = (f32[112,128]{1,0:T(8,128)S(1)}, f32[112,128]{1,0:T(8,128)S(1)}, u32[]{:S(2)}, u32[]{:S(2)}) collective-permute-start(f32[112,128]{1,0:T(8,128)S(1)} %add.58.one_ref), channel_id=1, source_target_pairs={{0,192},{64,128},{128,64},{192,0},{1,193},{65,129},{129,65},{193,1... | collective-permute-start | bytes 172040 | tf_op jit(solution)/shard_map/ppermute | solution.py:579
  78.7 2.2 %collective-permute-done.22 = f32[112,128]{1,0:T(8,128)S(1)} collective-permute-done((f32[112,128]{1,0:T(8,128)S(1)}, f32[112,128]{1,0:T(8,128)S(1)}, u32[]{:S(2)}, u32[]{:S(2)}) %collective-permute-start.22) | collective-permute-done | bytes 57376 | tf_op jit(solution)/shard_map/ppermute | solution.py:579
  80.9 5.8 %collective-permute-start.23 = (f32[448,128]{1,0:T(8,128)S(1)}, f32[448,128]{1,0:T(8,128)S(1)}, u32[]{:S(2)}, u32[]{:S(2)}) collective-permute-start(f32[448,128]{1,0:T(8,128)S(1)} %pad_maximum_fusion.1), channel_id=1, source_target_pairs={{0,4},{4,0},{1,5},{5,1},{2,6},{6,2},{3,7},{7,3},{8,12},{12,8},{9,1... | collective-permute-start | bytes 688136 | tf_op jit(solution)/shard_map/ppermute | solution.py:579
  87.8 1.4 %shard_map.83 = f32[864,128]{1,0:T(8,128)} custom-call(s32[8]{0:T(128)S(1)} %iota_xor_fusion.me_ref, f32[112,128]{1,0:T(8,128)S(1)} %add.58.one_ref, f32[112,128]{1,0:T(8,128)S(1)} %collective-permute-done.20.two_ref, f32[224,128]{1,0:T(8,128)S(1)} %pad_maximum_fusion.2.four_ref, f32[448,128]{1,0:T(8,128)S(1)} %collective-permute-done.23.eight_ref), custom_call_target="tpu_custom_call" | custom-call | bytes 1048576 | tf_op jit(solution)/shard_map/pallas_call | solution.py:638
  (90 shorter events, 14.6 us)
Async XLA Ops:
  1.7 8.9 %collective-permute-start = (bf16[512,128]{1,0:T(8,128)(2,1)S(1)}, bf16[512,128]{1,0:T(8,128)(2,1)S(1)}, u32[]{:S(2)}, u32[]{:S(2)}) collective-permute-start(bf16[512,128]{1,0:T(8,128)(2,1)S(1)} %bitcast.26), channel_id=1, source_target_pairs={{0,1},{1,2},{2,3},{3,0},{4,5},{5,6},{6,7},{7,4},{8,9},{9,10},{10,1... | collective-permute-start | bytes 393224 | tf_op jit(solution)/shard_map/ppermute | solution.py:574
  3.9 8.5 %collective-permute-start.1 = (bf16[512,128]{1,0:T(8,128)(2,1)S(1)}, bf16[512,128]{1,0:T(8,128)(2,1)S(1)}, u32[]{:S(2)}, u32[]{:S(2)}) collective-permute-start(bf16[512,128]{1,0:T(8,128)(2,1)S(1)} %bitcast.27), channel_id=1, source_target_pairs={{0,2},{1,3},{2,0},{3,1},{4,6},{5,7},{6,4},{7,5},{8,10},{9,11},{10,... | collective-permute-start | bytes 393224 | tf_op jit(solution)/shard_map/ppermute | solution.py:574
  6.5 5.9 %collective-permute-start.2 = (bf16[512,128]{1,0:T(8,128)(2,1)S(1)}, bf16[512,128]{1,0:T(8,128)(2,1)S(1)}, u32[]{:S(2)}, u32[]{:S(2)}) collective-permute-start(bf16[512,128]{1,0:T(8,128)(2,1)S(1)} %bitcast.28), channel_id=1, source_target_pairs={{0,3},{1,0},{2,1},{3,2},{4,7},{5,4},{6,5},{7,6},{8,11},{9,8},{10,9... | collective-permute-start | bytes 393224 | tf_op jit(solution)/shard_map/ppermute | solution.py:574
  7.7 20.5 %collective-permute-start.3 = (bf16[1376,128]{1,0:T(8,128)(2,1)S(1)}, bf16[1376,128]{1,0:T(8,128)(2,1)S(1)}, u32[]{:S(2)}, u32[]{:S(2)}) collective-permute-start(bf16[1376,128]{1,0:T(8,128)(2,1)S(1)} %pad_maximum_fusion.w0_ref), channel_id=1, source_target_pairs={{0,1},{1,2},{2,3},{3,0},{4,5},{5,6},{6,7},{7,4},{8,9},{9,10},{10,1... | collective-permute-start | bytes 1056776 | tf_op jit(solution)/shard_map/ppermute | solution.py:574
  8.2 20.1 %collective-permute-start.4 = (bf16[1376,128]{1,0:T(8,128)(2,1)S(1)}, bf16[1376,128]{1,0:T(8,128)(2,1)S(1)}, u32[]{:S(2)}, u32[]{:S(2)}) collective-permute-start(bf16[1376,128]{1,0:T(8,128)(2,1)S(1)} %pad_maximum_fusion.w0_ref), channel_id=1, source_target_pairs={{0,2},{1,3},{2,0},{3,1},{4,6},{5,7},{6,4},{7,5},{8,10},{9,11},{10,... | collective-permute-start | bytes 1056776 | tf_op jit(solution)/shard_map/ppermute | solution.py:574
  10.6 17.6 %collective-permute-start.5 = (bf16[1376,128]{1,0:T(8,128)(2,1)S(1)}, bf16[1376,128]{1,0:T(8,128)(2,1)S(1)}, u32[]{:S(2)}, u32[]{:S(2)}) collective-permute-start(bf16[1376,128]{1,0:T(8,128)(2,1)S(1)} %pad_maximum_fusion.w0_ref), channel_id=1, source_target_pairs={{0,3},{1,0},{2,1},{3,2},{4,7},{5,4},{6,5},{7,6},{8,11},{9,8},{10,9... | collective-permute-start | bytes 1056776 | tf_op jit(solution)/shard_map/ppermute | solution.py:574
  12.6 6.1 %collective-permute-start.6 = (bf16[272,128]{1,0:T(8,128)(2,1)S(1)}, bf16[272,128]{1,0:T(8,128)(2,1)S(1)}, u32[]{:S(2)}, u32[]{:S(2)}) collective-permute-start(bf16[272,128]{1,0:T(8,128)(2,1)S(1)} %get-tuple-element.29), channel_id=1, source_target_pairs={{0,4},{4,0},{1,5},{5,1},{2,6},{6,2},{3,7},{7,3},{8,12},{12,8},{9,1... | collective-permute-start | bytes 208904 | tf_op jit(solution)/shard_map/ppermute | solution.py:114
  16.1 5.9 %collective-permute-start.7 = (bf16[272,128]{1,0:T(8,128)(2,1)S(1)}, bf16[272,128]{1,0:T(8,128)(2,1)S(1)}, u32[]{:S(2)}, u32[]{:S(2)}) collective-permute-start(bf16[272,128]{1,0:T(8,128)(2,1)S(1)} %get-tuple-element.30), channel_id=1, source_target_pairs={{4,8},{20,24},{36,40},{52,56},{68,72},{84,88},{100,104},{116,120},... | collective-permute-start | bytes 208904 | tf_op jit(solution)/shard_map/ppermute | solution.py:113
  22.0 12.1 %collective-permute-start.9 = (bf16[368,128]{1,0:T(8,128)(2,1)S(1)}, bf16[368,128]{1,0:T(8,128)(2,1)S(1)}, u32[]{:S(2)}, u32[]{:S(2)}) collective-permute-start(bf16[368,128]{1,0:T(8,128)(2,1)S(1)} %constant_dynamic-update-slice_fusion.9), channel_id=1, source_target_pairs={{16,0},{20,4},{24,8},{28,12},{32,16},{36,20},{40,24},{44,28},{48,3... | collective-permute-start | bytes 282632 | tf_op jit(solution)/shard_map/ppermute | solution.py:36
  23.3 10.8 %collective-permute-start.8 = (bf16[368,128]{1,0:T(8,128)(2,1)S(1)}, bf16[368,128]{1,0:T(8,128)(2,1)S(1)}, u32[]{:S(2)}, u32[]{:S(2)}) collective-permute-start(bf16[368,128]{1,0:T(8,128)(2,1)S(1)} %constant_dynamic-update-slice_fusion), channel_id=1, source_target_pairs={{0,16},{4,20},{8,24},{12,28},{16,32},{20,36},{24,40},{28,44},{32,4... | collective-permute-start | bytes 282632 | tf_op jit(solution)/shard_map/ppermute | solution.py:36
  38.1 6.7 %collective-permute-start.14 = (f32[448,128]{1,0:T(8,128)S(1)}, f32[448,128]{1,0:T(8,128)S(1)}, u32[]{:S(2)}, u32[]{:S(2)}) collective-permute-start(f32[448,128]{1,0:T(8,128)S(1)} %get-tuple-element.41), channel_id=1, source_target_pairs={{0,4},{4,0},{1,5},{5,1},{2,6},{6,2},{3,7},{7,3},{8,12},{12,8},{9,1... | collective-permute-start | bytes 688136 | tf_op jit(solution)/shard_map/ppermute | solution.py:579
  39.0 3.7 %collective-permute-start.10 = (bf16[272,128]{1,0:T(8,128)(2,1)S(1)}, bf16[272,128]{1,0:T(8,128)(2,1)S(1)}, u32[]{:S(2)}, u32[]{:S(2)}) collective-permute-start(bf16[272,128]{1,0:T(8,128)(2,1)S(1)} %get-tuple-element.36), channel_id=1, source_target_pairs={{0,4},{4,0},{1,5},{5,1},{2,6},{6,2},{3,7},{7,3},{8,12},{12,8},{9,1... | collective-permute-start | bytes 208904 | tf_op jit(solution)/shard_map/ppermute | solution.py:114
  39.2 5.6 %collective-permute-start.11 = (bf16[272,128]{1,0:T(8,128)(2,1)S(1)}, bf16[272,128]{1,0:T(8,128)(2,1)S(1)}, u32[]{:S(2)}, u32[]{:S(2)}) collective-permute-start(bf16[272,128]{1,0:T(8,128)(2,1)S(1)} %get-tuple-element.37), channel_id=1, source_target_pairs={{4,8},{20,24},{36,40},{52,56},{68,72},{84,88},{100,104},{116,120},... | collective-permute-start | bytes 208904 | tf_op jit(solution)/shard_map/ppermute | solution.py:113
  44.9 9.2 %collective-permute-start.15 = (f32[224,128]{1,0:T(8,128)S(1)}, f32[224,128]{1,0:T(8,128)S(1)}, u32[]{:S(2)}, u32[]{:S(2)}) collective-permute-start(f32[224,128]{1,0:T(8,128)S(1)} %dynamic-slice_bitcast_fusion), channel_id=1, source_target_pairs={{0,192},{64,128},{128,64},{192,0},{1,193},{65,129},{129,65},{193,1... | collective-permute-start | bytes 344072 | tf_op jit(solution)/shard_map/ppermute | solution.py:579
  51.9 18.4 %collective-permute-start.13 = (bf16[368,128]{1,0:T(8,128)(2,1)S(1)}, bf16[368,128]{1,0:T(8,128)(2,1)S(1)}, u32[]{:S(2)}, u32[]{:S(2)}) collective-permute-start(bf16[368,128]{1,0:T(8,128)(2,1)S(1)} %constant_dynamic-update-slice_fusion.29), channel_id=1, source_target_pairs={{16,0},{20,4},{24,8},{28,12},{32,16},{36,20},{40,24},{44,28},{48,3... | collective-permute-start | bytes 282632 | tf_op jit(solution)/shard_map/ppermute | solution.py:36
  54.1 4.1 %collective-permute-start.16 = (f32[112,128]{1,0:T(8,128)S(1)}, f32[112,128]{1,0:T(8,128)S(1)}, u32[]{:S(2)}, u32[]{:S(2)}) collective-permute-start(f32[112,128]{1,0:T(8,128)S(1)} %dynamic-slice_bitcast_fusion.1), channel_id=1, source_target_pairs={{0,64},{64,0},{128,192},{192,128},{1,65},{65,1},{129,193},{193,129... | collective-permute-start | bytes 172040 | tf_op jit(solution)/shard_map/ppermute | solution.py:579
  56.5 13.9 %collective-permute-start.12 = (bf16[368,128]{1,0:T(8,128)(2,1)S(1)}, bf16[368,128]{1,0:T(8,128)(2,1)S(1)}, u32[]{:S(2)}, u32[]{:S(2)}) collective-permute-start(bf16[368,128]{1,0:T(8,128)(2,1)S(1)} %constant_dynamic-update-slice_fusion.20), channel_id=1, source_target_pairs={{0,16},{4,20},{8,24},{12,28},{16,32},{20,36},{24,40},{28,44},{32,4... | collective-permute-start | bytes 282632 | tf_op jit(solution)/shard_map/ppermute | solution.py:36
  58.3 4.4 %collective-permute-start.17 = (f32[112,128]{1,0:T(8,128)S(1)}, f32[112,128]{1,0:T(8,128)S(1)}, u32[]{:S(2)}, u32[]{:S(2)}) collective-permute-start(f32[112,128]{1,0:T(8,128)S(1)} %bitcast_add_fusion.1), channel_id=1, source_target_pairs={{0,8},{8,0},{16,24},{24,16},{32,40},{40,32},{48,56},{56,48},{1,9},... | collective-permute-start | bytes 172040 | tf_op jit(solution)/shard_map/ppermute | solution.py:579
  62.8 4.0 %collective-permute-start.18 = (f32[112,128]{1,0:T(8,128)S(1)}, f32[112,128]{1,0:T(8,128)S(1)}, u32[]{:S(2)}, u32[]{:S(2)}) collective-permute-start(f32[112,128]{1,0:T(8,128)S(1)} %add.56), channel_id=1, source_target_pairs={{0,16},{8,24},{16,0},{24,8},{32,48},{40,56},{48,32},{56,40},{1,17}... | collective-permute-start | bytes 172040 | tf_op jit(solution)/shard_map/ppermute | solution.py:579
  66.8 6.0 %collective-permute-start.19 = (f32[112,128]{1,0:T(8,128)S(1)}, f32[112,128]{1,0:T(8,128)S(1)}, u32[]{:S(2)}, u32[]{:S(2)}) collective-permute-start(f32[112,128]{1,0:T(8,128)S(1)} %add.57), channel_id=1, source_target_pairs={{0,48},{8,56},{16,32},{24,40},{32,16},{40,24},{48,0},{56,8},{1,49}... | collective-permute-start | bytes 172040 | tf_op jit(solution)/shard_map/ppermute | solution.py:579
  72.8 4.7 %collective-permute-start.20 = (f32[112,128]{1,0:T(8,128)S(1)}, f32[112,128]{1,0:T(8,128)S(1)}, u32[]{:S(2)}, u32[]{:S(2)}) collective-permute-start(f32[112,128]{1,0:T(8,128)S(1)} %add.58.one_ref), channel_id=1, source_target_pairs={{0,64},{64,0},{128,192},{192,128},{1,65},{65,1},{129,193},{193,129... | collective-permute-start | bytes 172040 | tf_op jit(solution)/shard_map/ppermute | solution.py:579
  74.4 4.2 %collective-permute-start.21 = (f32[112,128]{1,0:T(8,128)S(1)}, f32[112,128]{1,0:T(8,128)S(1)}, u32[]{:S(2)}, u32[]{:S(2)}) collective-permute-start(f32[112,128]{1,0:T(8,128)S(1)} %add.58.one_ref), channel_id=1, source_target_pairs={{0,192},{64,128},{128,64},{192,0},{1,193},{65,129},{129,65},{193,1... | collective-permute-start | bytes 172040 | tf_op jit(solution)/shard_map/ppermute | solution.py:579
  76.3 4.5 %collective-permute-start.22 = (f32[112,128]{1,0:T(8,128)S(1)}, f32[112,128]{1,0:T(8,128)S(1)}, u32[]{:S(2)}, u32[]{:S(2)}) collective-permute-start(f32[112,128]{1,0:T(8,128)S(1)} %add.58.one_ref), channel_id=1, source_target_pairs={{0,128},{64,192},{128,0},{192,64},{1,129},{65,193},{129,1},{193,65... | collective-permute-start | bytes 172040 | tf_op jit(solution)/shard_map/ppermute | solution.py:579
  80.9 6.9 %collective-permute-start.23 = (f32[448,128]{1,0:T(8,128)S(1)}, f32[448,128]{1,0:T(8,128)S(1)}, u32[]{:S(2)}, u32[]{:S(2)}) collective-permute-start(f32[448,128]{1,0:T(8,128)S(1)} %pad_maximum_fusion.1), channel_id=1, source_target_pairs={{0,4},{4,0},{1,5},{5,1},{2,6},{6,2},{3,7},{7,3},{8,12},{12,8},{9,1... | collective-permute-start | bytes 688136 | tf_op jit(solution)/shard_map/ppermute | solution.py:579
  (4 other events, 13.3 us)

commit v5 on v4

--- a/solution.py
+++ b/solution.py
@@ -580,7 +580,7 @@
 
 
 X_PARTNERS = ((1, 0, 3, 2), (3, 2, 1, 0), (2, 3, 0, 1))
-Z_PAIRS = ((1, 0, 3, 2, 5, 4, 7, 6), (2, 3, 0, 1, 6, 7, 4, 5), (6, 7, 4, 5, 2, 3, 0, 1))
+Z_PAIRS = tuple(tuple(i ^ mask for i in range(8)) for mask in (6, 1, 2))
 
 
 def place_kernel(me_ref, one_ref, two_ref, four_ref, eight_ref, out_ref):

time: 89.5 us -> 88.7 us (level)
  starting transfers between devices: 52.8 us -> 49.2 us
  waiting for transfers between devices: 13.1 us -> 15.8 us
    ppermute x10, starting transfers between devices: 24.9 us -> 21.2 us  [swapped(): return lax.ppermute(value, axis, list(enumerate(partner)))]
    ppermute x10, waiting for transfers between devices: 7.98 us -> 10.7 us  [swapped(): return lax.ppermute(value, axis, list(enumerate(partner)))]
  transfers between devices with their start and end apart: 24 -> 24, of which waited for: 7 -> 8; matrix products, arithmetic and copies ran while one was open for 2% -> 2% of each run, Pallas kernels for 14% -> 14%
where the time goes in v5:
time: 88.7 us; the launch traced here: 88.4 us
  starting transfers between devices  49.2 us (55%)
  Pallas kernels  17.8 us (20%)
  waiting for transfers between devices  15.8 us (18%)
  local copies, waits for them, and re-layouts  4.26 us (5%)
  between operations  1.11 us (1%)
    ppermute x10, starting transfers between devices, swapped(): return lax.ppermute(value, axis, list(enumerate(partner)))  21.2 us
    ppermute x10, waiting for transfers between devices, swapped(): return lax.ppermute(value, axis, list(enumerate(partner)))  10.7 us
    ppermute x4, starting transfers between devices, shifted(): lax.ppermute(value, SPACE, [(i, i + steps) for i in range(first, last)])  9.27 us
    ppermute x6, starting transfers between devices, ring_gather(): lax.ppermute(value, axis, [(i, (i + step) % count) for i in range(count)])  8.94 us
    ppermute x2, starting transfers between devices, exchange(): side_n = lax.ppermute(face_n, SPACE, across)  6.2 us
    pallas_call x1, Pallas kernels, inner(): pl.pallas_call(inner_kernel, out_shape=[jax.ShapeDtypeStruct((8, 8, 32, C...  5.86 us
    ppermute x2, waiting for transfers between devices, exchange(): side_n = lax.ppermute(face_n, SPACE, across)  5.11 us
    pallas_call x1, Pallas kernels, back_inner(): pl.pallas_call(back_inner_kernel, out_shape=jax.ShapeDtypeStruct((8, 8, 3...  4.15 us
  transfers between devices with their start and end apart: 24, of which 8 were waited for; matrix products, arithmetic and copies ran while one was open for 2% of the time, Pallas kernels for 14%

profile of v5, /device:TPU:1, one launch (start us, length us, event | category | flops | bytes accessed | tf_op | source)
XLA Modules:
  0.0 88.4 jit_solution(10971076908090736630)
XLA Ops:
  1.7 2.2 %collective-permute-start = (bf16[512,128]{1,0:T(8,128)(2,1)S(1)}, bf16[512,128]{1,0:T(8,128)(2,1)S(1)}, u32[]{:S(2)}, u32[]{:S(2)}) collective-permute-start(bf16[512,128]{1,0:T(8,128)(2,1)S(1)} %bitcast.26), channel_id=1, source_target_pairs={{0,1},{1,2},{2,3},{3,0},{4,5},{5,6},{6,7},{7,4},{8,9},{9,10},{10,1... | collective-permute-start | bytes 393224 | tf_op jit(solution)/shard_map/ppermute | solution.py:574
  3.9 2.6 %collective-permute-start.1 = (bf16[512,128]{1,0:T(8,128)(2,1)S(1)}, bf16[512,128]{1,0:T(8,128)(2,1)S(1)}, u32[]{:S(2)}, u32[]{:S(2)}) collective-permute-start(bf16[512,128]{1,0:T(8,128)(2,1)S(1)} %bitcast.27), channel_id=1, source_target_pairs={{0,2},{1,3},{2,0},{3,1},{4,6},{5,7},{6,4},{7,5},{8,10},{9,11},{10,... | collective-permute-start | bytes 393224 | tf_op jit(solution)/shard_map/ppermute | solution.py:574
  10.6 1.8 %collective-permute-start.5 = (bf16[1376,128]{1,0:T(8,128)(2,1)S(1)}, bf16[1376,128]{1,0:T(8,128)(2,1)S(1)}, u32[]{:S(2)}, u32[]{:S(2)}) collective-permute-start(bf16[1376,128]{1,0:T(8,128)(2,1)S(1)} %pad_maximum_fusion.w0_ref), channel_id=1, source_target_pairs={{0,3},{1,0},{2,1},{3,2},{4,7},{5,4},{6,5},{7,6},{8,11},{9,8},{10,9... | collective-permute-start | bytes 1056776 | tf_op jit(solution)/shard_map/ppermute | solution.py:574
  12.6 3.4 %collective-permute-start.6 = (bf16[272,128]{1,0:T(8,128)(2,1)S(1)}, bf16[272,128]{1,0:T(8,128)(2,1)S(1)}, u32[]{:S(2)}, u32[]{:S(2)}) collective-permute-start(bf16[272,128]{1,0:T(8,128)(2,1)S(1)} %get-tuple-element.29), channel_id=1, source_target_pairs={{0,4},{4,0},{1,5},{5,1},{2,6},{6,2},{3,7},{7,3},{8,12},{12,8},{9,1... | collective-permute-start | bytes 208904 | tf_op jit(solution)/shard_map/ppermute | solution.py:114
  16.1 2.6 %collective-permute-start.7 = (bf16[272,128]{1,0:T(8,128)(2,1)S(1)}, bf16[272,128]{1,0:T(8,128)(2,1)S(1)}, u32[]{:S(2)}, u32[]{:S(2)}) collective-permute-start(bf16[272,128]{1,0:T(8,128)(2,1)S(1)} %get-tuple-element.30), channel_id=1, source_target_pairs={{4,8},{20,24},{36,40},{52,56},{68,72},{84,88},{100,104},{116,120},... | collective-permute-start | bytes 208904 | tf_op jit(solution)/shard_map/ppermute | solution.py:113
  18.8 3.2 %collective-permute-done.7.side_n_ref = bf16[272,128]{1,0:T(8,128)(2,1)S(1)} collective-permute-done((bf16[272,128]{1,0:T(8,128)(2,1)S(1)}, bf16[272,128]{1,0:T(8,128)(2,1)S(1)}, u32[]{:S(2)}, u32[]{:S(2)}) %collective-permute-start.7) | collective-permute-done | bytes 69664 | tf_op jit(solution)/shard_map/ppermute | solution.py:113
  23.3 4.9 %collective-permute-start.8 = (bf16[368,128]{1,0:T(8,128)(2,1)S(1)}, bf16[368,128]{1,0:T(8,128)(2,1)S(1)}, u32[]{:S(2)}, u32[]{:S(2)}) collective-permute-start(bf16[368,128]{1,0:T(8,128)(2,1)S(1)} %constant_dynamic-update-slice_fusion), channel_id=1, source_target_pairs={{0,16},{4,20},{8,24},{12,28},{16,32},{20,36},{24,40},{28,44},{32,4... | collective-permute-start | bytes 282632 | tf_op jit(solution)/shard_map/ppermute | solution.py:36
  28.2 5.9 %shard_map.78 = (f32[8,8,32,128]{3,2,1,0:T(8,128)S(1)}, bf16[8,8,32,128]{3,2,1,0:T(8,128)(2,1)S(1)}, f32[4,64,8,128]{3,2,1,0:T(8,128)S(1)}) custom-call(s32[4,27]{1,0:T(4,128)S(1)} %copy-done.1, s32[1]{0:T(128)} %bitcast.chan_ref, f32[4,64,8,128]{3,2,1,0:T(8,128)S(1)} %get-tuple-element.25.tiles_ref, bf16[1376,128]{1,0:T(8,128)(2,1)S(1)} %pad_maximum_fusion.w0_ref, ...), custom_call_target="tpu_custom_call" | custom-call | flops 1811939328 | bytes 16777216 | tf_op jit(solution)/shard_map/pallas_call | solution.py:314
  34.1 4.0 %shard_map.79 = (f32[4,64,8,128]{3,2,1,0:T(8,128)S(1)}, f32[4,64,8,128]{3,2,1,0:T(8,128)S(1)}, bf16[272,128]{1,0:T(8,128)(2,1)S(1)}, bf16[272,128]{1,0:T(8,128)(...) custom-call(s32[1]{0:T(128)} %bitcast.1.core_ref.place_ref, ...), custom_call_target="tpu_custom_call" | custom-call | flops 905969664 | bytes 16777216 | tf_op jit(solution)/shard_map/pallas_call | solution.py:428
  39.2 3.6 %collective-permute-start.11 = (bf16[272,128]{1,0:T(8,128)(2,1)S(1)}, bf16[272,128]{1,0:T(8,128)(2,1)S(1)}, u32[]{:S(2)}, u32[]{:S(2)}) collective-permute-start(bf16[272,128]{1,0:T(8,128)(2,1)S(1)} %get-tuple-element.37), channel_id=1, source_target_pairs={{4,8},{20,24},{36,40},{52,56},{68,72},{84,88},{100,104},{116,120},... | collective-permute-start | bytes 208904 | tf_op jit(solution)/shard_map/ppermute | solution.py:113
  42.8 1.9 %collective-permute-done.11.side_n_ref = bf16[272,128]{1,0:T(8,128)(2,1)S(1)} collective-permute-done((bf16[272,128]{1,0:T(8,128)(2,1)S(1)}, bf16[272,128]{1,0:T(8,128)(2,1)S(1)}, u32[]{:S(2)}, u32[]{:S(2)}) %collective-permute-start.11) | collective-permute-done | bytes 69664 | tf_op jit(solution)/shard_map/ppermute | solution.py:113
  44.9 7.1 %collective-permute-start.15 = (f32[224,128]{1,0:T(8,128)S(1)}, f32[224,128]{1,0:T(8,128)S(1)}, u32[]{:S(2)}, u32[]{:S(2)}) collective-permute-start(f32[224,128]{1,0:T(8,128)S(1)} %dynamic-slice_bitcast_fusion), channel_id=1, source_target_pairs={{0,192},{64,128},{128,64},{192,0},{1,193},{65,129},{129,65},{193,1... | collective-permute-start | bytes 344072 | tf_op jit(solution)/shard_map/ppermute | solution.py:579
  54.1 2.3 %collective-permute-start.16 = (f32[112,128]{1,0:T(8,128)S(1)}, f32[112,128]{1,0:T(8,128)S(1)}, u32[]{:S(2)}, u32[]{:S(2)}) collective-permute-start(f32[112,128]{1,0:T(8,128)S(1)} %dynamic-slice_bitcast_fusion.1), channel_id=1, source_target_pairs={{0,64},{64,0},{128,192},{192,128},{1,65},{65,1},{129,193},{193,129... | collective-permute-start | bytes 172040 | tf_op jit(solution)/shard_map/ppermute | solution.py:579
  56.5 1.8 %collective-permute-start.12 = (bf16[368,128]{1,0:T(8,128)(2,1)S(1)}, bf16[368,128]{1,0:T(8,128)(2,1)S(1)}, u32[]{:S(2)}, u32[]{:S(2)}) collective-permute-start(bf16[368,128]{1,0:T(8,128)(2,1)S(1)} %constant_dynamic-update-slice_fusion.20), channel_id=1, source_target_pairs={{0,16},{4,20},{8,24},{12,28},{16,32},{20,36},{24,40},{28,44},{32,4... | collective-permute-start | bytes 282632 | tf_op jit(solution)/shard_map/ppermute | solution.py:36
  58.3 3.7 %collective-permute-start.17 = (f32[112,128]{1,0:T(8,128)S(1)}, f32[112,128]{1,0:T(8,128)S(1)}, u32[]{:S(2)}, u32[]{:S(2)}) collective-permute-start(f32[112,128]{1,0:T(8,128)S(1)} %bitcast_add_fusion.1), channel_id=1, source_target_pairs={{0,48},{8,56},{16,32},{24,40},{32,16},{40,24},{48,0},{56,8},{1,49}... | collective-permute-start | bytes 172040 | tf_op jit(solution)/shard_map/ppermute | solution.py:579
  62.0 4.2 %shard_map.81.part_ref = f32[8,8,32,128]{3,2,1,0:T(8,128)S(1)} custom-call(s32[4,27]{1,0:T(4,128)S(1)} %copy-done.1, f32[4,64,8,128]{3,2,1,0:T(8,128)S(1)} %get-tuple-element.35.tiles_ref, bf16[1152,128]{1,0:T(8,128)(2,1)S(1)} %shard_map.76.turned_ref), custom_call_target="tpu_custom_call" | custom-call | flops 905969664 | bytes 8388608 | tf_op jit(solution)/shard_map/pallas_call | solution.py:465
  66.3 3.0 %collective-permute-done.18 = f32[112,128]{1,0:T(8,128)S(1)} collective-permute-done((f32[112,128]{1,0:T(8,128)S(1)}, f32[112,128]{1,0:T(8,128)S(1)}, u32[]{:S(2)}, u32[]{:S(2)}) %collective-permute-start.18) | collective-permute-done | bytes 57376 | tf_op jit(solution)/shard_map/ppermute | solution.py:579
  69.4 1.7 %shard_map.82 = bf16[512,128]{1,0:T(8,128)(2,1)S(1)} custom-call(s32[1]{0:T(128)} %bitcast.1.core_ref.place_ref, s32[8,128]{1,0:T(8,128)S(1)} %get-tuple-element.34.index_in_ref, f32[4,64,8,128]{3,2,1,0:T(8,128)S(1)} %get-tuple-element.35.tiles_ref, bf16[272,128]{1,0:T(8,128)(2,1)S(1)} %collective-permute-done.10.side_m_ref, ...), custom_call_target="tpu_custom_call" | custom-call | flops 452984832 | bytes 8388608 | tf_op jit(solution)/shard_map/pallas_call | solution.py:553
  71.9 1.8 %collective-permute-done.19 = f32[112,128]{1,0:T(8,128)S(1)} collective-permute-done((f32[112,128]{1,0:T(8,128)S(1)}, f32[112,128]{1,0:T(8,128)S(1)}, u32[]{:S(2)}, u32[]{:S(2)}) %collective-permute-start.19) | collective-permute-done | bytes 57376 | tf_op jit(solution)/shard_map/ppermute | solution.py:579
  73.7 1.6 %collective-permute-start.20 = (f32[112,128]{1,0:T(8,128)S(1)}, f32[112,128]{1,0:T(8,128)S(1)}, u32[]{:S(2)}, u32[]{:S(2)}) collective-permute-start(f32[112,128]{1,0:T(8,128)S(1)} %add.58.one_ref), channel_id=1, source_target_pairs={{0,64},{64,0},{128,192},{192,128},{1,65},{65,1},{129,193},{193,129... | collective-permute-start | bytes 172040 | tf_op jit(solution)/shard_map/ppermute | solution.py:579
  75.3 1.9 %collective-permute-start.21 = (f32[112,128]{1,0:T(8,128)S(1)}, f32[112,128]{1,0:T(8,128)S(1)}, u32[]{:S(2)}, u32[]{:S(2)}) collective-permute-start(f32[112,128]{1,0:T(8,128)S(1)} %add.58.one_ref), channel_id=1, source_target_pairs={{0,192},{64,128},{128,64},{192,0},{1,193},{65,129},{129,65},{193,1... | collective-permute-start | bytes 172040 | tf_op jit(solution)/shard_map/ppermute | solution.py:579
  79.6 2.7 %collective-permute-done.22 = f32[112,128]{1,0:T(8,128)S(1)} collective-permute-done((f32[112,128]{1,0:T(8,128)S(1)}, f32[112,128]{1,0:T(8,128)S(1)}, u32[]{:S(2)}, u32[]{:S(2)}) %collective-permute-start.22) | collective-permute-done | bytes 57376 | tf_op jit(solution)/shard_map/ppermute | solution.py:579
  82.3 3.6 %collective-permute-start.23 = (f32[448,128]{1,0:T(8,128)S(1)}, f32[448,128]{1,0:T(8,128)S(1)}, u32[]{:S(2)}, u32[]{:S(2)}) collective-permute-start(f32[448,128]{1,0:T(8,128)S(1)} %pad_maximum_fusion.1), channel_id=1, source_target_pairs={{0,4},{4,0},{1,5},{5,1},{2,6},{6,2},{3,7},{7,3},{8,12},{12,8},{9,1... | collective-permute-start | bytes 688136 | tf_op jit(solution)/shard_map/ppermute | solution.py:579
  86.9 1.4 %shard_map.83 = f32[864,128]{1,0:T(8,128)} custom-call(s32[8]{0:T(128)S(1)} %iota_xor_fusion.me_ref, f32[112,128]{1,0:T(8,128)S(1)} %add.58.one_ref, f32[112,128]{1,0:T(8,128)S(1)} %collective-permute-done.20.two_ref, f32[224,128]{1,0:T(8,128)S(1)} %pad_maximum_fusion.2.four_ref, f32[448,128]{1,0:T(8,128)S(1)} %collective-permute-done.23.eight_ref), custom_call_target="tpu_custom_call" | custom-call | bytes 1048576 | tf_op jit(solution)/shard_map/pallas_call | solution.py:638
  (90 shorter events, 14.5 us)
Async XLA Ops:
  1.7 8.9 %collective-permute-start = (bf16[512,128]{1,0:T(8,128)(2,1)S(1)}, bf16[512,128]{1,0:T(8,128)(2,1)S(1)}, u32[]{:S(2)}, u32[]{:S(2)}) collective-permute-start(bf16[512,128]{1,0:T(8,128)(2,1)S(1)} %bitcast.26), channel_id=1, source_target_pairs={{0,1},{1,2},{2,3},{3,0},{4,5},{5,6},{6,7},{7,4},{8,9},{9,10},{10,1... | collective-permute-start | bytes 393224 | tf_op jit(solution)/shard_map/ppermute | solution.py:574
  3.9 8.5 %collective-permute-start.1 = (bf16[512,128]{1,0:T(8,128)(2,1)S(1)}, bf16[512,128]{1,0:T(8,128)(2,1)S(1)}, u32[]{:S(2)}, u32[]{:S(2)}) collective-permute-start(bf16[512,128]{1,0:T(8,128)(2,1)S(1)} %bitcast.27), channel_id=1, source_target_pairs={{0,2},{1,3},{2,0},{3,1},{4,6},{5,7},{6,4},{7,5},{8,10},{9,11},{10,... | collective-permute-start | bytes 393224 | tf_op jit(solution)/shard_map/ppermute | solution.py:574
  6.5 5.9 %collective-permute-start.2 = (bf16[512,128]{1,0:T(8,128)(2,1)S(1)}, bf16[512,128]{1,0:T(8,128)(2,1)S(1)}, u32[]{:S(2)}, u32[]{:S(2)}) collective-permute-start(bf16[512,128]{1,0:T(8,128)(2,1)S(1)} %bitcast.28), channel_id=1, source_target_pairs={{0,3},{1,0},{2,1},{3,2},{4,7},{5,4},{6,5},{7,6},{8,11},{9,8},{10,9... | collective-permute-start | bytes 393224 | tf_op jit(solution)/shard_map/ppermute | solution.py:574
  7.7 20.5 %collective-permute-start.3 = (bf16[1376,128]{1,0:T(8,128)(2,1)S(1)}, bf16[1376,128]{1,0:T(8,128)(2,1)S(1)}, u32[]{:S(2)}, u32[]{:S(2)}) collective-permute-start(bf16[1376,128]{1,0:T(8,128)(2,1)S(1)} %pad_maximum_fusion.w0_ref), channel_id=1, source_target_pairs={{0,1},{1,2},{2,3},{3,0},{4,5},{5,6},{6,7},{7,4},{8,9},{9,10},{10,1... | collective-permute-start | bytes 1056776 | tf_op jit(solution)/shard_map/ppermute | solution.py:574
  8.2 20.1 %collective-permute-start.4 = (bf16[1376,128]{1,0:T(8,128)(2,1)S(1)}, bf16[1376,128]{1,0:T(8,128)(2,1)S(1)}, u32[]{:S(2)}, u32[]{:S(2)}) collective-permute-start(bf16[1376,128]{1,0:T(8,128)(2,1)S(1)} %pad_maximum_fusion.w0_ref), channel_id=1, source_target_pairs={{0,2},{1,3},{2,0},{3,1},{4,6},{5,7},{6,4},{7,5},{8,10},{9,11},{10,... | collective-permute-start | bytes 1056776 | tf_op jit(solution)/shard_map/ppermute | solution.py:574
  10.6 17.6 %collective-permute-start.5 = (bf16[1376,128]{1,0:T(8,128)(2,1)S(1)}, bf16[1376,128]{1,0:T(8,128)(2,1)S(1)}, u32[]{:S(2)}, u32[]{:S(2)}) collective-permute-start(bf16[1376,128]{1,0:T(8,128)(2,1)S(1)} %pad_maximum_fusion.w0_ref), channel_id=1, source_target_pairs={{0,3},{1,0},{2,1},{3,2},{4,7},{5,4},{6,5},{7,6},{8,11},{9,8},{10,9... | collective-permute-start | bytes 1056776 | tf_op jit(solution)/shard_map/ppermute | solution.py:574
  12.6 6.1 %collective-permute-start.6 = (bf16[272,128]{1,0:T(8,128)(2,1)S(1)}, bf16[272,128]{1,0:T(8,128)(2,1)S(1)}, u32[]{:S(2)}, u32[]{:S(2)}) collective-permute-start(bf16[272,128]{1,0:T(8,128)(2,1)S(1)} %get-tuple-element.29), channel_id=1, source_target_pairs={{0,4},{4,0},{1,5},{5,1},{2,6},{6,2},{3,7},{7,3},{8,12},{12,8},{9,1... | collective-permute-start | bytes 208904 | tf_op jit(solution)/shard_map/ppermute | solution.py:114
  16.1 5.9 %collective-permute-start.7 = (bf16[272,128]{1,0:T(8,128)(2,1)S(1)}, bf16[272,128]{1,0:T(8,128)(2,1)S(1)}, u32[]{:S(2)}, u32[]{:S(2)}) collective-permute-start(bf16[272,128]{1,0:T(8,128)(2,1)S(1)} %get-tuple-element.30), channel_id=1, source_target_pairs={{4,8},{20,24},{36,40},{52,56},{68,72},{84,88},{100,104},{116,120},... | collective-permute-start | bytes 208904 | tf_op jit(solution)/shard_map/ppermute | solution.py:113
  22.0 12.1 %collective-permute-start.9 = (bf16[368,128]{1,0:T(8,128)(2,1)S(1)}, bf16[368,128]{1,0:T(8,128)(2,1)S(1)}, u32[]{:S(2)}, u32[]{:S(2)}) collective-permute-start(bf16[368,128]{1,0:T(8,128)(2,1)S(1)} %constant_dynamic-update-slice_fusion.9), channel_id=1, source_target_pairs={{16,0},{20,4},{24,8},{28,12},{32,16},{36,20},{40,24},{44,28},{48,3... | collective-permute-start | bytes 282632 | tf_op jit(solution)/shard_map/ppermute | solution.py:36
  23.3 10.8 %collective-permute-start.8 = (bf16[368,128]{1,0:T(8,128)(2,1)S(1)}, bf16[368,128]{1,0:T(8,128)(2,1)S(1)}, u32[]{:S(2)}, u32[]{:S(2)}) collective-permute-start(bf16[368,128]{1,0:T(8,128)(2,1)S(1)} %constant_dynamic-update-slice_fusion), channel_id=1, source_target_pairs={{0,16},{4,20},{8,24},{12,28},{16,32},{20,36},{24,40},{28,44},{32,4... | collective-permute-start | bytes 282632 | tf_op jit(solution)/shard_map/ppermute | solution.py:36
  38.1 6.7 %collective-permute-start.14 = (f32[448,128]{1,0:T(8,128)S(1)}, f32[448,128]{1,0:T(8,128)S(1)}, u32[]{:S(2)}, u32[]{:S(2)}) collective-permute-start(f32[448,128]{1,0:T(8,128)S(1)} %get-tuple-element.41), channel_id=1, source_target_pairs={{0,4},{4,0},{1,5},{5,1},{2,6},{6,2},{3,7},{7,3},{8,12},{12,8},{9,1... | collective-permute-start | bytes 688136 | tf_op jit(solution)/shard_map/ppermute | solution.py:579
  39.0 3.7 %collective-permute-start.10 = (bf16[272,128]{1,0:T(8,128)(2,1)S(1)}, bf16[272,128]{1,0:T(8,128)(2,1)S(1)}, u32[]{:S(2)}, u32[]{:S(2)}) collective-permute-start(bf16[272,128]{1,0:T(8,128)(2,1)S(1)} %get-tuple-element.36), channel_id=1, source_target_pairs={{0,4},{4,0},{1,5},{5,1},{2,6},{6,2},{3,7},{7,3},{8,12},{12,8},{9,1... | collective-permute-start | bytes 208904 | tf_op jit(solution)/shard_map/ppermute | solution.py:114
  39.2 5.6 %collective-permute-start.11 = (bf16[272,128]{1,0:T(8,128)(2,1)S(1)}, bf16[272,128]{1,0:T(8,128)(2,1)S(1)}, u32[]{:S(2)}, u32[]{:S(2)}) collective-permute-start(bf16[272,128]{1,0:T(8,128)(2,1)S(1)} %get-tuple-element.37), channel_id=1, source_target_pairs={{4,8},{20,24},{36,40},{52,56},{68,72},{84,88},{100,104},{116,120},... | collective-permute-start | bytes 208904 | tf_op jit(solution)/shard_map/ppermute | solution.py:113
  44.9 9.2 %collective-permute-start.15 = (f32[224,128]{1,0:T(8,128)S(1)}, f32[224,128]{1,0:T(8,128)S(1)}, u32[]{:S(2)}, u32[]{:S(2)}) collective-permute-start(f32[224,128]{1,0:T(8,128)S(1)} %dynamic-slice_bitcast_fusion), channel_id=1, source_target_pairs={{0,192},{64,128},{128,64},{192,0},{1,193},{65,129},{129,65},{193,1... | collective-permute-start | bytes 344072 | tf_op jit(solution)/shard_map/ppermute | solution.py:579
  51.9 17.5 %collective-permute-start.13 = (bf16[368,128]{1,0:T(8,128)(2,1)S(1)}, bf16[368,128]{1,0:T(8,128)(2,1)S(1)}, u32[]{:S(2)}, u32[]{:S(2)}) collective-permute-start(bf16[368,128]{1,0:T(8,128)(2,1)S(1)} %constant_dynamic-update-slice_fusion.29), channel_id=1, source_target_pairs={{16,0},{20,4},{24,8},{28,12},{32,16},{36,20},{40,24},{44,28},{48,3... | collective-permute-start | bytes 282632 | tf_op jit(solution)/shard_map/ppermute | solution.py:36
  54.1 4.1 %collective-permute-start.16 = (f32[112,128]{1,0:T(8,128)S(1)}, f32[112,128]{1,0:T(8,128)S(1)}, u32[]{:S(2)}, u32[]{:S(2)}) collective-permute-start(f32[112,128]{1,0:T(8,128)S(1)} %dynamic-slice_bitcast_fusion.1), channel_id=1, source_target_pairs={{0,64},{64,0},{128,192},{192,128},{1,65},{65,1},{129,193},{193,129... | collective-permute-start | bytes 172040 | tf_op jit(solution)/shard_map/ppermute | solution.py:579
  56.5 13.0 %collective-permute-start.12 = (bf16[368,128]{1,0:T(8,128)(2,1)S(1)}, bf16[368,128]{1,0:T(8,128)(2,1)S(1)}, u32[]{:S(2)}, u32[]{:S(2)}) collective-permute-start(bf16[368,128]{1,0:T(8,128)(2,1)S(1)} %constant_dynamic-update-slice_fusion.20), channel_id=1, source_target_pairs={{0,16},{4,20},{8,24},{12,28},{16,32},{20,36},{24,40},{28,44},{32,4... | collective-permute-start | bytes 282632 | tf_op jit(solution)/shard_map/ppermute | solution.py:36
  58.3 7.8 %collective-permute-start.17 = (f32[112,128]{1,0:T(8,128)S(1)}, f32[112,128]{1,0:T(8,128)S(1)}, u32[]{:S(2)}, u32[]{:S(2)}) collective-permute-start(f32[112,128]{1,0:T(8,128)S(1)} %bitcast_add_fusion.1), channel_id=1, source_target_pairs={{0,48},{8,56},{16,32},{24,40},{32,16},{40,24},{48,0},{56,8},{1,49}... | collective-permute-start | bytes 172040 | tf_op jit(solution)/shard_map/ppermute | solution.py:579
  66.2 3.1 %collective-permute-start.18 = (f32[112,128]{1,0:T(8,128)S(1)}, f32[112,128]{1,0:T(8,128)S(1)}, u32[]{:S(2)}, u32[]{:S(2)}) collective-permute-start(f32[112,128]{1,0:T(8,128)S(1)} %add.56), channel_id=1, source_target_pairs={{0,8},{8,0},{16,24},{24,16},{32,40},{40,32},{48,56},{56,48},{1,9},... | collective-permute-start | bytes 172040 | tf_op jit(solution)/shard_map/ppermute | solution.py:579
  69.3 4.4 %collective-permute-start.19 = (f32[112,128]{1,0:T(8,128)S(1)}, f32[112,128]{1,0:T(8,128)S(1)}, u32[]{:S(2)}, u32[]{:S(2)}) collective-permute-start(f32[112,128]{1,0:T(8,128)S(1)} %add.57), channel_id=1, source_target_pairs={{0,16},{8,24},{16,0},{24,8},{32,48},{40,56},{48,32},{56,40},{1,17}... | collective-permute-start | bytes 172040 | tf_op jit(solution)/shard_map/ppermute | solution.py:579
  73.7 4.7 %collective-permute-start.20 = (f32[112,128]{1,0:T(8,128)S(1)}, f32[112,128]{1,0:T(8,128)S(1)}, u32[]{:S(2)}, u32[]{:S(2)}) collective-permute-start(f32[112,128]{1,0:T(8,128)S(1)} %add.58.one_ref), channel_id=1, source_target_pairs={{0,64},{64,0},{128,192},{192,128},{1,65},{65,1},{129,193},{193,129... | collective-permute-start | bytes 172040 | tf_op jit(solution)/shard_map/ppermute | solution.py:579
  75.3 4.2 %collective-permute-start.21 = (f32[112,128]{1,0:T(8,128)S(1)}, f32[112,128]{1,0:T(8,128)S(1)}, u32[]{:S(2)}, u32[]{:S(2)}) collective-permute-start(f32[112,128]{1,0:T(8,128)S(1)} %add.58.one_ref), channel_id=1, source_target_pairs={{0,192},{64,128},{128,64},{192,0},{1,193},{65,129},{129,65},{193,1... | collective-permute-start | bytes 172040 | tf_op jit(solution)/shard_map/ppermute | solution.py:579
  77.2 5.0 %collective-permute-start.22 = (f32[112,128]{1,0:T(8,128)S(1)}, f32[112,128]{1,0:T(8,128)S(1)}, u32[]{:S(2)}, u32[]{:S(2)}) collective-permute-start(f32[112,128]{1,0:T(8,128)S(1)} %add.58.one_ref), channel_id=1, source_target_pairs={{0,128},{64,192},{128,0},{192,64},{1,129},{65,193},{129,1},{193,65... | collective-permute-start | bytes 172040 | tf_op jit(solution)/shard_map/ppermute | solution.py:579
  82.3 4.7 %collective-permute-start.23 = (f32[448,128]{1,0:T(8,128)S(1)}, f32[448,128]{1,0:T(8,128)S(1)}, u32[]{:S(2)}, u32[]{:S(2)}) collective-permute-start(f32[448,128]{1,0:T(8,128)S(1)} %pad_maximum_fusion.1), channel_id=1, source_target_pairs={{0,4},{4,0},{1,5},{5,1},{2,6},{6,2},{3,7},{7,3},{8,12},{12,8},{9,1... | collective-permute-start | bytes 688136 | tf_op jit(solution)/shard_map/ppermute | solution.py:579
  (4 other events, 13.3 us)
